TPU v7x, 128 devices: a whole 4x4x4 slice. The times are simulated.
128 devices in a mesh: tm: 32 (over z, x, core), llm: 4 (over y).
Axes of the slice: x: 4, y: 4, z: 4, core: 2. Of those that a mesh axis runs over, the one named last changes fastest.
Arguments:
- audio: bfloat16 [4, 4096, 1536], P('llm', 'tm'), may hold values from -6 to 6
- frame_counts: int32 [4], replicated, may hold values from 2048 to 4096
- text_lengths: int32 [32, 4], replicated, may hold values from 0 to 32
- norm_gain: float32 [1536], replicated, may hold values from 0.25 to 1.75
- w_query: bfloat16 [1536, 1536], replicated, may hold values from -4 to 4, as said below
- w_key: bfloat16 [1536, 1536], replicated, may hold values from -1 to 1, as said below
- w_value: bfloat16 [1536, 1536], replicated, may hold values from -0.15625 to 0.15625
- w_out: bfloat16 [1536, 1536], replicated, may hold values from -0.15625 to 0.15625
- conv_gain: float32 [1536], replicated, may hold values from 0.25 to 1.75
- conv_kernel: float32 [32, 1536], replicated, may hold values from -1 to 1
- latent_gain: float32 [1536], replicated, may hold values from 0.25 to 1.75
- llm_grads: bfloat16 [32, 256, 1536], P('tm', 'llm'), may hold values from -6 to 6
Outputs:
- llm_inputs: bfloat16 [32, 256, 1536], P('tm', 'llm')
- d_audio: bfloat16 [4, 4096, 1536], P('llm', 'tm')
Inputs may be any that keep to these rules, and one draw needn't show every extreme that they name: `w_query`: a 1536 x 1536 matrix. `w_key`: a 1536 x 1536 matrix.
All inputs are finite; a program needn't handle non-finite values.
Results may differ from a plain program's by a relative error of at most 0.02.
Values may be sent and summed in bfloat16 or wider, within the bound.
No kernel may reach another device: no remote copies, remote signals or barrier semaphores. Data moves between devices by JAX's collectives and lax.ppermute only.
A program may use at most 128 MiB of HBM per device.

v0:
```python
import jax
import jax.numpy as jnp
from jax import lax
from jax.sharding import PartitionSpec as P

HEADS = 16
REACH = 64
KERN = 32


EPSILON = 1e-06


def extended(cells, sides, width):
    for axis, dim in sides:
        count = lax.axis_size(axis)
        ends = count - 1
        head = lax.slice_in_dim(cells, 0, width, axis=dim)
        tail = lax.slice_in_dim(cells, cells.shape[dim] - width, cells.shape[dim], axis=dim)
        cells = jnp.concatenate(
            [
                lax.ppermute(tail, axis, [(i, (i + 1) % count) for i in range(ends)]),
                cells,
                lax.ppermute(head, axis, [((i + 1) % count, i) for i in range(ends)]),
            ],
            axis=dim,
        )
    return cells


def normalize(values_in, gain):
    widened = values_in.astype(jnp.float32)
    inverse = lax.rsqrt(jnp.mean(widened * widened, axis=-1, keepdims=True) + EPSILON)
    return widened * inverse * gain


def project(normed, w_query, w_key, w_value):
    queries = jnp.dot(normed, w_query, preferred_element_type=jnp.float32).astype(jnp.bfloat16)
    key_rows = jnp.dot(normed, w_key, preferred_element_type=jnp.float32).astype(jnp.bfloat16)
    value_rows = jnp.dot(normed, w_value, preferred_element_type=jnp.float32).astype(jnp.bfloat16)
    return (queries, key_rows, value_rows)


def attend(
    queries, key_float, value_float, query_pos, key_pos, frame_limit, frame_total, reach, heads
):
    query_count, width = queries.shape
    head_size = width // heads
    query_float = queries.astype(jnp.float32).reshape(query_count, heads, head_size)
    key_heads = key_float.reshape(key_float.shape[0], heads, head_size)
    value_heads = value_float.reshape(value_float.shape[0], heads, head_size)
    scores = jnp.einsum("qhd,khd->hqk", query_float, key_heads) * head_size ** (-0.5)
    lower = key_pos[None, :] >= query_pos[:, None] - reach
    upper = key_pos[None, :] < query_pos[:, None] + reach
    inside = (key_pos >= 0) & (key_pos < frame_total)
    spoken = (key_pos[None, :] < frame_limit) | (key_pos[None, :] == query_pos[:, None])
    allowed = lower & upper & inside[None, :] & spoken
    scores = jnp.where(allowed[None, :, :], scores, -1e30)
    highest = jnp.max(scores, axis=-1, keepdims=True)
    powers = jnp.exp(scores - highest)
    weights = (powers / jnp.sum(powers, axis=-1, keepdims=True)).astype(jnp.bfloat16)
    mixture = jnp.einsum("hqk,khd->qhd", weights.astype(jnp.float32), value_heads)
    return mixture.reshape(query_count, width).astype(jnp.bfloat16)


def attend_windows(queries, key_float, value_float, first_frame, frame_limit, frame_total):
    frame_rows, width = queries.shape
    span = 2 * REACH
    blocks = frame_rows // span
    query_blocks = queries.reshape(blocks, span, width)
    key_parts = key_float.reshape(blocks + 1, span, width)
    value_parts = value_float.reshape(blocks + 1, span, width)
    key_windows = jnp.concatenate([key_parts[:-1], key_parts[1:]], axis=1)
    value_windows = jnp.concatenate([value_parts[:-1], value_parts[1:]], axis=1)
    block_first = first_frame + span * jnp.arange(blocks, dtype=jnp.int32)
    query_pos = block_first[:, None] + jnp.arange(span, dtype=jnp.int32)[None, :]
    key_pos = block_first[:, None] - REACH + jnp.arange(2 * span, dtype=jnp.int32)[None, :]

    def one_window(query_in, key_in, value_in, query_at, key_at):
        return attend(
            query_in, key_in, value_in, query_at, key_at, frame_limit, frame_total, REACH, HEADS
        )

    mixed = jax.vmap(one_window)(query_blocks, key_windows, value_windows, query_pos, key_pos)
    return mixed.reshape(frame_rows, width)


def mix_out(signal, attended, w_out):
    return (
        signal.astype(jnp.float32) + jnp.dot(attended, w_out, preferred_element_type=jnp.float32)
    ).astype(jnp.bfloat16)


def conv_input(hidden, gain, spoken_rows):
    return (normalize(hidden, gain) * spoken_rows).astype(jnp.bfloat16)


def finish(hidden, padded_float, kernel, gain):
    frame_rows = hidden.shape[0]
    summed = jnp.zeros(hidden.shape, jnp.float32)
    for lag_index in range(kernel.shape[0]):
        summed = summed + kernel[lag_index] * padded_float[lag_index : lag_index + frame_rows]
    updated = hidden.astype(jnp.float32) + jax.nn.silu(summed)
    pooled = jnp.mean(updated.reshape(frame_rows // 4, 4, updated.shape[1]), axis=1)
    return normalize(pooled, gain).astype(jnp.bfloat16)


def route_positions(frame_counts, text_lengths, pooled_dev):
    slice_index = jnp.arange(text_lengths.shape[0], dtype=jnp.int32)[:, None]
    live_rows = jnp.clip(frame_counts[None, :] // 4 - slice_index * pooled_dev, 0, pooled_dev)
    starts = jnp.cumsum(text_lengths + live_rows, axis=1) - live_rows
    row_index = jnp.arange(pooled_dev, dtype=jnp.int32)
    placed = starts[:, :, None] + row_index[None, None, :]
    return jnp.where(row_index[None, None, :] < live_rows[:, :, None], placed, -1)


def extend(values_in, margin):
    return extended(values_in, (("tm", 0),), margin)


def give_back(padded_grad, margin, frame_rows):
    rim_pair = jnp.concatenate([padded_grad[:margin], padded_grad[margin + frame_rows :]], axis=0)
    arrived = extended(rim_pair.astype(jnp.bfloat16), (("tm", 0),), margin).astype(rim_pair.dtype)
    own_part = padded_grad[margin : margin + frame_rows]
    return jnp.concatenate(
        [
            own_part[:margin] + arrived[:margin],
            own_part[margin : frame_rows - margin],
            own_part[frame_rows - margin :] + arrived[3 * margin :],
        ],
        axis=0,
    )


def on_device(
    audio,
    frame_counts,
    text_lengths,
    norm_gain,
    w_query,
    w_key,
    w_value,
    w_out,
    conv_gain,
    conv_kernel,
    latent_gain,
    llm_grads,
):
    signal = audio[0]
    frame_rows = signal.shape[0]
    width = signal.shape[1]
    pooled_dev = frame_rows // 4
    shard_slots = frame_rows // 2
    side = KERN // 2
    slice_index = lax.axis_index("tm")
    record = lax.axis_index("llm")
    slice_total = lax.axis_size("tm")
    record_total = lax.axis_size("llm")
    record_pick = jnp.arange(record_total, dtype=jnp.int32) == record
    frame_limit = jnp.sum(jnp.where(record_pick, frame_counts, 0))
    first_frame = slice_index * frame_rows
    frame_total = frame_rows * slice_total
    query_pos = first_frame + jnp.arange(frame_rows, dtype=jnp.int32)
    normed, norm_back = jax.vjp(
        lambda source: normalize(source, norm_gain).astype(jnp.bfloat16), signal
    )
    (queries, key_rows, value_rows), proj_back = jax.vjp(
        lambda source: project(source, w_query, w_key, w_value), normed
    )
    wide_pair = extend(jnp.concatenate([key_rows, value_rows], axis=1), REACH)
    key_float = wide_pair[:, :width].astype(jnp.float32)
    value_float = wide_pair[:, width:].astype(jnp.float32)
    attended, attend_back = jax.vjp(
        lambda query_in, key_in, value_in: attend_windows(
            query_in, key_in, value_in, first_frame, frame_limit, frame_total
        ),
        queries,
        key_float,
        value_float,
    )
    hidden, mix_back = jax.vjp(
        lambda source, mixed_in: mix_out(source, mixed_in, w_out), signal, attended
    )
    spoken_rows = (query_pos < frame_limit).astype(jnp.float32)[:, None]
    conv_in, conv_back = jax.vjp(lambda source: conv_input(source, conv_gain, spoken_rows), hidden)
    padded_conv = extend(conv_in, side).astype(jnp.float32)
    latent, tail_back = jax.vjp(
        lambda source, padded_in: finish(source, padded_in, conv_kernel, latent_gain),
        hidden,
        padded_conv,
    )
    positions = route_positions(frame_counts, text_lengths, pooled_dev)
    slice_pick = (jnp.arange(slice_total, dtype=jnp.int32) == slice_index)[:, None, None]
    slice_positions = jnp.sum(jnp.where(slice_pick, positions, 0), axis=0)
    own_positions = jnp.sum(jnp.where(record_pick[:, None], slice_positions, 0), axis=0)
    flat_positions = slice_positions.reshape(-1)
    local_slot = flat_positions - record * shard_slots
    placing = (
        (flat_positions >= 0)[None, :]
        & (local_slot[None, :] == jnp.arange(shard_slots, dtype=jnp.int32)[:, None])
    ).astype(jnp.bfloat16)
    target = jnp.where(own_positions >= 0, own_positions // shard_slots, -1)
    heading = target[None, :] == jnp.arange(record_total, dtype=jnp.int32)[:, None]
    outgoing = jnp.where(heading[:, :, None], latent[None, :, :], jnp.zeros((), jnp.bfloat16))
    arrived = lax.all_to_all(outgoing, "llm", split_axis=0, concat_axis=0, tiled=True)
    llm_rows = jnp.dot(
        placing,
        arrived.reshape(record_total * pooled_dev, width),
        preferred_element_type=jnp.float32,
    ).astype(jnp.bfloat16)
    sending_back = jnp.dot(placing.T, llm_grads[0], preferred_element_type=jnp.float32).astype(
        jnp.bfloat16
    )
    came_back = lax.all_to_all(
        sending_back.reshape(record_total, pooled_dev, width),
        "llm",
        split_axis=0,
        concat_axis=0,
        tiled=True,
    )
    latent_grad = jnp.sum(
        jnp.where(heading[:, :, None], came_back.astype(jnp.float32), 0.0), axis=0
    ).astype(jnp.bfloat16)
    grad_hidden_tail, grad_padded = tail_back(latent_grad)
    grad_conv = give_back(grad_padded, side, frame_rows).astype(jnp.bfloat16)
    (grad_hidden_conv,) = conv_back(grad_conv)
    grad_hidden = grad_hidden_tail + grad_hidden_conv
    grad_signal_mix, grad_attended = mix_back(grad_hidden)
    grad_queries, grad_key_float, grad_value_float = attend_back(grad_attended)
    grad_pair = give_back(
        jnp.concatenate([grad_key_float, grad_value_float], axis=1), REACH, frame_rows
    )
    grad_keys = grad_pair[:, :width].astype(jnp.bfloat16)
    grad_values = grad_pair[:, width:].astype(jnp.bfloat16)
    (grad_normed,) = proj_back((grad_queries, grad_keys, grad_values))
    (grad_signal_norm,) = norm_back(grad_normed)
    grad_signal = grad_signal_mix + grad_signal_norm
    return (llm_rows[None], grad_signal[None])


def solution(mesh):
    placed = (
        P("llm", "tm", None),
        P(),
        P(),
        P(),
        P(),
        P(),
        P(),
        P(),
        P(),
        P(),
        P(),
        P("tm", "llm", None),
    )
    return jax.shard_map(
        on_device,
        mesh=mesh,
        in_specs=placed,
        out_specs=(P("tm", "llm", None), P("llm", "tm", None)),
        check_vma=False,
    )
```

profile of v0, /device:TPU:39, one launch (start us, length us, event | category | flops | bytes accessed | tf_op | source)
XLA Modules:
  0.0 151.7 jit_solution(3129073693771040410)
XLA Ops:
  0.6 1.2 fusion.30
  2.5 3.4 %convolution_convert_fusion.6 = bf16[128,1536]{1,0:T(8,128)(2,1)S(1)} fusion(bf16[1536,1536]{1,0:T(8,128)(2,1)} %param.18, bf16[1,128,1536]{2,1,0:T(8,128)(2,1)} %param.12, f32[1536]{0:T(1024)} %param.15, f32[128]{0:T(128)S(1)} %fusion.89), kind=kOutput, calls=%fused_computation.15 | convolution fusion | flops 604962816 | bytes 5511680 | tf_op jit(solution)/shard_map/jvp()/dot_general | solution.py:40
  8.1 4.0 %collective-permute-start = (bf16[64,3072]{1,0:T(8,128)(2,1)}, bf16[64,3072]{1,0:T(8,128)(2,1)S(1)}, u32[]{:S(2)}, u32[]{:S(2)}) collective-permute-start(bf16[64,3072]{1,0:T(8,128)(2,1)} %get-tuple-element.92), channel_id=1, source_target_pairs={{0,4},{4,8},{8,12},{12,16},{16,20},{20,24},{24,28},{28,32},{32,36}... | collective-permute-start | bytes 1179656 | tf_op jit(solution)/shard_map/ppermute | solution.py:22
  12.2 1.9 %collective-permute-start.1 = (bf16[64,3072]{1,0:T(8,128)(2,1)S(1)}, bf16[64,3072]{1,0:T(8,128)(2,1)S(1)}, u32[]{:S(2)}, u32[]{:S(2)}) collective-permute-start(bf16[64,3072]{1,0:T(8,128)(2,1)S(1)} %get-tuple-element.93), channel_id=1, source_target_pairs={{4,0},{8,4},{12,8},{16,12},{20,16},{24,20},{28,24},{32,28},{36,32}... | collective-permute-start | bytes 1179656 | tf_op jit(solution)/shard_map/ppermute | solution.py:24
  16.4 4.2 %all-to-all-start.1 = ((bf16[4,32,1536]{2,1,0:T(8,128)(2,1)}), bf16[4,32,1536]{2,1,0:T(8,128)(2,1)S(1)}, u32[]{:S(2)}, u32[]{:S(2)}) async-start(bf16[4,32,1536]{2,1,0:T(8,128)(2,1)} %bitcast.15), calls=%async_computation.1 | async-start | bytes 786432 | tf_op jit(solution)/shard_map/all_to_all | solution.py:214
  22.6 3.2 %convolution_convert_fusion.5 = bf16[128,1536]{1,0:T(8,128)(2,1)S(1)} fusion(bf16[1536,1536]{1,0:T(8,128)(2,1)} %param.16, bf16[1,128,1536]{2,1,0:T(8,128)(2,1)S(1)} %copy-done.2, f32[1536]{0:T(1024)S(1)} %copy-done.25, f32[128]{0:T(128)S(1)} %fusion.89), kind=kOutput, calls=%fused_computation.14 | convolution fusion | flops 604962816 | bytes 5511680 | tf_op jit(solution)/shard_map/jvp()/dot_general | solution.py:38
  25.9 1.2 compare_convert_fusion
  32.2 2.0 %fusion.118 = (f32[16,128]{1,0:T(8,128)S(1)}, f32[16,128,256]{2,1,0:T(8,128)S(1)}) fusion(bf16[128,16,96]{0,2,1:T(8,128)(2,1)} %bitcast.100, bf16[1,128,16,96]{1,3,2,0:T(8,128)(2,1)} %bitcast.104, bf16[1,128,16,96]{1,3,2,0:T(8,128)(2,1)} %bitcast.102, pred[128,256]{1,0:T(8,128)(4,1)} %or_and_fusion), kind=kOutput, calls=%fused_computation.308 | convolution fusion | flops 103806976 | bytes 3317760 | tf_op jit(solution)/shard_map/jvp(vmap(qhd,khd->hqk))/dot_general | solution.py:52
  34.9 1.1 fusion.16
  38.1 6.0 %collective-permute-start.2 = (bf16[16,1536]{1,0:T(8,128)(2,1)S(1)}, bf16[16,1536]{1,0:T(8,128)(2,1)S(1)}, u32[]{:S(2)}, u32[]{:S(2)}) collective-permute-start(bf16[16,1536]{1,0:T(8,128)(2,1)S(1)} %get-tuple-element.96), channel_id=1, source_target_pairs={{0,4},{4,8},{8,12},{12,16},{16,20},{20,24},{24,28},{28,32},{32,36}... | collective-permute-start | bytes 147464 | tf_op jit(solution)/shard_map/ppermute | solution.py:22
  44.1 2.1 %collective-permute-start.3 = (bf16[16,1536]{1,0:T(8,128)(2,1)S(1)}, bf16[16,1536]{1,0:T(8,128)(2,1)S(1)}, u32[]{:S(2)}, u32[]{:S(2)}) collective-permute-start(bf16[16,1536]{1,0:T(8,128)(2,1)S(1)} %get-tuple-element.97), channel_id=1, source_target_pairs={{4,0},{8,4},{12,8},{16,12},{20,16},{24,20},{28,24},{32,28},{36,32}... | collective-permute-start | bytes 147464 | tf_op jit(solution)/shard_map/ppermute | solution.py:24
  46.9 4.8 %collective-permute-done.3 = bf16[16,1536]{1,0:T(8,128)(2,1)S(1)} collective-permute-done((bf16[16,1536]{1,0:T(8,128)(2,1)S(1)}, bf16[16,1536]{1,0:T(8,128)(2,1)S(1)}, u32[]{:S(2)}, u32[]{:S(2)}) %collective-permute-start.3) | collective-permute-done | bytes 49184 | tf_op jit(solution)/shard_map/ppermute | solution.py:24
  52.0 4.2 %multiply_add_fusion = (f32[128,1536]{1,0:T(8,128)}, f32[128,1536]{1,0:T(8,128)}) fusion(f32[128,1536]{1,0:T(8,128)S(1)} %get-tuple-element.112, f32[160,1536]{1,0:T(8,128)S(1)} %maximum_convert_fusion.1, f32[1536]{0:T(1024)S(1)} %copy-done.75, f32[1536]{0:T(1024)S(1)} %get-tuple-element.35, f32[1536]{0:T(1024)S(1)} %get-tuple-element.5, ...), kind=kLoop, calls=%fused_computation.146 | loop fusion | flops 13369344 | bytes 27721728 | tf_op jit(solution)/shard_map/jvp()/add | solution.py:103
  56.2 2.3 %reshape.611 = f32[32,4,1536]{2,1,0:T(4,128)} reshape(f32[128,1536]{1,0:T(8,128)} %get-tuple-element.42) | data formatting | bytes 1572864 | tf_op jit(solution)/shard_map/jvp()/reshape | solution.py:104
  58.5 1.6 %reduce_sum.161 = f32[32,1536]{1,0:T(8,128)S(1)} reduce(f32[32,4,1536]{2,1,0:T(4,128)} %reshape.611, f32[]{:T(128)} %constant.84.clone.1), dimensions={1}, to_apply=%region_8.9 | reduce | flops 147456 | bytes 983044 | tf_op jit(solution)/shard_map/jvp()/reduce_sum | solution.py:104
  60.1 1.1 multiply_reduce_fusion.2
  61.2 1.7 %fusion.75 = (f32[32,1536]{1,0:T(8,128)S(1)}, bf16[32,1536]{1,0:T(8,128)(2,1)}) fusion(f32[32,1536]{1,0:T(8,128)S(1)} %reduce_sum.161, f32[32]{0:T(128)S(1)} %get-tuple-element.106, f32[32]{0:T(128)S(1)} %get-tuple-element.104, f32[1536]{0:T(1024)} %param.22, bf16[32,1536]{1,0:T(8,128)(2,1)} %select_reduce_fusion, f32[32]{0:T(128)S(1)} %get-tuple-element.105), kind=kLoop, calls=%fused_computation.196 | loop fusion | flops 491520 | bytes 596352 | tf_op jit(solution)/shard_map/transpose(jvp())/div | solution.py:104
  64.0 2.4 %reshape.614 = f32[128,1536]{1,0:T(8,128)} reshape(f32[32,4,1536]{2,1,0:T(4,128)} %broadcast_in_dim.148) | data formatting | bytes 1572864 | tf_op jit(solution)/shard_map/transpose(jvp())/reshape | solution.py:104
  66.4 2.6 %broadcast_multiply_fusion = (f32[128,1536]{1,0:T(8,128)}, f32[128,1536]{1,0:T(8,128)S(1)}) fusion(f32[1536]{0:T(1024)S(1)} %copy-done.76, f32[128,1536]{1,0:T(8,128)} %get-tuple-element.43, f32[128,1536]{1,0:T(8,128)} %reshape.614), kind=kLoop, calls=%fused_computation.162 | loop fusion | flops 1966080 | bytes 3151872 | tf_op jit(solution)/shard_map/transpose(jvp())/mul | solution.py:102
  69.2 1.9 %broadcast_multiply_fusion.1 = (f32[128,1536]{1,0:T(8,128)S(1)}, f32[128,1536]{1,0:T(8,128)S(1)}, f32[128,1536]{1,0:T(8,128)S(1)}, f32[128,1536]{1,0:T(8,128)S(1...) fusion(f32[128,1536]{1,0:T(8,128)S(1)} %get-tuple-element.41, ...), kind=kLoop, calls=%fused_computation.163 | loop fusion | flops 3538944 | bytes 15052800 | tf_op jit(solution)/shard_map/transpose(jvp())/mul | solution.py:102
  71.2 2.7 %broadcast_multiply_fusion.2 = (f32[128,1536]{1,0:T(8,128)S(1)}, f32[128,1536]{1,0:T(8,128)S(1)}, f32[128,1536]{1,0:T(8,128)S(1)}, f32[128,1536]{1,0:T(8,128)S(1...) fusion(f32[128,1536]{1,0:T(8,128)S(1)} %get-tuple-element.41, ...), kind=kLoop, calls=%fused_computation.164 | loop fusion | flops 2555904 | bytes 11089920 | tf_op jit(solution)/shard_map/transpose(jvp())/mul | solution.py:102
  74.0 5.8 %fusion.107 = (bf16[160,1536]{1,0:T(8,128)(2,1)S(1)}, f32[160,1536]{1,0:T(8,128)}) fusion(f32[128,1536]{1,0:T(8,128)} %get-tuple-element.87, f32[128,1536]{1,0:T(8,128)S(1)} %get-tuple-element.58, f32[128,1536]{1,0:T(8,128)S(1)} %get-tuple-element.59, f32[128,1536]{1,0:T(8,128)S(1)} %get-tuple-element.60, f32[128,1536]{1,0:T(8,128)S(1)} %get-tuple-element.61, ...), kind=kLoop, calls=%fused_computation.299 | loop fusion | flops 7864320 | bytes 26640384 | tf_op jit(solution)/shard_map/convert.13
  79.8 1.9 %collective-permute-start.4 = (bf16[16,1536]{1,0:T(8,128)(2,1)S(1)}, bf16[16,1536]{1,0:T(8,128)(2,1)S(1)}, u32[]{:S(2)}, u32[]{:S(2)}) collective-permute-start(bf16[16,1536]{1,0:T(8,128)(2,1)S(1)} %get-tuple-element.94), channel_id=1, source_target_pairs={{0,4},{4,8},{8,12},{12,16},{16,20},{20,24},{24,28},{28,32},{32,36}... | collective-permute-start | bytes 147464 | tf_op jit(solution)/shard_map/ppermute | solution.py:22
  81.7 2.4 %collective-permute-start.5 = (bf16[16,1536]{1,0:T(8,128)(2,1)S(1)}, bf16[16,1536]{1,0:T(8,128)(2,1)}, u32[]{:S(2)}, u32[]{:S(2)}) collective-permute-start(bf16[16,1536]{1,0:T(8,128)(2,1)S(1)} %get-tuple-element.95), channel_id=1, source_target_pairs={{4,0},{8,4},{12,8},{16,12},{20,16},{24,20},{28,24},{32,28},{36,32}... | collective-permute-start | bytes 147464 | tf_op jit(solution)/shard_map/ppermute | solution.py:24
  85.7 4.5 %all-to-all-start = ((bf16[4,32,1536]{2,1,0:T(8,128)(2,1)}), bf16[4,32,1536]{2,1,0:T(8,128)(2,1)}, u32[]{:S(2)}, u32[]{:S(2)}) async-start(bf16[4,32,1536]{2,1,0:T(8,128)(2,1)} %broadcast_select_fusion), calls=%async_computation | async-start | bytes 786432 | tf_op jit(solution)/shard_map/all_to_all | solution.py:205
  91.3 1.2 multiply_reduce_fusion
  93.3 1.3 fusion.72
  95.4 4.0 %convolution_convert_fusion.3 = bf16[128,1536]{1,0:T(8,128)(2,1)S(1)} fusion(bf16[128,1536]{1,0:T(8,128)(2,1)S(1)} %fusion.72, bf16[1536,1536]{1,0:T(8,128)(2,1)} %param.19), kind=kOutput, calls=%fused_computation.12 | convolution fusion | flops 604176384 | bytes 5505024 | tf_op jit(solution)/shard_map/transpose(jvp())/dot_general | solution.py:90
  99.6 1.5 %fusion.103 = f32[16,96,256]{2,1,0:T(8,128)S(1)} fusion(bf16[16,96,128]{2,1,0:T(8,128)(2,1)S(1)} %bitcast.97, f32[16,128,256]{2,1,0:T(8,128)S(1)} %get-tuple-element.110, f32[16,128]{1,0:T(8,128)S(1)} %copy-done.78, f32[16,128]{1,0:T(8,128)S(1)} %get-tuple-element.109), kind=kOutput, calls=%fused_computation.297 | convolution fusion | flops 102236160 | bytes 4079616 | tf_op jit(solution)/shard_map/transpose(jvp(vmap(hqk,khd->qhd)))/dot_general | solution.py:62
  101.2 2.0 %fusion.11 = (f32[16,128]{1,0:T(8,128)S(1)}, bf16[16,128,256]{2,1,0:T(8,128)(2,1)}) fusion(f32[16,128,256]{2,1,0:T(8,128)S(1)} %get-tuple-element.110, f32[16,128]{1,0:T(8,128)S(1)} %copy-done.79, f32[16,128]{1,0:T(8,128)S(1)} %get-tuple-element.109, bf16[16,96,128]{2,1,0:T(8,128)(2,1)S(1)} %bitcast.98, bf16[1,128,16,96]{1,3,2,0:T(8,128)(2,1)S(1)} %bitcast.96, ...), kind=kOutput, calls=%fused_computation.28 | convolution fusion | flops 104855552 | bytes 4349952 | tf_op jit(solution)/shard_map/transpose(jvp(vmap(hqk,khd->qhd)))/dot_general | solution.py:62
  103.2 1.3 fusion.111
  104.5 1.4 copy.47
  105.9 2.3 %copy.48 = f32[1,128,1536]{2,1,0:T(8,128)} copy(f32[1,128,1536]{1,2,0:T(8,128)} %get-tuple-element.50) | data formatting | bytes 1572864
  108.2 2.9 %convert_reduce_fusion = (f32[16,128]{1,0:T(8,128)S(1)}, pred[16,128,256]{2,1,0:T(32,128)(4,1)S(1)}, f32[16,128]{1,0:T(8,128)S(1)}) fusion(f32[16,128,256]{2,1,0:T(8,128)S(1)} %get-tuple-element.110, f32[16,128]{1,0:T(8,128)S(1)} %get-tuple-element.109, f32[16,128]{1,0:T(8,128)S(1)} %neg.15, f32[16,128]{1,0:T(8,128)S(1)} %copy-done.78, ...), kind=kLoop, calls=%fused_computation.30 | loop fusion | flops 4714496 | bytes 3710976 | tf_op jit(solution)/shard_map/jvp(vmap())/reduce_sum | solution.py:59
  111.2 1.4 fusion.14
  112.5 1.3 fusion.112
  113.8 2.3 %copy.45 = f32[1,128,1536]{2,1,0:T(8,128)} copy(f32[1,128,1536]{1,2,0:T(8,128)} %get-tuple-element.51) | data formatting | bytes 1572864
  116.1 2.3 %copy.46 = f32[1,128,1536]{2,1,0:T(8,128)} copy(f32[1,128,1536]{1,2,0:T(8,128)} %get-tuple-element.52) | data formatting | bytes 1572864
  118.4 1.4 pad_add_fusion
  121.7 5.7 %collective-permute-start.6 = (bf16[64,3072]{1,0:T(8,128)(2,1)S(1)}, bf16[64,3072]{1,0:T(8,128)(2,1)}, u32[]{:S(2)}, u32[]{:S(2)}) collective-permute-start(bf16[64,3072]{1,0:T(8,128)(2,1)S(1)} %get-tuple-element.47), channel_id=1, source_target_pairs={{0,4},{4,8},{8,12},{12,16},{16,20},{20,24},{24,28},{28,32},{32,36}... | collective-permute-start | bytes 1179656 | tf_op jit(solution)/shard_map/ppermute | solution.py:22
  127.4 1.9 %collective-permute-start.7 = (bf16[64,3072]{1,0:T(8,128)(2,1)S(1)}, bf16[64,3072]{1,0:T(8,128)(2,1)}, u32[]{:S(2)}, u32[]{:S(2)}) collective-permute-start(bf16[64,3072]{1,0:T(8,128)(2,1)S(1)} %get-tuple-element.48), channel_id=1, source_target_pairs={{4,0},{8,4},{12,8},{16,12},{20,16},{24,20},{28,24},{32,28},{36,32}... | collective-permute-start | bytes 1179656 | tf_op jit(solution)/shard_map/ppermute | solution.py:24
  129.4 2.9 %fusion.17 = bf16[16,128,96]{1,2,0:T(8,128)(2,1)} fusion(bf16[1,128,16,96]{1,3,2,0:T(8,128)(2,1)S(1)} %bitcast.105, bf16[1,128,16,96]{1,3,2,0:T(8,128)(2,1)S(1)} %bitcast.103, pred[16,128,256]{2,1,0:T(32,128)(4,1)S(1)} %copy-done.18, f32[16,128]{1,0:T(8,128)S(1)} %negate_divide_fusion, pred[128,256]{1,0:T(8,128)(4,1)S(1)} %copy-done.80, ...), kind=kOutput, calls=%fused_computation.50 | convolution fusion | flops 106954752 | bytes 4915200 | tf_op jit(solution)/shard_map/transpose(jvp(vmap(qhd,khd->hqk)))/dot_general | solution.py:52
  132.3 1.9 %fusion.7 = bf16[1,64,1536]{2,1,0:T(8,128)(2,1)} fusion(bf16[128,1536]{1,0:T(8,128)(2,1)} %bitcast.12, s32[128]{0:T(128)S(1)} %copy-done.86, pred[128]{0:T(512)(128)(4,1)S(1)} %copy-done.88), kind=kOutput, calls=%fused_computation.24 | convolution fusion | flops 25280512 | bytes 590464 | tf_op jit(solution)/shard_map/dot_general | solution.py:206
  134.2 4.6 %collective-permute-done.7 = bf16[64,3072]{1,0:T(8,128)(2,1)} collective-permute-done((bf16[64,3072]{1,0:T(8,128)(2,1)S(1)}, bf16[64,3072]{1,0:T(8,128)(2,1)}, u32[]{:S(2)}, u32[]{:S(2)}) %collective-permute-start.7) | collective-permute-done | bytes 393248 | tf_op jit(solution)/shard_map/ppermute | solution.py:24
  138.7 1.9 %fusion.35 = (bf16[64,3072]{1,0:T(8,128)(2,1)S(1)}, bf16[64,3072]{1,0:T(8,128)(2,1)S(1)}) fusion(f32[256,1536]{1,0:T(8,128)} %bitcast.90, f32[256,1536]{1,0:T(8,128)} %bitcast.88, bf16[64,3072]{1,0:T(8,128)(2,1)} %collective-permute-done.7, bf16[64,3072]{1,0:T(8,128)(2,1)S(1)} %get-tuple-element.47, bf16[64,3072]{1,0:T(8,128)(2,1)S(1)} %get-tuple-element.48, ...), kind=kLoop, calls=%fused_computation.73 | loop fusion | flops 4325376 | bytes 5505024 | tf_op jit(solution)/shard_map/add | solution.py:127
  140.7 4.0 %convolution_convert_fusion.1 = bf16[128,1536]{1,0:T(8,128)(2,1)S(1)} fusion(bf16[1536,1536]{1,0:T(8,128)(2,1)} %param.17, bf16[128,3072]{1,0:T(8,128)(2,1)S(1)} %maximum_convert_fusion), kind=kOutput, calls=%fused_computation.10 | convolution fusion | flops 604176384 | bytes 5505024 | tf_op jit(solution)/shard_map/transpose(jvp())/dot_general | solution.py:39
  144.8 4.0 %fusion.3 = bf16[128,1536]{1,0:T(8,128)(2,1)S(1)} fusion(bf16[128,1536]{1,0:T(8,128)(2,1)S(1)} %convolution_convert_fusion.1, bf16[1536,1536]{1,0:T(8,128)(2,1)} %param.18, bf16[128,3072]{1,0:T(8,128)(2,1)S(1)} %maximum_convert_fusion), kind=kOutput, calls=%fused_computation.19 | convolution fusion | flops 604372992 | bytes 5898240 | tf_op jit(solution)/shard_map/transpose(jvp())/dot_general | solution.py:40
  148.9 1.8 %fusion.33 = (f32[128]{0:T(128)S(1)}, f32[128,1536]{1,0:T(8,128)S(1)}) fusion(bf16[1,128,1536]{2,1,0:T(8,128)(2,1)S(1)} %copy-done.2, f32[1536]{0:T(1024)S(1)} %copy-done.25, bf16[128,1536]{1,0:T(8,128)(2,1)S(1)} %fusion.3, bf16[128,1536]{0,1:T(8,128)(2,1)S(1)} %bitcast.106, bf16[1536,1536]{1,0:T(8,128)(2,1)S(1)} %bitcast.86), kind=kOutput, calls=%fused_computation.71 | convolution fusion | flops 605355904 | bytes 6691328 | tf_op jit(solution)/shard_map/transpose(jvp())/dot_general | solution.py:38
  (271 shorter events, 24.0 us)
Async XLA Ops:
  0.6 14.7 %copy-start = (bf16[1,64,1536]{2,1,0:T(8,128)(2,1)S(1)}, bf16[1,64,1536]{2,1,0:T(8,128)(2,1)}, u32[]{:S(2)}) copy-start(bf16[1,64,1536]{2,1,0:T(8,128)(2,1)} %param.23) | copy-start | bytes 589828
  2.4 20.2 %copy-start.81 = (f32[128]{0:T(128)}, f32[128]{0:T(128)S(1)}, u32[]{:S(2)}) copy-start(f32[128]{0:T(128)S(1)} %fusion.89) | copy-start | bytes 1540
  7.3 13.3 %copy-start.24 = (f32[32,1536]{1,0:T(8,128)S(1)}, f32[32,1536]{1,0:T(8,128)}, u32[]{:S(2)}) copy-start(f32[32,1536]{1,0:T(8,128)} %param.21) | copy-start | bytes 589828
  8.1 21.4 %collective-permute-start = (bf16[64,3072]{1,0:T(8,128)(2,1)}, bf16[64,3072]{1,0:T(8,128)(2,1)S(1)}, u32[]{:S(2)}, u32[]{:S(2)}) collective-permute-start(bf16[64,3072]{1,0:T(8,128)(2,1)} %get-tuple-element.92), channel_id=1, source_target_pairs={{0,4},{4,8},{8,12},{12,16},{16,20},{20,24},{24,28},{28,32},{32,36}... | collective-permute-start | bytes 1179656 | tf_op jit(solution)/shard_map/ppermute | solution.py:22
  12.2 17.3 %collective-permute-start.1 = (bf16[64,3072]{1,0:T(8,128)(2,1)S(1)}, bf16[64,3072]{1,0:T(8,128)(2,1)S(1)}, u32[]{:S(2)}, u32[]{:S(2)}) collective-permute-start(bf16[64,3072]{1,0:T(8,128)(2,1)S(1)} %get-tuple-element.93), channel_id=1, source_target_pairs={{4,0},{8,4},{12,8},{16,12},{20,16},{24,20},{28,24},{32,28},{36,32}... | collective-permute-start | bytes 1179656 | tf_op jit(solution)/shard_map/ppermute | solution.py:24
  15.3 10.5 %copy-start.85 = (s32[128]{0:T(128)}, s32[128]{0:T(128)S(1)}, u32[]{:S(2)}) copy-start(s32[128]{0:T(128)S(1)} %sub.76) | copy-start | bytes 1540
  15.4 10.5 %copy-start.87 = (pred[128]{0:T(512)(128)(4,1)}, pred[128]{0:T(512)(128)(4,1)S(1)}, u32[]{:S(2)}) copy-start(pred[128]{0:T(512)(128)(4,1)S(1)} %ge.56) | copy-start | bytes 388
  16.4 12.3 %all-to-all-start.1 = ((bf16[4,32,1536]{2,1,0:T(8,128)(2,1)}), bf16[4,32,1536]{2,1,0:T(8,128)(2,1)S(1)}, u32[]{:S(2)}, u32[]{:S(2)}) async-start(bf16[4,32,1536]{2,1,0:T(8,128)(2,1)} %bitcast.15), calls=%async_computation.1 | async-start | bytes 786432 | tf_op jit(solution)/shard_map/all_to_all | solution.py:214
  20.9 30.8 %copy-start.27 = (f32[1536]{0:T(1024)}, f32[1536]{0:T(1024)S(1)}, u32[]{:S(2)}) copy-start(f32[1536]{0:T(1024)S(1)} %get-tuple-element.11) | copy-start | bytes 18436
  20.9 30.8 %copy-start.29 = (f32[1536]{0:T(1024)}, f32[1536]{0:T(1024)S(1)}, u32[]{:S(2)}) copy-start(f32[1536]{0:T(1024)S(1)} %get-tuple-element.12) | copy-start | bytes 18436
  21.0 30.8 %copy-start.31 = (f32[1536]{0:T(1024)}, f32[1536]{0:T(1024)S(1)}, u32[]{:S(2)}) copy-start(f32[1536]{0:T(1024)S(1)} %get-tuple-element.13) | copy-start | bytes 18436
  21.0 30.8 %copy-start.33 = (f32[1536]{0:T(1024)}, f32[1536]{0:T(1024)S(1)}, u32[]{:S(2)}) copy-start(f32[1536]{0:T(1024)S(1)} %get-tuple-element.14) | copy-start | bytes 18436
  21.0 30.8 %copy-start.35 = (f32[1536]{0:T(1024)}, f32[1536]{0:T(1024)S(1)}, u32[]{:S(2)}) copy-start(f32[1536]{0:T(1024)S(1)} %get-tuple-element.15) | copy-start | bytes 18436
  21.0 30.8 %copy-start.37 = (f32[1536]{0:T(1024)}, f32[1536]{0:T(1024)S(1)}, u32[]{:S(2)}) copy-start(f32[1536]{0:T(1024)S(1)} %get-tuple-element.16) | copy-start | bytes 18436
  21.0 30.8 %copy-start.39 = (f32[1536]{0:T(1024)}, f32[1536]{0:T(1024)S(1)}, u32[]{:S(2)}) copy-start(f32[1536]{0:T(1024)S(1)} %get-tuple-element.17) | copy-start | bytes 18436
  21.0 30.8 %copy-start.41 = (f32[1536]{0:T(1024)}, f32[1536]{0:T(1024)S(1)}, u32[]{:S(2)}) copy-start(f32[1536]{0:T(1024)S(1)} %get-tuple-element.18) | copy-start | bytes 18436
  21.0 30.8 %copy-start.43 = (f32[1536]{0:T(1024)}, f32[1536]{0:T(1024)S(1)}, u32[]{:S(2)}) copy-start(f32[1536]{0:T(1024)S(1)} %get-tuple-element.19) | copy-start | bytes 18436
  21.0 30.8 %copy-start.45 = (f32[1536]{0:T(1024)}, f32[1536]{0:T(1024)S(1)}, u32[]{:S(2)}) copy-start(f32[1536]{0:T(1024)S(1)} %get-tuple-element.20) | copy-start | bytes 18436
  21.0 30.8 %copy-start.47 = (f32[1536]{0:T(1024)}, f32[1536]{0:T(1024)S(1)}, u32[]{:S(2)}) copy-start(f32[1536]{0:T(1024)S(1)} %get-tuple-element.21) | copy-start | bytes 18436
  21.0 30.8 %copy-start.49 = (f32[1536]{0:T(1024)}, f32[1536]{0:T(1024)S(1)}, u32[]{:S(2)}) copy-start(f32[1536]{0:T(1024)S(1)} %get-tuple-element.22) | copy-start | bytes 18436
  21.9 30.0 %copy-start.51 = (f32[1536]{0:T(1024)}, f32[1536]{0:T(1024)S(1)}, u32[]{:S(2)}) copy-start(f32[1536]{0:T(1024)S(1)} %get-tuple-element.23) | copy-start | bytes 18436
  21.9 30.0 %copy-start.53 = (f32[1536]{0:T(1024)}, f32[1536]{0:T(1024)S(1)}, u32[]{:S(2)}) copy-start(f32[1536]{0:T(1024)S(1)} %get-tuple-element.24) | copy-start | bytes 18436
  21.9 30.1 %copy-start.55 = (f32[1536]{0:T(1024)}, f32[1536]{0:T(1024)S(1)}, u32[]{:S(2)}) copy-start(f32[1536]{0:T(1024)S(1)} %get-tuple-element.25) | copy-start | bytes 18436
  21.9 30.1 %copy-start.57 = (f32[1536]{0:T(1024)}, f32[1536]{0:T(1024)S(1)}, u32[]{:S(2)}) copy-start(f32[1536]{0:T(1024)S(1)} %get-tuple-element.26) | copy-start | bytes 18436
  21.9 30.1 %copy-start.59 = (f32[1536]{0:T(1024)}, f32[1536]{0:T(1024)S(1)}, u32[]{:S(2)}) copy-start(f32[1536]{0:T(1024)S(1)} %get-tuple-element.27) | copy-start | bytes 18436
  21.9 30.1 %copy-start.61 = (f32[1536]{0:T(1024)}, f32[1536]{0:T(1024)S(1)}, u32[]{:S(2)}) copy-start(f32[1536]{0:T(1024)S(1)} %get-tuple-element.28) | copy-start | bytes 18436
  21.9 30.1 %copy-start.63 = (f32[1536]{0:T(1024)}, f32[1536]{0:T(1024)S(1)}, u32[]{:S(2)}) copy-start(f32[1536]{0:T(1024)S(1)} %get-tuple-element.29) | copy-start | bytes 18436
  21.9 30.1 %copy-start.65 = (f32[1536]{0:T(1024)}, f32[1536]{0:T(1024)S(1)}, u32[]{:S(2)}) copy-start(f32[1536]{0:T(1024)S(1)} %get-tuple-element.30) | copy-start | bytes 18436
  21.9 30.1 %copy-start.67 = (f32[1536]{0:T(1024)}, f32[1536]{0:T(1024)S(1)}, u32[]{:S(2)}) copy-start(f32[1536]{0:T(1024)S(1)} %get-tuple-element.31) | copy-start | bytes 18436
  21.9 30.1 %copy-start.69 = (f32[1536]{0:T(1024)}, f32[1536]{0:T(1024)S(1)}, u32[]{:S(2)}) copy-start(f32[1536]{0:T(1024)S(1)} %get-tuple-element.32) | copy-start | bytes 18436
  21.9 30.1 %copy-start.71 = (f32[1536]{0:T(1024)}, f32[1536]{0:T(1024)S(1)}, u32[]{:S(2)}) copy-start(f32[1536]{0:T(1024)S(1)} %get-tuple-element.33) | copy-start | bytes 18436
  21.9 30.1 %copy-start.73 = (f32[1536]{0:T(1024)}, f32[1536]{0:T(1024)S(1)}, u32[]{:S(2)}) copy-start(f32[1536]{0:T(1024)S(1)} %get-tuple-element.35) | copy-start | bytes 18436
  34.8 11.4 %copy-start.77 = (f32[16,128]{1,0:T(8,128)}, f32[16,128]{1,0:T(8,128)S(1)}, u32[]{:S(2)}) copy-start(f32[16,128]{1,0:T(8,128)S(1)} %fusion.12) | copy-start | bytes 24580
  37.6 14.2 %copy-start.96 = (f32[128]{0:T(128)}, f32[128]{0:T(128)S(1)}, u32[]{:S(2)}) copy-start(f32[128]{0:T(128)S(1)} %get-tuple-element.111) | copy-start | bytes 1540
  37.6 14.4 %copy-start.75 = (f32[1536]{0:T(1024)S(1)}, f32[1536]{0:T(1024)}, u32[]{:S(2)}) copy-start(f32[1536]{0:T(1024)} %get-tuple-element.34) | copy-start | bytes 18436
  38.1 8.7 %collective-permute-start.2 = (bf16[16,1536]{1,0:T(8,128)(2,1)S(1)}, bf16[16,1536]{1,0:T(8,128)(2,1)S(1)}, u32[]{:S(2)}, u32[]{:S(2)}) collective-permute-start(bf16[16,1536]{1,0:T(8,128)(2,1)S(1)} %get-tuple-element.96), channel_id=1, source_target_pairs={{0,4},{4,8},{8,12},{12,16},{16,20},{20,24},{24,28},{28,32},{32,36}... | collective-permute-start | bytes 147464 | tf_op jit(solution)/shard_map/ppermute | solution.py:22
  44.1 7.5 %collective-permute-start.3 = (bf16[16,1536]{1,0:T(8,128)(2,1)S(1)}, bf16[16,1536]{1,0:T(8,128)(2,1)S(1)}, u32[]{:S(2)}, u32[]{:S(2)}) collective-permute-start(bf16[16,1536]{1,0:T(8,128)(2,1)S(1)} %get-tuple-element.97), channel_id=1, source_target_pairs={{4,0},{8,4},{12,8},{16,12},{20,16},{24,20},{28,24},{32,28},{36,32}... | collective-permute-start | bytes 147464 | tf_op jit(solution)/shard_map/ppermute | solution.py:24
  74.0 10.2 %copy-start.22 = (bf16[32,1536]{1,0:T(8,128)(2,1)S(1)}, bf16[32,1536]{1,0:T(8,128)(2,1)}, u32[]{:S(2)}) copy-start(bf16[32,1536]{1,0:T(8,128)(2,1)} %get-tuple-element.99) | copy-start | bytes 294916
  74.0 10.2 %copy-start.90 = (pred[4,32]{1,0:T(4,128)(4,1)S(1)}, pred[4,32]{1,0:T(4,128)(4,1)}, u32[]{:S(2)}) copy-start(pred[4,32]{1,0:T(4,128)(4,1)} %copy-done.89) | copy-start | bytes 388
  79.8 11.6 %copy-start.84 = (f32[128]{0:T(128)S(1)}, f32[128]{0:T(128)}, u32[]{:S(2)}) copy-start(f32[128]{0:T(128)} %compare_convert_fusion) | copy-start | bytes 1540
  79.8 13.5 %copy-start.92 = (f32[128]{0:T(128)S(1)}, f32[128]{0:T(128)}, u32[]{:S(2)}) copy-start(f32[128]{0:T(128)} %copy-done.91) | copy-start | bytes 1540
  79.8 10.5 %collective-permute-start.4 = (bf16[16,1536]{1,0:T(8,128)(2,1)S(1)}, bf16[16,1536]{1,0:T(8,128)(2,1)S(1)}, u32[]{:S(2)}, u32[]{:S(2)}) collective-permute-start(bf16[16,1536]{1,0:T(8,128)(2,1)S(1)} %get-tuple-element.94), channel_id=1, source_target_pairs={{0,4},{4,8},{8,12},{12,16},{16,20},{20,24},{24,28},{28,32},{32,36}... | collective-permute-start | bytes 147464 | tf_op jit(solution)/shard_map/ppermute | solution.py:22
  81.7 8.6 %collective-permute-start.5 = (bf16[16,1536]{1,0:T(8,128)(2,1)S(1)}, bf16[16,1536]{1,0:T(8,128)(2,1)}, u32[]{:S(2)}, u32[]{:S(2)}) collective-permute-start(bf16[16,1536]{1,0:T(8,128)(2,1)S(1)} %get-tuple-element.95), channel_id=1, source_target_pairs={{4,0},{8,4},{12,8},{16,12},{20,16},{24,20},{28,24},{32,28},{36,32}... | collective-permute-start | bytes 147464 | tf_op jit(solution)/shard_map/ppermute | solution.py:24
  85.7 46.5 %all-to-all-start = ((bf16[4,32,1536]{2,1,0:T(8,128)(2,1)}), bf16[4,32,1536]{2,1,0:T(8,128)(2,1)}, u32[]{:S(2)}, u32[]{:S(2)}) async-start(bf16[4,32,1536]{2,1,0:T(8,128)(2,1)} %broadcast_select_fusion), calls=%async_computation | async-start | bytes 786432 | tf_op jit(solution)/shard_map/all_to_all | solution.py:205
  120.2 9.2 %copy-start.8 = (bf16[16,128,256]{2,1,0:T(8,128)(2,1)S(1)}, bf16[16,128,256]{2,1,0:T(8,128)(2,1)}, u32[]{:S(2)}) copy-start(bf16[16,128,256]{2,1,0:T(8,128)(2,1)} %get-tuple-element.114) | copy-start | bytes 3145732
  121.7 12.4 %collective-permute-start.6 = (bf16[64,3072]{1,0:T(8,128)(2,1)S(1)}, bf16[64,3072]{1,0:T(8,128)(2,1)}, u32[]{:S(2)}, u32[]{:S(2)}) collective-permute-start(bf16[64,3072]{1,0:T(8,128)(2,1)S(1)} %get-tuple-element.47), channel_id=1, source_target_pairs={{0,4},{4,8},{8,12},{12,16},{16,20},{20,24},{24,28},{28,32},{32,36}... | collective-permute-start | bytes 1179656 | tf_op jit(solution)/shard_map/ppermute | solution.py:22
  127.4 11.3 %collective-permute-start.7 = (bf16[64,3072]{1,0:T(8,128)(2,1)S(1)}, bf16[64,3072]{1,0:T(8,128)(2,1)}, u32[]{:S(2)}, u32[]{:S(2)}) collective-permute-start(bf16[64,3072]{1,0:T(8,128)(2,1)S(1)} %get-tuple-element.48), channel_id=1, source_target_pairs={{4,0},{8,4},{12,8},{16,12},{20,16},{24,20},{28,24},{32,28},{36,32}... | collective-permute-start | bytes 1179656 | tf_op jit(solution)/shard_map/ppermute | solution.py:24
  138.7 10.1 %slice-start.2 = ((s8[4718592]{0:T(1024)(128)(4,1)}), s8[4194304]{0:T(1024)(128)(4,1)S(1)}, s32[]{:S(2)}) async-start(s8[4718592]{0:T(1024)(128)(4,1)} %bitcast.85), calls=%async_computation.4 | async-start | bytes 8388608
  (64 other events, 239.1 us)
where the time goes:
time: 153 us; the launch traced here: 152 us
  other arithmetic  42.4 us (28%)
  matrix products  36 us (24%)
  starting transfers between devices  34.7 us (23%)
  local copies, waits for them, and re-layouts  27 us (18%)
  waiting for transfers between devices  9.4 us (6%)
  between operations  2.28 us (1%)
    ppermute x4, starting transfers between devices, extended(): lax.ppermute(tail, axis, [(i, (i + 1) % count) for i in range(ends)])  17.6 us
    unnamed x208, local copies, waits for them, and re-layouts  13 us
    ppermute x4, waiting for transfers between devices, extended(): lax.ppermute(head, axis, [((i + 1) % count, i) for i in range(ends)])  9.38 us
    ppermute x4, starting transfers between devices, extended(): lax.ppermute(head, axis, [((i + 1) % count, i) for i in range(ends)])  8.35 us
    dot_general x2, matrix products, project(): jnp.dot(normed, w_value, preferred_element_type=jnp.float32)  7.48 us
    mul x3, other arithmetic, finish(): kernel[lag_index] * padded_float[lag_index:lag_index + frame_rows]  7.25 us
    another operation x4, other arithmetic  7.07 us
    dot_general x3, matrix products, attend(): jnp.einsum('qhd,khd->hqk', query_float, key_heads) * head_size ** (-0.5)  6.2 us
  transfers between devices with their start and end apart: 10, of which 2 were waited for; matrix products, arithmetic and copies ran while one was open for 31% of the time, Pallas kernels for 0%

commit v1 on v0

v1 whole, which is shorter than its diff:
```python
import functools

import jax
import jax.numpy as jnp
from jax import lax
from jax.experimental import pallas as pl
from jax.experimental.pallas import tpu as pltpu
from jax.sharding import PartitionSpec as P

D = 1536
REACH = 64
KERN = 32
FR = 128
HALO = 96
EXT = FR + 2 * HALO
QR = FR + 64
SR = FR + 32
PR = SR // 4
LR = FR // 4
SLOTS = 64
NREC = 4
HEAD = 96
LANE = 128
NB = D // LANE
COL = 256
NC = D // COL
GROUP = 4 * HEAD
EPSILON = 1e-06
SCALE = HEAD ** (-0.5)
BF = jnp.bfloat16
F32 = jnp.float32
WINDOWS = ((0, 1), (0, 2), (1, 3), (2, 3))

ANY = pl.BlockSpec(memory_space=pl.ANY)
SMEM = pl.BlockSpec(memory_space=pltpu.SMEM)


def dot(a, b):
    return lax.dot_general(a, b, (((1,), (0,)), ((), ())), preferred_element_type=F32)


def dot_t(a, b):
    return lax.dot_general(a, b, (((1,), (1,)), ((), ())), preferred_element_type=F32)


def t_dot(a, b):
    return lax.dot_general(a, b, (((0,), (0,)), ((), ())), preferred_element_type=F32)


def lanes(c, width=LANE):
    return pl.ds(pl.multiple_of(c * width, width), width)


def routes(fc, tl, slice_index):
    starts, lives = [], []
    total = 0
    for b in range(NREC):
        live = jnp.clip(fc[b] // 4 - slice_index * LR, 0, LR)
        total = total + tl[slice_index, b]
        starts.append(total)
        lives.append(live)
        total = total + live
    return starts, lives


def pick(values, index):
    out = values[0]
    for b in range(1, NREC):
        out = jnp.where(index == b, values[b], out)
    return out


def prepare(fc, tl, audio, grads, send_a, send_b, o0, o1, o2, o3, g_buf, o_buf, sems):
    tm = lax.axis_index("tm")
    llm = lax.axis_index("llm")
    off_a = (1 - tm % 2) * (FR - HALO)
    off_b = (FR - HALO) - off_a
    ca = pltpu.make_async_copy(audio.at[pl.ds(pl.multiple_of(off_a, 32), HALO)], send_a, sems.at[0])
    cb = pltpu.make_async_copy(audio.at[pl.ds(pl.multiple_of(off_b, 32), HALO)], send_b, sems.at[1])
    cg = pltpu.make_async_copy(grads, g_buf, sems.at[2])
    cg.start()
    ca.start()
    cb.start()
    starts, lives = routes(fc, tl, tm)
    row = lax.broadcasted_iota(jnp.int32, (LR, SLOTS), 0)
    slot = lax.broadcasted_iota(jnp.int32, (LR, SLOTS), 1) + llm * SLOTS
    cg.wait()
    copies = []
    for j, out in enumerate((o0, o1, o2, o3)):
        b = llm ^ j
        chosen = (row < pick(lives, b)) & (slot == row + pick(starts, b))
        o_buf[j] = dot(jnp.where(chosen, 1.0, 0.0).astype(BF), g_buf[...]).astype(BF)
        copy = pltpu.make_async_copy(o_buf.at[j], out, sems.at[3 + j])
        copy.start()
        copies.append(copy)
    for copy in [ca, cb] + copies:
        copy.wait()


def main_kernel(
    fc, audio, recv_a, recv_b, lat_grad, edge_a, edge_b, w_query, w_key, w_value, w_out,
    norm_gain, conv_gain, latent_gain, taps,
    latent_out, dhid_out, dn_out, send_a, send_b,
    x_s, n_s, q_s, k_s, v_s, wq_s, wk_s, wv_s, wo_s, ng_s, cg_s, lg_s, tap_s,
    att_s, p_s, bias_s, biasl_s, biasr_s, h_s, ci_s, dsilu_s, up_s, pool_s, g_s, gst_s, norm_t, lat_s,
    ds_s, us_s, dnc_s, dhid_s, datt_s, dq_s, dk_s, dv_s, dn_s, edge_s, w_sems, sems,
):
    tm = lax.axis_index("tm")
    llm = lax.axis_index("llm")
    n_tm = lax.axis_size("tm")
    even = tm % 2 == 0
    parity = tm % 2
    first = tm * FR
    total = n_tm * FR
    limit = fc[llm]

    left_row = pl.multiple_of((1 - parity) * (HALO + FR), 32)
    right_row = pl.multiple_of(parity * (HALO + FR), 32)
    small = [
        pltpu.make_async_copy(audio, x_s.at[pl.ds(HALO, FR)], sems.at[0]),
        pltpu.make_async_copy(recv_a, x_s.at[pl.ds(left_row, HALO)], sems.at[1]),
        pltpu.make_async_copy(recv_b, x_s.at[pl.ds(right_row, HALO)], sems.at[2]),
        pltpu.make_async_copy(norm_gain, ng_s, sems.at[3]),
    ]
    late = [
        pltpu.make_async_copy(conv_gain, cg_s, sems.at[4]),
        pltpu.make_async_copy(latent_gain, lg_s, sems.at[5]),
        pltpu.make_async_copy(taps, tap_s, sems.at[6]),
        pltpu.make_async_copy(lat_grad, gst_s.at[pl.ds(16, LR)], sems.at[7]),
        pltpu.make_async_copy(edge_a, gst_s.at[pl.ds(pl.multiple_of((1 - parity) * 48, 16), 16)], sems.at[8]),
        pltpu.make_async_copy(edge_b, gst_s.at[pl.ds(pl.multiple_of(parity * 48, 16), 16)], sems.at[9]),
    ]
    for copy in small:
        copy.start()

    def w_copy(n, j):
        src = (w_key, w_value, w_query, w_out)[n]
        dst = (wk_s, wv_s, wq_s, wo_s)[n]
        return pltpu.make_async_copy(src.at[:, lanes(j, COL)], dst.at[:, lanes(j, COL)], w_sems.at[n, j])

    for n in range(4):
        for j in range(NC):
            w_copy(n, j).start()
    for copy in late:
        copy.start()

    def bias_of(rows, cols, q_first, k_first):
        qe = lax.broadcasted_iota(jnp.int32, (rows, cols), 0) + q_first
        ke = lax.broadcasted_iota(jnp.int32, (rows, cols), 1) + k_first
        kt = ke + (first - HALO)
        ok = (ke >= qe - REACH) & (ke < qe + REACH) & (kt >= 0) & (kt < total) & ((kt < limit) | (ke == qe))
        return jnp.where(ok, 0.0, -1e30)

    bias_s[...] = bias_of(FR, 256, HALO, 32)
    biasl_s[...] = bias_of(32, 160, 64, 0)
    biasr_s[...] = bias_of(32, 160, 224, 160)

    for copy in small:
        copy.wait()

    @pl.loop(0, EXT // 64)
    def _(r):
        rows = pl.ds(pl.multiple_of(r * 64, 64), 64)
        x = x_s[rows, :].astype(F32)
        inv = lax.rsqrt(jnp.mean(x * x, axis=-1, keepdims=True) + EPSILON)
        n_s[rows, :] = (x * inv * ng_s[...]).astype(BF)

    for n, (w_s, out_s, lo, hi) in enumerate(
        ((wk_s, k_s, 0, EXT), (wv_s, v_s, 0, EXT), (wq_s, q_s, 64, 64 + QR))
    ):
        @pl.loop(0, NC)
        def _(j, n=n, w_s=w_s, out_s=out_s, lo=lo, hi=hi):
            w_copy(n, j).wait()
            out_s[:, lanes(j, COL)] = dot(n_s[lo:hi, :], w_s[:, lanes(j, COL)]).astype(BF)

    lane_of = lax.broadcasted_iota(jnp.int32, (1, GROUP), 1)

    def head_mask(j, lo, hi):
        lane = lane_of[:, : (hi - lo) * LANE] + lo * LANE
        return jnp.where((lane >= j * HEAD) & (lane < (j + 1) * HEAD), 1.0, 0.0).astype(BF)

    def softmax(scores):
        powers = jnp.exp(scores - jnp.max(scores, axis=-1, keepdims=True))
        return powers * (1.0 / jnp.sum(powers, axis=-1, keepdims=True))

    def window(g, lo, hi):
        return pl.ds(pl.multiple_of(g * GROUP + lo * LANE, LANE), (hi - lo) * LANE)

    def add_tiles(tiles, lo, value):
        for t in range(value.shape[1] // LANE):
            part = value[:, t * LANE : (t + 1) * LANE]
            tiles[lo + t] = part if tiles[lo + t] is None else tiles[lo + t] + part

    @pl.loop(0, 4)
    def _(g):
        own, left, right = [None] * 3, [None] * 3, [None] * 3
        for j, (lo, hi) in enumerate(WINDOWS):
            win = window(g, lo, hi)
            mask = head_mask(j, lo, hi)
            q = q_s[:, win] * mask
            k = k_s[:, win]
            v = v_s[:, win] * mask
            p = softmax(dot_t(q[32:160], k[32:288]) * SCALE + bias_s[...]).astype(BF)
            p_s[g * 4 + j] = p
            add_tiles(own, lo, dot(p, v[32:288]))
            p = softmax(dot_t(q[0:32], k[0:160]) * SCALE + biasl_s[...]).astype(BF)
            add_tiles(left, lo, dot(p, v[0:160]))
            p = softmax(dot_t(q[160:192], k[160:320]) * SCALE + biasr_s[...]).astype(BF)
            add_tiles(right, lo, dot(p, v[160:320]))
        for t in range(3):
            at = window(g, t, t + 1)
            att_s[0:32, at] = left[t].astype(BF)
            att_s[32:160, at] = own[t].astype(BF)
            att_s[160:192, at] = right[t].astype(BF)

    def hidden_step(j, squares):
        w_copy(3, j).wait()
        cols = lanes(j, COL)
        h = dot(att_s[...], wo_s[:, cols]) + x_s[64 : 64 + QR, cols].astype(F32)
        h = h.astype(BF).astype(F32)
        h_s[2 * j] = h[:, :LANE]
        h_s[2 * j + 1] = h[:, LANE:]
        return squares + h[:, :LANE] * h[:, :LANE] + h[:, LANE:] * h[:, LANE:]

    squares = lax.fori_loop(0, NC, hidden_step, jnp.zeros((QR, LANE), F32))
    inv_h = lax.rsqrt(jnp.sum(squares, axis=-1, keepdims=True) * (1.0 / D) + EPSILON)
    frame = lax.broadcasted_iota(jnp.int32, (QR, 1), 0) + (first - 32)
    spoken = jnp.where((frame >= 0) & (frame < limit), 1.0, 0.0)
    inv_spoken = inv_h * spoken

    for copy in late:
        copy.wait()

    row = lax.broadcasted_iota(jnp.int32, (PR, 64), 0)
    col = lax.broadcasted_iota(jnp.int32, (PR, 64), 1)
    at = tm * LR + row - 4
    chosen = (col == row + 12) & (at >= 0) & (at < n_tm * LR)
    g_s[...] = dot(jnp.where(chosen, 1.0, 0.0).astype(BF), gst_s[...])

    def conv_step(c, carry):
        squares, along = carry
        cols = lanes(c)
        ci_s[...] = (h_s[c] * inv_spoken * cg_s[:, cols]).astype(BF).astype(F32)
        kern = tap_s[:, cols]
        acc = jnp.zeros((SR, LANE), F32)
        for s in range(8):
            xs = ci_s[s : s + SR + 24, :]
            for u in range(4):
                m = s + 8 * u
                acc = acc + kern[m : m + 1, :] * xs[8 * u : 8 * u + SR]
        sig = 1.0 / (1.0 + jnp.exp(-acc))
        silu = acc * sig
        dsilu_s[c] = sig + silu * (1.0 - sig)
        up_s[...] = h_s[c, 16 : 16 + SR, :] + silu
        pooled = up_s[pl.ds(0, PR, 4), :]
        for u in range(1, 4):
            pooled = pooled + up_s[pl.ds(u, PR, 4), :]
        pooled = pooled * 0.25
        pool_s[c] = pooled
        return squares + pooled * pooled, along + g_s[:, cols] * lg_s[:, cols] * pooled

    zero = jnp.zeros((PR, LANE), F32)
    squares, along = lax.fori_loop(0, NB, conv_step, (zero, zero))
    inv_p = lax.rsqrt(jnp.sum(squares, axis=-1, keepdims=True) * (1.0 / D) + EPSILON)
    back_p = inv_p * inv_p * inv_p * (jnp.sum(along, axis=-1, keepdims=True) * (1.0 / D))

    inv_own = inv_h[32:160]
    spoken_own = spoken[32:160]

    def conv_back(c, along):
        cols = lanes(c)
        pooled = pool_s[c]
        gain = lg_s[:, cols]
        norm_t[...] = pooled * inv_p * gain
        lat_s[:, cols] = norm_t[4:36, :].astype(BF)
        dpool = (g_s[:, cols] * gain * inv_p - pooled * back_p) * 0.25
        for u in range(4):
            up_s[pl.ds(u, PR, 4), :] = dpool
        ds_s[...] = up_s[...] * dsilu_s[c]
        us_s[c] = up_s[16 : 16 + FR, :]
        kern = tap_s[:, cols]
        acc = jnp.zeros((FR, LANE), F32)
        for s in range(8):
            base = 8 if s == 0 else s
            xs = ds_s[base : base + FR + 24, :]
            for u in range(4):
                m = 32 - base - 8 * u
                acc = acc + kern[m : m + 1, :] * xs[8 * u : 8 * u + FR]
        dn = acc.astype(BF).astype(F32) * spoken_own * cg_s[:, cols]
        dnc_s[c] = dn
        return along + dn * h_s[c, 32:160, :]

    along = lax.fori_loop(0, NB, conv_back, jnp.zeros((FR, LANE), F32))
    latent_copy = pltpu.make_async_copy(lat_s, latent_out, sems.at[10])
    latent_copy.start()
    back_h = inv_own * inv_own * inv_own * (jnp.sum(along, axis=-1, keepdims=True) * (1.0 / D))

    @pl.loop(0, NB)
    def _(c):
        dhid_s[:, lanes(c)] = (us_s[c] + dnc_s[c] * inv_own - h_s[c, 32:160, :] * back_h).astype(BF)

    dhid_copy = pltpu.make_async_copy(dhid_s, dhid_out, sems.at[11])
    dhid_copy.start()

    @pl.loop(0, NC)
    def _(j):
        datt_s[:, lanes(j, COL)] = dot_t(dhid_s[...], wo_s[lanes(j, COL), :]).astype(BF)

    @pl.loop(0, 4)
    def _(g):
        dq, dk, dv = [None] * 3, [None] * 3, [None] * 3
        for j, (lo, hi) in enumerate(WINDOWS):
            win = window(g, lo, hi)
            mask = head_mask(j, lo, hi)
            q = q_s[32:160, win] * mask
            k = k_s[32:288, win] * mask
            v = v_s[32:288, win]
            do = datt_s[:, win] * mask
            p = p_s[g * 4 + j]
            dp = dot_t(do, v)
            pf = p.astype(F32)
            pd = pf * dp
            ds = ((pd - pf * jnp.sum(pd, axis=-1, keepdims=True)) * SCALE).astype(BF)
            add_tiles(dq, lo, dot(ds, k))
            add_tiles(dk, lo, t_dot(ds, q))
            add_tiles(dv, lo, t_dot(p, do))
        for t in range(3):
            at = window(g, t, t + 1)
            dq_s[:, at] = dq[t].astype(BF)
            dk_s[:, at] = dk[t].astype(BF)
            dv_s[:, at] = dv[t].astype(BF)

    @pl.loop(0, NC)
    def _(j):
        cols = lanes(j, COL)
        both = dot_t(dk_s[...], wk_s[cols, :]) + dot_t(dv_s[...], wv_s[cols, :])
        dn_s[:, cols] = both[64:192] + dot_t(dq_s[...], wq_s[cols, :])
        edge_s[0:64, cols] = both[0:64].astype(BF)
        edge_s[64:128, cols] = both[192:256].astype(BF)

    row_a = pl.multiple_of((1 - parity) * 64, 64)
    row_b = pl.multiple_of(parity * 64, 64)
    outs = [
        pltpu.make_async_copy(edge_s.at[pl.ds(row_a, 64)], send_a, sems.at[12]),
        pltpu.make_async_copy(edge_s.at[pl.ds(row_b, 64)], send_b, sems.at[13]),
        pltpu.make_async_copy(dn_s, dn_out, sems.at[14]),
    ]
    for copy in outs:
        copy.start()
    for copy in [latent_copy, dhid_copy] + outs:
        copy.wait()


def finish(
    fc, tl, audio, dhid, dn, recv_a, recv_b, l0, l1, l2, l3, norm_gain,
    rows_out, grad_out,
    x_s, dh_s, dn_s, r_s, lat_s, ng_s, out_s, rows_s, sems,
):
    tm = lax.axis_index("tm")
    llm = lax.axis_index("llm")
    parity = tm % 2
    copies = [
        pltpu.make_async_copy(audio, x_s, sems.at[0]),
        pltpu.make_async_copy(dhid, dh_s, sems.at[1]),
        pltpu.make_async_copy(dn, dn_s, sems.at[2]),
        pltpu.make_async_copy(recv_a, r_s.at[pl.ds(pl.multiple_of((1 - parity) * 64, 64), 64)], sems.at[3]),
        pltpu.make_async_copy(recv_b, r_s.at[pl.ds(pl.multiple_of(parity * 64, 64), 64)], sems.at[4]),
        pltpu.make_async_copy(norm_gain, ng_s, sems.at[5]),
    ]
    lat_copies = [
        pltpu.make_async_copy(source, lat_s.at[pl.ds(j * LR, LR)], sems.at[6 + j])
        for j, source in enumerate((l0, l1, l2, l3))
    ]
    for copy in copies + lat_copies:
        copy.start()
    starts, lives = routes(fc, tl, tm)
    slot = lax.broadcasted_iota(jnp.int32, (SLOTS, NREC * LR), 0) + llm * SLOTS
    col = lax.broadcasted_iota(jnp.int32, (SLOTS, NREC * LR), 1)
    chosen = jnp.zeros((SLOTS, NREC * LR), F32)
    for j in range(NREC):
        b = llm ^ j
        r = col - j * LR
        hit = (r >= 0) & (r < pick(lives, b)) & (slot == r + pick(starts, b))
        chosen = jnp.where(hit, 1.0, chosen)
    for copy in copies:
        copy.wait()
    keep_left = jnp.where(tm > 0, 1.0, 0.0)
    keep_right = jnp.where(tm < lax.axis_size("tm") - 1, 1.0, 0.0)
    for half in range(2):
        rows = slice(half * 64, half * 64 + 64)
        keep = keep_left if half == 0 else keep_right
        x = x_s[rows, :].astype(F32)
        inv = lax.rsqrt(jnp.mean(x * x, axis=-1, keepdims=True) + EPSILON)
        g = (dn_s[rows, :] + r_s[rows, :].astype(F32) * keep).astype(BF).astype(F32) * ng_s[...]
        back = inv * inv * inv * jnp.mean(g * x, axis=-1, keepdims=True)
        out_s[rows, :] = (dh_s[rows, :].astype(F32) + g * inv - x * back).astype(BF)
    grad_copy = pltpu.make_async_copy(out_s, grad_out, sems.at[10])
    grad_copy.start()
    for copy in lat_copies:
        copy.wait()
    rows_s[...] = dot(chosen.astype(BF), lat_s[...]).astype(BF)
    rows_copy = pltpu.make_async_copy(rows_s, rows_out, sems.at[11])
    rows_copy.start()
    grad_copy.wait()
    rows_copy.wait()


def swap(count, cells_a, cells_b):
    pairs_a = [(i, i ^ 1) for i in range(count)]
    pairs_b = [(i, min(max(((i + 1) ^ 1) - 1, 0), count - 1)) for i in range(count)]
    return lax.ppermute(cells_a, "tm", pairs_a), lax.ppermute(cells_b, "tm", pairs_b)


def exchange(count, cells):
    return [
        lax.ppermute(cells[j], "llm", [(i, i ^ j) for i in range(count)]) for j in range(1, count)
    ]


def call(kernel, outs, scratch, specs, name, limit, flops):
    return pl.pallas_call(
        kernel,
        out_shape=outs,
        in_specs=specs,
        out_specs=[ANY] * len(outs),
        scratch_shapes=scratch,
        compiler_params=pltpu.CompilerParams(vmem_limit_bytes=limit),
        cost_estimate=pl.CostEstimate(flops=flops, bytes_accessed=4_000_000, transcendentals=0),
        name=name,
    )


def shape(rows, dtype=BF, cols=D):
    return jax.ShapeDtypeStruct((rows, cols), dtype)


MIB = 1024 * 1024


def on_device(
    audio, frame_counts, text_lengths, norm_gain, w_query, w_key, w_value, w_out,
    conv_gain, conv_kernel, latent_gain, llm_grads,
):
    signal = audio[0]
    n_tm = lax.axis_size("tm")
    n_llm = lax.axis_size("llm")
    norm_row, conv_row, latent_row = (g.reshape(1, D) for g in (norm_gain, conv_gain, latent_gain))
    V = pltpu.VMEM
    dma = pltpu.SemaphoreType.DMA

    send_a, send_b, o0, o1, o2, o3 = call(
        prepare,
        [shape(HALO)] * 2 + [shape(LR)] * 4,
        [V((SLOTS, D), BF), V((NREC, LR, D), BF), dma((7,))],
        [SMEM, SMEM, ANY, ANY],
        "prepare", 8 * MIB, 10_000_000,
    )(frame_counts, text_lengths, signal, llm_grads[0])
    recv_a, recv_b = swap(n_tm, send_a, send_b)
    came = exchange(n_llm, [o0, o1, o2, o3])
    lat_grad = o0 + came[0] + came[1] + came[2]
    even = lax.axis_index("tm") % 2 == 0
    edge_a, edge_b = swap(
        n_tm,
        jnp.where(even, lat_grad[16:], lat_grad[:16]),
        jnp.where(even, lat_grad[:16], lat_grad[16:]),
    )

    latent, dhid, dn, back_a, back_b = call(
        main_kernel,
        [shape(LR), shape(FR), shape(FR, F32), shape(64), shape(64)],
        [
            V((EXT, D), BF), V((EXT, D), BF), V((QR, D), BF), V((EXT, D), BF), V((EXT, D), BF),
            V((D, D), BF), V((D, D), BF), V((D, D), BF), V((D, D), BF),
            V((1, D), F32), V((1, D), F32), V((1, D), F32), V((KERN, D), F32),
            V((QR, D), BF), V((16, FR, 256), BF), V((FR, 256), F32), V((32, 160), F32), V((32, 160), F32),
            V((NB, QR, LANE), F32), V((QR, LANE), F32), V((NB, SR, LANE), F32), V((SR, LANE), F32),
            V((NB, PR, LANE), F32), V((PR, D), F32), V((64, D), BF), V((PR, LANE), F32), V((LR, D), BF),
            V((SR, LANE), F32), V((NB, FR, LANE), F32), V((NB, FR, LANE), F32), V((FR, D), BF),
            V((FR, D), BF), V((FR, D), BF), V((256, D), BF), V((256, D), BF), V((FR, D), F32), V((FR, D), BF),
            dma((4, NC)), dma((15,)),
        ],
        [SMEM] + [ANY] * 14,
        "main", 50 * MIB, 10_000_000_000,
    )(
        frame_counts, signal, recv_a, recv_b, lat_grad, edge_a, edge_b,
        w_query, w_key, w_value, w_out, norm_row, conv_row, latent_row, conv_kernel,
    )
    ret_a, ret_b = swap(n_tm, back_a, back_b)
    others = exchange(n_llm, [latent] * n_llm)
    rows, grad = call(
        finish,
        [shape(SLOTS), shape(FR)],
        [
            V((FR, D), BF), V((FR, D), BF), V((FR, D), F32), V((FR, D), BF), V((NREC * LR, D), BF),
            V((1, D), F32), V((FR, D), BF), V((SLOTS, D), BF), dma((12,)),
        ],
        [SMEM, SMEM] + [ANY] * 10,
        "finish", 8 * MIB, 10_000_000,
    )(frame_counts, text_lengths, signal, dhid, dn, ret_a, ret_b, latent, *others, norm_row)
    return (rows[None], grad[None])


def solution(mesh):
    placed = (P("llm", "tm", None),) + (P(),) * 10 + (P("tm", "llm", None),)
    return jax.shard_map(
        on_device,
        mesh=mesh,
        in_specs=placed,
        out_specs=(P("tm", "llm", None), P("llm", "tm", None)),
        check_vma=False,
    )
```

time: 153 us -> 82.1 us (0.54)
  Pallas kernels: 0 us -> 44.9 us
  other arithmetic: 42.4 us -> 0.03 us
  matrix products: 36 us -> 0 us
  local copies, waits for them, and re-layouts: 27 us -> 8.02 us
  starting transfers between devices: 34.7 us -> 20.8 us
  waiting for transfers between devices: 9.4 us -> 7.07 us
    pallas_call x0 -> x3, Pallas kernels: none -> 44.9 us  [the longest x1 38.8 us: on_device(): call(main_kernel, [shape(LR), shape(FR), shape(FR, F32), shape(64), shape...]
    dot_general x16 -> x0, matrix products: 36 us -> none  [the longest x2 7.48 us: project(): jnp.dot(normed, w_value, preferred_element_type=jnp.float32)]
    reduce_sum x9 -> x0, other arithmetic: 10.2 us -> none  [the longest x1 2.91 us: attend(): highest = jnp.max(scores, axis=-1, keepdims=True)]
    all_to_all x2 -> x0, starting transfers between devices: 8.71 us -> none  [the longest x1 4.53 us: on_device(): lax.all_to_all(outgoing, 'llm', split_axis=0, concat_axis=0, tiled=True)]
    add x6 -> x1, other arithmetic: 7.49 us -> 0.02 us  [on_device(): lat_grad = o0 + came[0] + came[1] + came[2]]
    mul x4 -> x0, other arithmetic: 7.25 us -> none  [the longest x3 7.25 us: finish(): kernel[lag_index] * padded_float[lag_index:lag_index + frame_rows]]
    unnamed x208 -> x13, local copies, waits for them, and re-layouts: 13 us -> 5.91 us
    another operation x5 -> x0, other arithmetic: 7.11 us -> none
  transfers between devices with their start and end apart: 10 -> 12, of which waited for: 2 -> 5; matrix products, arithmetic and copies ran while one was open for 31% -> 3% of each run, Pallas kernels for 0% -> 0%
where the time goes in v1:
time: 82.1 us; the launch traced here: 81.6 us
  Pallas kernels  44.9 us (55%)
  starting transfers between devices  20.8 us (25%)
  local copies, waits for them, and re-layouts  8.02 us (10%)
  waiting for transfers between devices  7.07 us (9%)
    pallas_call x1, Pallas kernels, on_device(): call(main_kernel, [shape(LR), shape(FR), shape(FR, F32), shape(64), shape...  38.8 us
    ppermute x3, starting transfers between devices, swap(): lax.ppermute(cells_b, 'tm', pairs_b)  11.9 us
    ppermute x6, starting transfers between devices, exchange(): lax.ppermute(cells[j], 'llm', [(i, i ^ j) for i in range(count)])  7.33 us
    ppermute x6, waiting for transfers between devices, exchange(): lax.ppermute(cells[j], 'llm', [(i, i ^ j) for i in range(count)])  6 us
    unnamed x13, local copies, waits for them, and re-layouts  5.91 us
    pallas_call x1, Pallas kernels, on_device(): call(finish, [shape(SLOTS), shape(FR)], [V((FR, D), BF), V((FR, D), BF),...  3.73 us
    pallas_call x1, Pallas kernels, on_device(): call(prepare, [shape(HALO)] * 2 + [shape(LR)] * 4, [V((SLOTS, D), BF), V(...  2.4 us
    reshape x3, local copies, waits for them, and re-layouts, on_device(): g.reshape(1, D)  2.11 us
  transfers between devices with their start and end apart: 12, of which 5 were waited for; matrix products, arithmetic and copies ran while one was open for 3% of the time, Pallas kernels for 0%

profile of v1, /device:TPU:39, one launch (start us, length us, event | category | flops | bytes accessed | tf_op | source)
XLA Modules:
  0.0 81.6 jit_solution(10883860819827793468)
XLA Ops:
  0.6 0.8 copy.15.tl
  1.4 0.0 copy-start
  1.4 1.0 %copy-done = bf16[1,128,1536]{2,1,0:T(8,128)(2,1)S(1)} copy-done((bf16[1,128,1536]{2,1,0:T(8,128)(2,1)S(1)}, bf16[1,128,1536]{2,1,0:T(8,128)(2,1)}, u32[]{:S(2)}) %copy-start) | copy-done | bytes 393240
  2.4 0.0 copy-start.2
  2.4 0.9 %copy-done.2 = bf16[1,64,1536]{2,1,0:T(8,128)(2,1)S(1)} copy-done((bf16[1,64,1536]{2,1,0:T(8,128)(2,1)S(1)}, bf16[1,64,1536]{2,1,0:T(8,128)(2,1)}, u32[]{:S(2)}) %copy-start.2) | copy-done | bytes 196632
  3.3 0.0 copy-start.3
  3.3 0.7 copy-done.3
  4.0 2.4 %prepare.1 = (bf16[96,1536]{1,0:T(8,128)(2,1)S(1)}, bf16[96,1536]{1,0:T(8,128)(2,1)S(1)}, bf16[32,1536]{1,0:T(8,128)(2,1)S(1)}, bf16[32,1536]{1,0:T(8,128)(2,1)S...) custom-call(s32[4]{0:T(128)S(1)} %copy-done.3, s32[32,4]{1,0:T(8,128)S(1)} %copy.15.tl, ...), custom_call_target="tpu_custom_call" | custom-call | flops 10000000 | bytes 4000000 | tf_op jit(solution)/shard_map/prepare/pallas_call | solution.py:451
  6.4 1.4 %collective-permute-start.2 = (bf16[32,1536]{1,0:T(8,128)(2,1)S(1)}, bf16[32,1536]{1,0:T(8,128)(2,1)S(1)}, u32[]{:S(2)}, u32[]{:S(2)}) collective-permute-start(bf16[32,1536]{1,0:T(8,128)(2,1)S(1)} %get-tuple-element.18), channel_id=1, source_target_pairs={{0,1},{1,0},{2,3},{3,2},{4,5},{5,4},{6,7},{7,6},{8,9},{9,8},{10,11... | collective-permute-start | bytes 294920 | tf_op jit(solution)/shard_map/ppermute | solution.py:416
  7.8 2.6 %collective-permute-start.3 = (bf16[32,1536]{1,0:T(8,128)(2,1)S(1)}, bf16[32,1536]{1,0:T(8,128)(2,1)S(1)}, u32[]{:S(2)}, u32[]{:S(2)}) collective-permute-start(bf16[32,1536]{1,0:T(8,128)(2,1)S(1)} %get-tuple-element.19), channel_id=1, source_target_pairs={{0,2},{1,3},{2,0},{3,1},{4,6},{5,7},{6,4},{7,5},{8,10},{9,11},{10,... | collective-permute-start | bytes 294920 | tf_op jit(solution)/shard_map/ppermute | solution.py:416
  10.4 0.0 collective-permute-start.4
  10.4 1.5 %collective-permute-start = (bf16[96,1536]{1,0:T(8,128)(2,1)S(1)}, bf16[96,1536]{1,0:T(8,128)(2,1)S(1)}, u32[]{:S(2)}, u32[]{:S(2)}) collective-permute-start(bf16[96,1536]{1,0:T(8,128)(2,1)S(1)} %get-tuple-element.15), channel_id=1, source_target_pairs={{0,4},{4,0},{8,12},{12,8},{16,20},{20,16},{24,28},{28,24},{32,36},... | collective-permute-start | bytes 884744 | tf_op jit(solution)/shard_map/ppermute | solution.py:411
  11.8 3.3 %collective-permute-start.1 = (bf16[96,1536]{1,0:T(8,128)(2,1)S(1)}, bf16[96,1536]{1,0:T(8,128)(2,1)S(1)}, u32[]{:S(2)}, u32[]{:S(2)}) collective-permute-start(bf16[96,1536]{1,0:T(8,128)(2,1)S(1)} %get-tuple-element.16), channel_id=1, source_target_pairs={{0,0},{4,8},{8,4},{12,16},{16,12},{20,24},{24,20},{28,32},{32,28},... | collective-permute-start | bytes 884744 | tf_op jit(solution)/shard_map/ppermute | solution.py:411
  15.2 0.0 collective-permute-done.2
  15.2 0.0 collective-permute-done.3
  15.2 1.9 %collective-permute-done.4 = bf16[32,1536]{1,0:T(8,128)(2,1)S(1)} collective-permute-done((bf16[32,1536]{1,0:T(8,128)(2,1)S(1)}, bf16[32,1536]{1,0:T(8,128)(2,1)S(1)}, u32[]{:S(2)}, u32[]{:S(2)}) %collective-permute-start.4) | collective-permute-done | bytes 98336 | tf_op jit(solution)/shard_map/ppermute | solution.py:416
  17.2 4.3 %collective-permute-start.6 = (bf16[16,1536]{1,0:T(8,128)(2,1)S(1)}, bf16[16,1536]{1,0:T(8,128)(2,1)S(1)}, u32[]{:S(2)}, u32[]{:S(2)}) collective-permute-start(bf16[16,1536]{1,0:T(8,128)(2,1)S(1)} %get-tuple-element.28), channel_id=1, source_target_pairs={{0,0},{4,8},{8,4},{12,16},{16,12},{20,24},{24,20},{28,32},{32,28},... | collective-permute-start | bytes 147464 | tf_op jit(solution)/shard_map/ppermute | solution.py:411
  21.4 0.1 collective-permute-start.5
  21.5 0.7 reshape.13.norm_gain
  22.2 0.7 reshape.14.conv_gain
  22.9 0.7 reshape.15.latent_gain
  23.6 1.1 %collective-permute-done.6.edge_b = bf16[16,1536]{1,0:T(8,128)(2,1)S(1)} collective-permute-done((bf16[16,1536]{1,0:T(8,128)(2,1)S(1)}, bf16[16,1536]{1,0:T(8,128)(2,1)S(1)}, u32[]{:S(2)}, u32[]{:S(2)}) %collective-permute-start.6) | collective-permute-done | bytes 49184 | tf_op jit(solution)/shard_map/ppermute | solution.py:411
  24.7 0.0 collective-permute-done.5.edge_a
  24.7 0.0 collective-permute-done.recv_a
  24.7 0.0 collective-permute-done.1.recv_b
  24.7 0.0 copy-start.1
  24.7 1.0 %copy-done.1 = bf16[1,128,1536]{2,1,0:T(8,128)(2,1)S(1)} copy-done((bf16[1,128,1536]{2,1,0:T(8,128)(2,1)S(1)}, bf16[1,128,1536]{2,1,0:T(8,128)(2,1)}, u32[]{:S(2)}) %copy-start.1) | copy-done | bytes 393240
  25.7 0.0 copy-start.4
  25.7 0.7 copy-done.4
  26.4 0.0 copy-start.5
  26.4 0.9 %copy-done.5 = f32[32,1536]{1,0:T(8,128)S(1)} copy-done((f32[32,1536]{1,0:T(8,128)S(1)}, f32[32,1536]{1,0:T(8,128)}, u32[]{:S(2)}) %copy-start.5) | copy-done | bytes 196632
  27.3 38.8 %main.1 = (bf16[32,1536]{1,0:T(8,128)(2,1)S(1)}, bf16[128,1536]{1,0:T(8,128)(2,1)S(1)}, f32[128,1536]{1,0:T(8,128)S(1)}, bf16[64,1536]{1,0:T(8,128)(2,1)S(1)}, bf16[64,1536]{1,0:T(8,128)(2,1)S(1)}) custom-call(s32[4]{0:T(128)S(1)} %copy-done.4, bf16[128,1536]{1,0:T(8,128)(2,1)S(1)} %bitcast.5, bf16[96,1536]{1,0:T(8,128)(2,1)S(1)} %collective-permute-done.recv_a, ...), custom_call_target="tpu_custom_call" | custom-call | flops 10000000000 | bytes 4000000 | tf_op jit(solution)/shard_map/main/pallas_call | solution.py:468
  66.1 0.1 collective-permute-start.7
  66.2 4.3 %collective-permute-start.8 = (bf16[64,1536]{1,0:T(8,128)(2,1)S(1)}, bf16[64,1536]{1,0:T(8,128)(2,1)S(1)}, u32[]{:S(2)}, u32[]{:S(2)}) collective-permute-start(bf16[64,1536]{1,0:T(8,128)(2,1)S(1)} %get-tuple-element.24), channel_id=1, source_target_pairs={{0,0},{4,8},{8,4},{12,16},{16,12},{20,24},{24,20},{28,32},{32,28},... | collective-permute-start | bytes 589832 | tf_op jit(solution)/shard_map/ppermute | solution.py:411
  70.4 1.0 %collective-permute-start.11 = (bf16[32,1536]{1,0:T(8,128)(2,1)S(1)}, bf16[32,1536]{1,0:T(8,128)(2,1)S(1)}, u32[]{:S(2)}, u32[]{:S(2)}) collective-permute-start(bf16[32,1536]{1,0:T(8,128)(2,1)S(1)} %get-tuple-element.25.l0), channel_id=1, source_target_pairs={{0,3},{1,2},{2,1},{3,0},{4,7},{5,6},{6,5},{7,4},{8,11},{9,10},{10,... | collective-permute-start | bytes 294920 | tf_op jit(solution)/shard_map/ppermute | solution.py:416
  71.4 0.1 collective-permute-start.10
  71.6 2.2 %collective-permute-start.9 = (bf16[32,1536]{1,0:T(8,128)(2,1)S(1)}, bf16[32,1536]{1,0:T(8,128)(2,1)S(1)}, u32[]{:S(2)}, u32[]{:S(2)}) collective-permute-start(bf16[32,1536]{1,0:T(8,128)(2,1)S(1)} %get-tuple-element.25.l0), channel_id=1, source_target_pairs={{0,1},{1,0},{2,3},{3,2},{4,5},{5,4},{6,7},{7,6},{8,9},{9,8},{10,11... | collective-permute-start | bytes 294920 | tf_op jit(solution)/shard_map/ppermute | solution.py:416
  73.8 3.4 %collective-permute-done.11.l3 = bf16[32,1536]{1,0:T(8,128)(2,1)S(1)} collective-permute-done((bf16[32,1536]{1,0:T(8,128)(2,1)S(1)}, bf16[32,1536]{1,0:T(8,128)(2,1)S(1)}, u32[]{:S(2)}, u32[]{:S(2)}) %collective-permute-start.11) | collective-permute-done | bytes 98336 | tf_op jit(solution)/shard_map/ppermute | solution.py:416
  77.1 0.2 collective-permute-done.10.l2
  77.4 0.5 collective-permute-done.9.l1
  77.8 0.0 collective-permute-done.7.recv_a
  77.9 0.0 collective-permute-done.8.recv_b
  77.9 3.7 %finish.1 = (bf16[64,1536]{1,0:T(8,128)(2,1)}, bf16[128,1536]{1,0:T(8,128)(2,1)}) custom-call(s32[4]{0:T(128)S(1)} %copy-done.4, s32[32,4]{1,0:T(8,128)S(1)} %copy.15.tl, bf16[128,1536]{1,0:T(8,128)(2,1)S(1)} %bitcast.6, bf16[128,1536]{1,0:T(8,128)(2,1)S(1)} %get-tuple-element.21.dhid, f32[128,1536]{1,0:T(8,128)S(1)} %get-tuple-element.22.dn, ...), custom_call_target="tpu_custom_call" | custom-call | flops 10000000 | bytes 4000000 | tf_op jit(solution)/shard_map/finish/pallas_call | solution.py:490
  (2 shorter events, 0.0 us)
Async XLA Ops:
  1.4 1.0 %copy-start = (bf16[1,128,1536]{2,1,0:T(8,128)(2,1)S(1)}, bf16[1,128,1536]{2,1,0:T(8,128)(2,1)}, u32[]{:S(2)}) copy-start(bf16[1,128,1536]{2,1,0:T(8,128)(2,1)} %param.12) | copy-start | bytes 1179652
  2.4 0.9 %copy-start.2 = (bf16[1,64,1536]{2,1,0:T(8,128)(2,1)S(1)}, bf16[1,64,1536]{2,1,0:T(8,128)(2,1)}, u32[]{:S(2)}) copy-start(bf16[1,64,1536]{2,1,0:T(8,128)(2,1)} %param.23) | copy-start | bytes 589828
  3.3 0.7 copy-start.3
  6.4 8.8 %collective-permute-start.2 = (bf16[32,1536]{1,0:T(8,128)(2,1)S(1)}, bf16[32,1536]{1,0:T(8,128)(2,1)S(1)}, u32[]{:S(2)}, u32[]{:S(2)}) collective-permute-start(bf16[32,1536]{1,0:T(8,128)(2,1)S(1)} %get-tuple-element.18), channel_id=1, source_target_pairs={{0,1},{1,0},{2,3},{3,2},{4,5},{5,4},{6,7},{7,6},{8,9},{9,8},{10,11... | collective-permute-start | bytes 294920 | tf_op jit(solution)/shard_map/ppermute | solution.py:416
  7.8 7.4 %collective-permute-start.3 = (bf16[32,1536]{1,0:T(8,128)(2,1)S(1)}, bf16[32,1536]{1,0:T(8,128)(2,1)S(1)}, u32[]{:S(2)}, u32[]{:S(2)}) collective-permute-start(bf16[32,1536]{1,0:T(8,128)(2,1)S(1)} %get-tuple-element.19), channel_id=1, source_target_pairs={{0,2},{1,3},{2,0},{3,1},{4,6},{5,7},{6,4},{7,5},{8,10},{9,11},{10,... | collective-permute-start | bytes 294920 | tf_op jit(solution)/shard_map/ppermute | solution.py:416
  10.4 6.8 %collective-permute-start.4 = (bf16[32,1536]{1,0:T(8,128)(2,1)S(1)}, bf16[32,1536]{1,0:T(8,128)(2,1)S(1)}, u32[]{:S(2)}, u32[]{:S(2)}) collective-permute-start(bf16[32,1536]{1,0:T(8,128)(2,1)S(1)} %get-tuple-element.20), channel_id=1, source_target_pairs={{0,3},{1,2},{2,1},{3,0},{4,7},{5,6},{6,5},{7,4},{8,11},{9,10},{10,... | collective-permute-start | bytes 294920 | tf_op jit(solution)/shard_map/ppermute | solution.py:416
  10.4 14.3 %collective-permute-start = (bf16[96,1536]{1,0:T(8,128)(2,1)S(1)}, bf16[96,1536]{1,0:T(8,128)(2,1)S(1)}, u32[]{:S(2)}, u32[]{:S(2)}) collective-permute-start(bf16[96,1536]{1,0:T(8,128)(2,1)S(1)} %get-tuple-element.15), channel_id=1, source_target_pairs={{0,4},{4,0},{8,12},{12,8},{16,20},{20,16},{24,28},{28,24},{32,36},... | collective-permute-start | bytes 884744 | tf_op jit(solution)/shard_map/ppermute | solution.py:411
  11.8 12.9 %collective-permute-start.1 = (bf16[96,1536]{1,0:T(8,128)(2,1)S(1)}, bf16[96,1536]{1,0:T(8,128)(2,1)S(1)}, u32[]{:S(2)}, u32[]{:S(2)}) collective-permute-start(bf16[96,1536]{1,0:T(8,128)(2,1)S(1)} %get-tuple-element.16), channel_id=1, source_target_pairs={{0,0},{4,8},{8,4},{12,16},{16,12},{20,24},{24,20},{28,32},{32,28},... | collective-permute-start | bytes 884744 | tf_op jit(solution)/shard_map/ppermute | solution.py:411
  17.2 7.5 %collective-permute-start.6 = (bf16[16,1536]{1,0:T(8,128)(2,1)S(1)}, bf16[16,1536]{1,0:T(8,128)(2,1)S(1)}, u32[]{:S(2)}, u32[]{:S(2)}) collective-permute-start(bf16[16,1536]{1,0:T(8,128)(2,1)S(1)} %get-tuple-element.28), channel_id=1, source_target_pairs={{0,0},{4,8},{8,4},{12,16},{16,12},{20,24},{24,20},{28,32},{32,28},... | collective-permute-start | bytes 147464 | tf_op jit(solution)/shard_map/ppermute | solution.py:411
  21.4 3.3 %collective-permute-start.5 = (bf16[16,1536]{1,0:T(8,128)(2,1)S(1)}, bf16[16,1536]{1,0:T(8,128)(2,1)S(1)}, u32[]{:S(2)}, u32[]{:S(2)}) collective-permute-start(bf16[16,1536]{1,0:T(8,128)(2,1)S(1)} %get-tuple-element.29), channel_id=1, source_target_pairs={{0,4},{4,0},{8,12},{12,8},{16,20},{20,16},{24,28},{28,24},{32,36},... | collective-permute-start | bytes 147464 | tf_op jit(solution)/shard_map/ppermute | solution.py:411
  24.7 1.0 %copy-start.1 = (bf16[1,128,1536]{2,1,0:T(8,128)(2,1)S(1)}, bf16[1,128,1536]{2,1,0:T(8,128)(2,1)}, u32[]{:S(2)}) copy-start(bf16[1,128,1536]{2,1,0:T(8,128)(2,1)} %param.12) | copy-start | bytes 1179652
  25.7 0.7 copy-start.4
  26.4 0.9 %copy-start.5 = (f32[32,1536]{1,0:T(8,128)S(1)}, f32[32,1536]{1,0:T(8,128)}, u32[]{:S(2)}) copy-start(f32[32,1536]{1,0:T(8,128)} %taps.1) | copy-start | bytes 589828
  66.1 11.8 %collective-permute-start.7 = (bf16[64,1536]{1,0:T(8,128)(2,1)S(1)}, bf16[64,1536]{1,0:T(8,128)(2,1)S(1)}, u32[]{:S(2)}, u32[]{:S(2)}) collective-permute-start(bf16[64,1536]{1,0:T(8,128)(2,1)S(1)} %get-tuple-element.23), channel_id=1, source_target_pairs={{0,4},{4,0},{8,12},{12,8},{16,20},{20,16},{24,28},{28,24},{32,36},... | collective-permute-start | bytes 589832 | tf_op jit(solution)/shard_map/ppermute | solution.py:411
  66.2 11.7 %collective-permute-start.8 = (bf16[64,1536]{1,0:T(8,128)(2,1)S(1)}, bf16[64,1536]{1,0:T(8,128)(2,1)S(1)}, u32[]{:S(2)}, u32[]{:S(2)}) collective-permute-start(bf16[64,1536]{1,0:T(8,128)(2,1)S(1)} %get-tuple-element.24), channel_id=1, source_target_pairs={{0,0},{4,8},{8,4},{12,16},{16,12},{20,24},{24,20},{28,32},{32,28},... | collective-permute-start | bytes 589832 | tf_op jit(solution)/shard_map/ppermute | solution.py:411
  70.4 6.7 %collective-permute-start.11 = (bf16[32,1536]{1,0:T(8,128)(2,1)S(1)}, bf16[32,1536]{1,0:T(8,128)(2,1)S(1)}, u32[]{:S(2)}, u32[]{:S(2)}) collective-permute-start(bf16[32,1536]{1,0:T(8,128)(2,1)S(1)} %get-tuple-element.25.l0), channel_id=1, source_target_pairs={{0,3},{1,2},{2,1},{3,0},{4,7},{5,6},{6,5},{7,4},{8,11},{9,10},{10,... | collective-permute-start | bytes 294920 | tf_op jit(solution)/shard_map/ppermute | solution.py:416
  71.4 6.0 %collective-permute-start.10 = (bf16[32,1536]{1,0:T(8,128)(2,1)S(1)}, bf16[32,1536]{1,0:T(8,128)(2,1)S(1)}, u32[]{:S(2)}, u32[]{:S(2)}) collective-permute-start(bf16[32,1536]{1,0:T(8,128)(2,1)S(1)} %get-tuple-element.25.l0), channel_id=1, source_target_pairs={{0,2},{1,3},{2,0},{3,1},{4,6},{5,7},{6,4},{7,5},{8,10},{9,11},{10,... | collective-permute-start | bytes 294920 | tf_op jit(solution)/shard_map/ppermute | solution.py:416
  71.6 6.3 %collective-permute-start.9 = (bf16[32,1536]{1,0:T(8,128)(2,1)S(1)}, bf16[32,1536]{1,0:T(8,128)(2,1)S(1)}, u32[]{:S(2)}, u32[]{:S(2)}) collective-permute-start(bf16[32,1536]{1,0:T(8,128)(2,1)S(1)} %get-tuple-element.25.l0), channel_id=1, source_target_pairs={{0,1},{1,0},{2,3},{3,2},{4,5},{5,4},{6,7},{7,6},{8,9},{9,8},{10,11... | collective-permute-start | bytes 294920 | tf_op jit(solution)/shard_map/ppermute | solution.py:416

commit v2 on v1

--- a/solution.py
+++ b/solution.py
@@ -22,7 +22,7 @@
 HEAD = 96
 LANE = 128
 NB = D // LANE
-COL = 256
+COL = 768
 NC = D // COL
 GROUP = 4 * HEAD
 EPSILON = 1e-06
@@ -32,7 +32,6 @@
 WINDOWS = ((0, 1), (0, 2), (1, 3), (2, 3))
 
 ANY = pl.BlockSpec(memory_space=pl.ANY)
-SMEM = pl.BlockSpec(memory_space=pltpu.SMEM)
 
 
 def dot(a, b):
@@ -56,7 +55,7 @@
     total = 0
     for b in range(NREC):
         live = jnp.clip(fc[b] // 4 - slice_index * LR, 0, LR)
-        total = total + tl[slice_index, b]
+        total = total + tl[b, slice_index]
         starts.append(total)
         lives.append(live)
         total = total + live
@@ -70,7 +69,11 @@
     return out
 
 
-def prepare(fc, tl, audio, grads, send_a, send_b, o0, o1, o2, o3, g_buf, o_buf, sems):
+def prepare(fc_in, tl_in, audio, grads, send_a, send_b, o0, o1, o2, o3, fc, tl, g_buf, o_buf, sems):
+    cf = pltpu.make_async_copy(fc_in, fc, sems.at[7])
+    ct = pltpu.make_async_copy(tl_in, tl, sems.at[8])
+    cf.start()
+    ct.start()
     tm = lax.axis_index("tm")
     llm = lax.axis_index("llm")
     off_a = (1 - tm % 2) * (FR - HALO)
@@ -81,6 +84,8 @@
     cg.start()
     ca.start()
     cb.start()
+    cf.wait()
+    ct.wait()
     starts, lives = routes(fc, tl, tm)
     row = lax.broadcasted_iota(jnp.int32, (LR, SLOTS), 0)
     slot = lax.broadcasted_iota(jnp.int32, (LR, SLOTS), 1) + llm * SLOTS
@@ -98,11 +103,11 @@
 
 
 def main_kernel(
-    fc, audio, recv_a, recv_b, lat_grad, edge_a, edge_b, w_query, w_key, w_value, w_out,
+    fc_in, audio, recv_a, recv_b, lat_grad, edge_a, edge_b, w_query, w_key, w_value, w_out,
     norm_gain, conv_gain, latent_gain, taps,
     latent_out, dhid_out, dn_out, send_a, send_b,
-    x_s, n_s, q_s, k_s, v_s, wq_s, wk_s, wv_s, wo_s, ng_s, cg_s, lg_s, tap_s,
-    att_s, p_s, bias_s, biasl_s, biasr_s, h_s, ci_s, dsilu_s, up_s, pool_s, g_s, gst_s, norm_t, lat_s,
+    fc, x_s, n_s, q_s, k_s, v_s, wq_s, wk_s, wv_s, wo_s, ng_s, cg_s, lg_s, tap_s,
+    att_s, p_s, bias_s, h_s, ci_s, dsilu_s, up_s, pool_s, g_s, gst_s, norm_t, lat_s,
     ds_s, us_s, dnc_s, dhid_s, datt_s, dq_s, dk_s, dv_s, dn_s, edge_s, w_sems, sems,
 ):
     tm = lax.axis_index("tm")
@@ -112,7 +117,8 @@
     parity = tm % 2
     first = tm * FR
     total = n_tm * FR
-    limit = fc[llm]
+    fc_copy = pltpu.make_async_copy(fc_in, fc, sems.at[15])
+    fc_copy.start()
 
     left_row = pl.multiple_of((1 - parity) * (HALO + FR), 32)
     right_row = pl.multiple_of(parity * (HALO + FR), 32)
@@ -144,6 +150,9 @@
     for copy in late:
         copy.start()
 
+    fc_copy.wait()
+    limit = fc[llm]
+
     def bias_of(rows, cols, q_first, k_first):
         qe = lax.broadcasted_iota(jnp.int32, (rows, cols), 0) + q_first
         ke = lax.broadcasted_iota(jnp.int32, (rows, cols), 1) + k_first
@@ -151,9 +160,9 @@
         ok = (ke >= qe - REACH) & (ke < qe + REACH) & (kt >= 0) & (kt < total) & ((kt < limit) | (ke == qe))
         return jnp.where(ok, 0.0, -1e30)
 
-    bias_s[...] = bias_of(FR, 256, HALO, 32)
-    biasl_s[...] = bias_of(32, 160, 64, 0)
-    biasr_s[...] = bias_of(32, 160, 224, 160)
+    bias_s[0:32, :] = bias_of(32, 256, 64, 0)
+    bias_s[32:160, :] = bias_of(FR, 256, HALO, 32)
+    bias_s[160:192, :] = bias_of(32, 256, 224, 64)
 
     for copy in small:
         copy.wait()
@@ -163,7 +172,9 @@
         rows = pl.ds(pl.multiple_of(r * 64, 64), 64)
         x = x_s[rows, :].astype(F32)
         inv = lax.rsqrt(jnp.mean(x * x, axis=-1, keepdims=True) + EPSILON)
-        n_s[rows, :] = (x * inv * ng_s[...]).astype(BF)
+        for c in range(NB):
+            cols = slice(c * LANE, (c + 1) * LANE)
+            n_s[rows, cols] = (x[:, cols] * inv * ng_s[c : c + 1, :]).astype(BF)
 
     for n, (w_s, out_s, lo, hi) in enumerate(
         ((wk_s, k_s, 0, EXT), (wv_s, v_s, 0, EXT), (wq_s, q_s, 64, 64 + QR))
@@ -179,10 +190,6 @@
         lane = lane_of[:, : (hi - lo) * LANE] + lo * LANE
         return jnp.where((lane >= j * HEAD) & (lane < (j + 1) * HEAD), 1.0, 0.0).astype(BF)
 
-    def softmax(scores):
-        powers = jnp.exp(scores - jnp.max(scores, axis=-1, keepdims=True))
-        return powers * (1.0 / jnp.sum(powers, axis=-1, keepdims=True))
-
     def window(g, lo, hi):
         return pl.ds(pl.multiple_of(g * GROUP + lo * LANE, LANE), (hi - lo) * LANE)
 
@@ -193,34 +200,45 @@
 
     @pl.loop(0, 4)
     def _(g):
-        own, left, right = [None] * 3, [None] * 3, [None] * 3
+        heads = []
         for j, (lo, hi) in enumerate(WINDOWS):
             win = window(g, lo, hi)
-            mask = head_mask(j, lo, hi)
-            q = q_s[:, win] * mask
+            q = q_s[:, win] * head_mask(j, lo, hi)
             k = k_s[:, win]
-            v = v_s[:, win] * mask
-            p = softmax(dot_t(q[32:160], k[32:288]) * SCALE + bias_s[...]).astype(BF)
-            p_s[g * 4 + j] = p
-            add_tiles(own, lo, dot(p, v[32:288]))
-            p = softmax(dot_t(q[0:32], k[0:160]) * SCALE + biasl_s[...]).astype(BF)
-            add_tiles(left, lo, dot(p, v[0:160]))
-            p = softmax(dot_t(q[160:192], k[160:320]) * SCALE + biasr_s[...]).astype(BF)
-            add_tiles(right, lo, dot(p, v[160:320]))
+            heads.append(
+                jnp.concatenate(
+                    [dot_t(q[0:32], k[0:256]), dot_t(q[32:160], k[32:288]), dot_t(q[160:192], k[64:320])], axis=0
+                )
+            )
+        heads = [scores * SCALE + bias_s[...] for scores in heads]
+        highest = [jnp.max(scores, axis=-1, keepdims=True) for scores in heads]
+        heads = [jnp.exp(scores - top) for scores, top in zip(heads, highest)]
+        inverse = [1.0 / jnp.sum(powers, axis=-1, keepdims=True) for powers in heads]
+        heads = [(powers * inv).astype(BF) for powers, inv in zip(heads, inverse)]
+        parts = [[None] * 3 for _ in range(3)]
+        for j, (lo, hi) in enumerate(WINDOWS):
+            v = v_s[:, window(g, lo, hi)] * head_mask(j, lo, hi)
+            p = heads[j]
+            p_s[g * 4 + j] = p[32:160]
+            add_tiles(parts[0], lo, dot(p[0:32], v[0:256]))
+            add_tiles(parts[1], lo, dot(p[32:160], v[32:288]))
+            add_tiles(parts[2], lo, dot(p[160:192], v[64:320]))
         for t in range(3):
             at = window(g, t, t + 1)
-            att_s[0:32, at] = left[t].astype(BF)
-            att_s[32:160, at] = own[t].astype(BF)
-            att_s[160:192, at] = right[t].astype(BF)
+            att_s[0:32, at] = parts[0][t].astype(BF)
+            att_s[32:160, at] = parts[1][t].astype(BF)
+            att_s[160:192, at] = parts[2][t].astype(BF)
 
     def hidden_step(j, squares):
         w_copy(3, j).wait()
         cols = lanes(j, COL)
         h = dot(att_s[...], wo_s[:, cols]) + x_s[64 : 64 + QR, cols].astype(F32)
         h = h.astype(BF).astype(F32)
-        h_s[2 * j] = h[:, :LANE]
-        h_s[2 * j + 1] = h[:, LANE:]
-        return squares + h[:, :LANE] * h[:, :LANE] + h[:, LANE:] * h[:, LANE:]
+        for t in range(COL // LANE):
+            part = h[:, t * LANE : (t + 1) * LANE]
+            h_s[j * (COL // LANE) + t] = part
+            squares = squares + part * part
+        return squares
 
     squares = lax.fori_loop(0, NC, hidden_step, jnp.zeros((QR, LANE), F32))
     inv_h = lax.rsqrt(jnp.sum(squares, axis=-1, keepdims=True) * (1.0 / D) + EPSILON)
@@ -240,7 +258,7 @@
     def conv_step(c, carry):
         squares, along = carry
         cols = lanes(c)
-        ci_s[...] = (h_s[c] * inv_spoken * cg_s[:, cols]).astype(BF).astype(F32)
+        ci_s[...] = (h_s[c] * inv_spoken * cg_s[pl.ds(c, 1), :]).astype(BF).astype(F32)
         kern = tap_s[:, cols]
         acc = jnp.zeros((SR, LANE), F32)
         for s in range(8):
@@ -257,7 +275,7 @@
             pooled = pooled + up_s[pl.ds(u, PR, 4), :]
         pooled = pooled * 0.25
         pool_s[c] = pooled
-        return squares + pooled * pooled, along + g_s[:, cols] * lg_s[:, cols] * pooled
+        return squares + pooled * pooled, along + g_s[:, cols] * lg_s[pl.ds(c, 1), :] * pooled
 
     zero = jnp.zeros((PR, LANE), F32)
     squares, along = lax.fori_loop(0, NB, conv_step, (zero, zero))
@@ -270,7 +288,7 @@
     def conv_back(c, along):
         cols = lanes(c)
         pooled = pool_s[c]
-        gain = lg_s[:, cols]
+        gain = lg_s[pl.ds(c, 1), :]
         norm_t[...] = pooled * inv_p * gain
         lat_s[:, cols] = norm_t[4:36, :].astype(BF)
         dpool = (g_s[:, cols] * gain * inv_p - pooled * back_p) * 0.25
@@ -286,7 +304,7 @@
             for u in range(4):
                 m = 32 - base - 8 * u
                 acc = acc + kern[m : m + 1, :] * xs[8 * u : 8 * u + FR]
-        dn = acc.astype(BF).astype(F32) * spoken_own * cg_s[:, cols]
+        dn = acc.astype(BF).astype(F32) * spoken_own * cg_s[pl.ds(c, 1), :]
         dnc_s[c] = dn
         return along + dn * h_s[c, 32:160, :]
 
@@ -308,22 +326,21 @@
 
     @pl.loop(0, 4)
     def _(g):
+        heads = []
+        for j, (lo, hi) in enumerate(WINDOWS):
+            win = window(g, lo, hi)
+            heads.append(dot_t(datt_s[:, win] * head_mask(j, lo, hi), v_s[32:288, win]))
+        weights = [p_s[g * 4 + j].astype(F32) for j in range(4)]
+        heads = [w * dp for w, dp in zip(weights, heads)]
+        sums = [jnp.sum(pd, axis=-1, keepdims=True) for pd in heads]
+        heads = [((pd - w * total) * SCALE).astype(BF) for pd, w, total in zip(heads, weights, sums)]
         dq, dk, dv = [None] * 3, [None] * 3, [None] * 3
         for j, (lo, hi) in enumerate(WINDOWS):
             win = window(g, lo, hi)
             mask = head_mask(j, lo, hi)
-            q = q_s[32:160, win] * mask
-            k = k_s[32:288, win] * mask
-            v = v_s[32:288, win]
-            do = datt_s[:, win] * mask
-            p = p_s[g * 4 + j]
-            dp = dot_t(do, v)
-            pf = p.astype(F32)
-            pd = pf * dp
-            ds = ((pd - pf * jnp.sum(pd, axis=-1, keepdims=True)) * SCALE).astype(BF)
-            add_tiles(dq, lo, dot(ds, k))
-            add_tiles(dk, lo, t_dot(ds, q))
-            add_tiles(dv, lo, t_dot(p, do))
+            add_tiles(dq, lo, dot(heads[j], k_s[32:288, win] * mask))
+            add_tiles(dk, lo, t_dot(heads[j], q_s[32:160, win] * mask))
+            add_tiles(dv, lo, t_dot(p_s[g * 4 + j], datt_s[:, win] * mask))
         for t in range(3):
             at = window(g, t, t + 1)
             dq_s[:, at] = dq[t].astype(BF)
@@ -352,10 +369,14 @@
 
 
 def finish(
-    fc, tl, audio, dhid, dn, recv_a, recv_b, l0, l1, l2, l3, norm_gain,
+    fc_in, tl_in, audio, dhid, dn, recv_a, recv_b, l0, l1, l2, l3, norm_gain,
     rows_out, grad_out,
-    x_s, dh_s, dn_s, r_s, lat_s, ng_s, out_s, rows_s, sems,
+    fc, tl, x_s, dh_s, dn_s, r_s, lat_s, ng_s, out_s, rows_s, sems,
 ):
+    cf = pltpu.make_async_copy(fc_in, fc, sems.at[12])
+    ct = pltpu.make_async_copy(tl_in, tl, sems.at[13])
+    cf.start()
+    ct.start()
     tm = lax.axis_index("tm")
     llm = lax.axis_index("llm")
     parity = tm % 2
@@ -373,6 +394,8 @@
     ]
     for copy in copies + lat_copies:
         copy.start()
+    cf.wait()
+    ct.wait()
     starts, lives = routes(fc, tl, tm)
     slot = lax.broadcasted_iota(jnp.int32, (SLOTS, NREC * LR), 0) + llm * SLOTS
     col = lax.broadcasted_iota(jnp.int32, (SLOTS, NREC * LR), 1)
@@ -391,9 +414,14 @@
         keep = keep_left if half == 0 else keep_right
         x = x_s[rows, :].astype(F32)
         inv = lax.rsqrt(jnp.mean(x * x, axis=-1, keepdims=True) + EPSILON)
-        g = (dn_s[rows, :] + r_s[rows, :].astype(F32) * keep).astype(BF).astype(F32) * ng_s[...]
-        back = inv * inv * inv * jnp.mean(g * x, axis=-1, keepdims=True)
-        out_s[rows, :] = (dh_s[rows, :].astype(F32) + g * inv - x * back).astype(BF)
+        along = jnp.zeros((64, LANE), F32)
+        for c in range(NB):
+            cols = slice(c * LANE, (c + 1) * LANE)
+            g = (dn_s[rows, cols] + r_s[rows, cols].astype(F32) * keep).astype(BF).astype(F32) * ng_s[c : c + 1, :]
+            dn_s[rows, cols] = g
+            along = along + g * x[:, cols]
+        back = inv * inv * inv * (jnp.sum(along, axis=-1, keepdims=True) * (1.0 / D))
+        out_s[rows, :] = (dh_s[rows, :].astype(F32) + dn_s[rows, :] * inv - x * back).astype(BF)
     grad_copy = pltpu.make_async_copy(out_s, grad_out, sems.at[10])
     grad_copy.start()
     for copy in lat_copies:
@@ -407,8 +435,13 @@
 
 def swap(count, cells_a, cells_b):
     pairs_a = [(i, i ^ 1) for i in range(count)]
-    pairs_b = [(i, min(max(((i + 1) ^ 1) - 1, 0), count - 1)) for i in range(count)]
-    return lax.ppermute(cells_a, "tm", pairs_a), lax.ppermute(cells_b, "tm", pairs_b)
+    n = lax.axis_size("llm")
+    full_b = []
+    for i in range(count):
+        partner = ((i + 1) ^ 1) - 1
+        end = partner < 0 or partner >= count
+        full_b += [(i * n + y, i * n + (y ^ 1) if end else partner * n + y) for y in range(n)]
+    return lax.ppermute(cells_a, "tm", pairs_a), lax.ppermute(cells_b, ("tm", "llm"), full_b)
 
 
 def exchange(count, cells):
@@ -437,24 +470,55 @@
 MIB = 1024 * 1024
 
 
+def hbm(array):
+    return pltpu.with_memory_space_constraint(array, pltpu.HBM)
+
+
+def run_main(*operands):
+    V = pltpu.VMEM
+    S = pltpu.SMEM
+    dma = pltpu.SemaphoreType.DMA
+    return call(
+        main_kernel,
+        [shape(LR), shape(FR), shape(FR, F32), shape(64), shape(64)],
+        [
+            S((NREC,), jnp.int32),
+            V((EXT, D), BF), V((EXT, D), BF), V((QR, D), BF), V((EXT, D), BF), V((EXT, D), BF),
+            V((D, D), BF), V((D, D), BF), V((D, D), BF), V((D, D), BF),
+            V((NB, LANE), F32), V((NB, LANE), F32), V((NB, LANE), F32), V((KERN, D), F32),
+            V((QR, D), BF), V((16, FR, 256), BF), V((QR, 256), F32),
+            V((NB, QR, LANE), F32), V((QR, LANE), F32), V((NB, SR, LANE), F32), V((SR, LANE), F32),
+            V((NB, PR, LANE), F32), V((PR, D), F32), V((64, D), BF), V((PR, LANE), F32), V((LR, D), BF),
+            V((SR, LANE), F32), V((NB, FR, LANE), F32), V((NB, FR, LANE), F32), V((FR, D), BF),
+            V((FR, D), BF), V((FR, D), BF), V((256, D), BF), V((256, D), BF), V((FR, D), F32), V((FR, D), BF),
+            dma((4, NC)), dma((16,)),
+        ],
+        [ANY] * 15,
+        "main", 50 * MIB, 10_000_000_000,
+    )(*operands)
+
+
 def on_device(
     audio, frame_counts, text_lengths, norm_gain, w_query, w_key, w_value, w_out,
     conv_gain, conv_kernel, latent_gain, llm_grads,
 ):
-    signal = audio[0]
+    signal = hbm(audio[0])
     n_tm = lax.axis_size("tm")
     n_llm = lax.axis_size("llm")
-    norm_row, conv_row, latent_row = (g.reshape(1, D) for g in (norm_gain, conv_gain, latent_gain))
+    norm_row, conv_row, latent_row = (hbm(g.reshape(NB, LANE)) for g in (norm_gain, conv_gain, latent_gain))
+    fc, tl, taps = hbm(frame_counts), hbm(text_lengths.T), hbm(conv_kernel)
+    weights = [hbm(w) for w in (w_query, w_key, w_value, w_out)]
     V = pltpu.VMEM
+    S = pltpu.SMEM
     dma = pltpu.SemaphoreType.DMA
 
     send_a, send_b, o0, o1, o2, o3 = call(
         prepare,
         [shape(HALO)] * 2 + [shape(LR)] * 4,
-        [V((SLOTS, D), BF), V((NREC, LR, D), BF), dma((7,))],
-        [SMEM, SMEM, ANY, ANY],
+        [S((NREC,), jnp.int32), S((NREC, n_tm), jnp.int32), V((SLOTS, D), BF), V((NREC, LR, D), BF), dma((9,))],
+        [ANY] * 4,
         "prepare", 8 * MIB, 10_000_000,
-    )(frame_counts, text_lengths, signal, llm_grads[0])
+    )(fc, tl, signal, hbm(llm_grads[0]))
     recv_a, recv_b = swap(n_tm, send_a, send_b)
     came = exchange(n_llm, [o0, o1, o2, o3])
     lat_grad = o0 + came[0] + came[1] + came[2]
@@ -465,25 +529,9 @@
         jnp.where(even, lat_grad[:16], lat_grad[16:]),
     )
 
-    latent, dhid, dn, back_a, back_b = call(
-        main_kernel,
-        [shape(LR), shape(FR), shape(FR, F32), shape(64), shape(64)],
-        [
-            V((EXT, D), BF), V((EXT, D), BF), V((QR, D), BF), V((EXT, D), BF), V((EXT, D), BF),
-            V((D, D), BF), V((D, D), BF), V((D, D), BF), V((D, D), BF),
-            V((1, D), F32), V((1, D), F32), V((1, D), F32), V((KERN, D), F32),
-            V((QR, D), BF), V((16, FR, 256), BF), V((FR, 256), F32), V((32, 160), F32), V((32, 160), F32),
-            V((NB, QR, LANE), F32), V((QR, LANE), F32), V((NB, SR, LANE), F32), V((SR, LANE), F32),
-            V((NB, PR, LANE), F32), V((PR, D), F32), V((64, D), BF), V((PR, LANE), F32), V((LR, D), BF),
-            V((SR, LANE), F32), V((NB, FR, LANE), F32), V((NB, FR, LANE), F32), V((FR, D), BF),
-            V((FR, D), BF), V((FR, D), BF), V((256, D), BF), V((256, D), BF), V((FR, D), F32), V((FR, D), BF),
-            dma((4, NC)), dma((15,)),
-        ],
-        [SMEM] + [ANY] * 14,
-        "main", 50 * MIB, 10_000_000_000,
-    )(
-        frame_counts, signal, recv_a, recv_b, lat_grad, edge_a, edge_b,
-        w_query, w_key, w_value, w_out, norm_row, conv_row, latent_row, conv_kernel,
+    latent, dhid, dn, back_a, back_b = run_main(
+        fc, signal, recv_a, recv_b, lat_grad, edge_a, edge_b,
+        *weights, norm_row, conv_row, latent_row, taps,
     )
     ret_a, ret_b = swap(n_tm, back_a, back_b)
     others = exchange(n_llm, [latent] * n_llm)
@@ -491,12 +539,13 @@
         finish,
         [shape(SLOTS), shape(FR)],
         [
+            S((NREC,), jnp.int32), S((NREC, n_tm), jnp.int32),
             V((FR, D), BF), V((FR, D), BF), V((FR, D), F32), V((FR, D), BF), V((NREC * LR, D), BF),
-            V((1, D), F32), V((FR, D), BF), V((SLOTS, D), BF), dma((12,)),
+            V((NB, LANE), F32), V((FR, D), BF), V((SLOTS, D), BF), dma((14,)),
         ],
-        [SMEM, SMEM] + [ANY] * 10,
+        [ANY] * 12,
         "finish", 8 * MIB, 10_000_000,
-    )(frame_counts, text_lengths, signal, dhid, dn, ret_a, ret_b, latent, *others, norm_row)
+    )(fc, tl, signal, dhid, dn, ret_a, ret_b, latent, *others, norm_row)
     return (rows[None], grad[None])
 
 

time: 82.1 us -> 62.5 us (0.76)
  Pallas kernels: 44.9 us -> 35.2 us
  local copies, waits for them, and re-layouts: 8.02 us -> 0 us
  starting transfers between devices: 20.8 us -> 15.1 us
  waiting for transfers between devices: 7.07 us -> 11.1 us
    pallas_call x3, Pallas kernels: 44.9 us -> 35.2 us  [the longest x1 30.1 us: run_main(): call(main_kernel, [shape(LR), shape(FR), shape(FR, F32), shape(64), shape...]
    unnamed x13 -> x0, local copies, waits for them, and re-layouts: 5.91 us -> none
    ppermute x3, starting transfers between devices: 11.9 us -> 6.3 us  [swap(): lax.ppermute(cells_b, ('tm', 'llm'), full_b)]
    ppermute x3, waiting for transfers between devices: 1.06 us -> 3.27 us  [swap(): lax.ppermute(cells_b, ('tm', 'llm'), full_b)]
    reshape x3 -> x0, local copies, waits for them, and re-layouts: 2.11 us -> none  [on_device(): g.reshape(1, D)]
    ppermute x6, waiting for transfers between devices: 6 us -> 7.83 us  [exchange(): lax.ppermute(cells[j], 'llm', [(i, i ^ j) for i in range(count)])]
  transfers between devices with their start and end apart: 12 -> 12, of which waited for: 5 -> 6; matrix products, arithmetic and copies ran while one was open for 3% -> 0% of each run, Pallas kernels for 0% -> 0%
where the time goes in v2:
time: 62.5 us; the launch traced here: 62.1 us
  Pallas kernels  35.2 us (56%)
  starting transfers between devices  15.1 us (24%)
  waiting for transfers between devices  11.1 us (18%)
  between operations  0.68 us (1%)
    pallas_call x1, Pallas kernels, run_main(): call(main_kernel, [shape(LR), shape(FR), shape(FR, F32), shape(64), shape...  30.1 us
    ppermute x6, waiting for transfers between devices, exchange(): lax.ppermute(cells[j], 'llm', [(i, i ^ j) for i in range(count)])  7.83 us
    ppermute x6, starting transfers between devices, exchange(): lax.ppermute(cells[j], 'llm', [(i, i ^ j) for i in range(count)])  7.25 us
    ppermute x3, starting transfers between devices, swap(): lax.ppermute(cells_b, ('tm', 'llm'), full_b)  6.3 us
    ppermute x3, waiting for transfers between devices, swap(): lax.ppermute(cells_b, ('tm', 'llm'), full_b)  3.27 us
    pallas_call x1, Pallas kernels, on_device(): call(finish, [shape(SLOTS), shape(FR)], [S((NREC,), jnp.int32), S((NREC,...  3.01 us
    pallas_call x1, Pallas kernels, on_device(): call(prepare, [shape(HALO)] * 2 + [shape(LR)] * 4, [S((NREC,), jnp.int32)...  2.13 us
    ppermute x3, starting transfers between devices, swap(): lax.ppermute(cells_a, 'tm', pairs_a)  1.54 us
  transfers between devices with their start and end apart: 12, of which 6 were waited for; matrix products, arithmetic and copies ran while one was open for 0% of the time, Pallas kernels for 0%

profile of v2, /device:TPU:39, one launch (start us, length us, event | category | flops | bytes accessed | tf_op | source)
XLA Modules:
  0.0 62.1 jit_solution(8273414632318938168)
XLA Ops:
  0.6 2.1 %prepare.1 = (bf16[96,1536]{1,0:T(8,128)(2,1)S(1)}, bf16[96,1536]{1,0:T(8,128)(2,1)S(1)}, bf16[32,1536]{1,0:T(8,128)(2,1)S(1)}, bf16[32,1536]{1,0:T(8,128)(2,1)S...) custom-call(s32[4]{0:T(128)} %fc_in.5, s32[4,32]{1,0:T(4,128)} %bitcast.14, bf16[128,1536]{1,0:T(8,128)(2,1)} %bitcast.8, ...), custom_call_target="tpu_custom_call" | custom-call | flops 10000000 | bytes 4000000 | tf_op jit(solution)/shard_map/prepare/pallas_call | solution.py:515
  2.8 1.4 %collective-permute-start.2 = (bf16[32,1536]{1,0:T(8,128)(2,1)S(1)}, bf16[32,1536]{1,0:T(8,128)(2,1)S(1)}, u32[]{:S(2)}, u32[]{:S(2)}) collective-permute-start(bf16[32,1536]{1,0:T(8,128)(2,1)S(1)} %get-tuple-element.18), channel_id=1, source_target_pairs={{0,1},{1,0},{2,3},{3,2},{4,5},{5,4},{6,7},{7,6},{8,9},{9,8},{10,11... | collective-permute-start | bytes 294920 | tf_op jit(solution)/shard_map/ppermute | solution.py:449
  4.1 2.6 %collective-permute-start.3 = (bf16[32,1536]{1,0:T(8,128)(2,1)S(1)}, bf16[32,1536]{1,0:T(8,128)(2,1)S(1)}, u32[]{:S(2)}, u32[]{:S(2)}) collective-permute-start(bf16[32,1536]{1,0:T(8,128)(2,1)S(1)} %get-tuple-element.19), channel_id=1, source_target_pairs={{0,2},{1,3},{2,0},{3,1},{4,6},{5,7},{6,4},{7,5},{8,10},{9,11},{10,... | collective-permute-start | bytes 294920 | tf_op jit(solution)/shard_map/ppermute | solution.py:449
  6.8 0.0 collective-permute-start.4
  6.8 1.5 %collective-permute-start = (bf16[96,1536]{1,0:T(8,128)(2,1)S(1)}, bf16[96,1536]{1,0:T(8,128)(2,1)S(1)}, u32[]{:S(2)}, u32[]{:S(2)}) collective-permute-start(bf16[96,1536]{1,0:T(8,128)(2,1)S(1)} %get-tuple-element.15), channel_id=1, source_target_pairs={{0,4},{4,0},{8,12},{12,8},{16,20},{20,16},{24,28},{28,24},{32,36},... | collective-permute-start | bytes 884744 | tf_op jit(solution)/shard_map/ppermute | solution.py:444
  8.2 1.4 %collective-permute-start.1 = (bf16[96,1536]{1,0:T(8,128)(2,1)S(1)}, bf16[96,1536]{1,0:T(8,128)(2,1)S(1)}, u32[]{:S(2)}, u32[]{:S(2)}) collective-permute-start(bf16[96,1536]{1,0:T(8,128)(2,1)S(1)} %get-tuple-element.16), channel_id=1, source_target_pairs={{0,1},{1,0},{2,3},{3,2},{4,8},{5,9},{6,10},{7,11},{8,4},{9,5},{10,... | collective-permute-start | bytes 884744 | tf_op jit(solution)/shard_map/ppermute | solution.py:444
  9.7 0.0 collective-permute-done.2
  9.7 1.1 %collective-permute-done.3 = bf16[32,1536]{1,0:T(8,128)(2,1)S(1)} collective-permute-done((bf16[32,1536]{1,0:T(8,128)(2,1)S(1)}, bf16[32,1536]{1,0:T(8,128)(2,1)S(1)}, u32[]{:S(2)}, u32[]{:S(2)}) %collective-permute-start.3) | collective-permute-done | bytes 98336 | tf_op jit(solution)/shard_map/ppermute | solution.py:449
  10.8 2.7 %collective-permute-done.4 = bf16[32,1536]{1,0:T(8,128)(2,1)S(1)} collective-permute-done((bf16[32,1536]{1,0:T(8,128)(2,1)S(1)}, bf16[32,1536]{1,0:T(8,128)(2,1)S(1)}, u32[]{:S(2)}, u32[]{:S(2)}) %collective-permute-start.4) | collective-permute-done | bytes 98336 | tf_op jit(solution)/shard_map/ppermute | solution.py:449
  13.6 2.4 %collective-permute-start.6 = (bf16[16,1536]{1,0:T(8,128)(2,1)S(1)}, bf16[16,1536]{1,0:T(8,128)(2,1)S(1)}, u32[]{:S(2)}, u32[]{:S(2)}) collective-permute-start(bf16[16,1536]{1,0:T(8,128)(2,1)S(1)} %get-tuple-element.28), channel_id=1, source_target_pairs={{0,1},{1,0},{2,3},{3,2},{4,8},{5,9},{6,10},{7,11},{8,4},{9,5},{10,... | collective-permute-start | bytes 147464 | tf_op jit(solution)/shard_map/ppermute | solution.py:444
  16.0 0.0 collective-permute-start.5
  16.0 3.3 %collective-permute-done.6.edge_b = bf16[16,1536]{1,0:T(8,128)(2,1)S(1)} collective-permute-done((bf16[16,1536]{1,0:T(8,128)(2,1)S(1)}, bf16[16,1536]{1,0:T(8,128)(2,1)S(1)}, u32[]{:S(2)}, u32[]{:S(2)}) %collective-permute-start.6) | collective-permute-done | bytes 49184 | tf_op jit(solution)/shard_map/ppermute | solution.py:444
  19.3 0.0 collective-permute-done.5.edge_a
  19.3 0.0 collective-permute-done.recv_a
  19.3 0.0 collective-permute-done.1.recv_b
  19.3 30.1 %main.1 = (bf16[32,1536]{1,0:T(8,128)(2,1)S(1)}, bf16[128,1536]{1,0:T(8,128)(2,1)S(1)}, f32[128,1536]{1,0:T(8,128)S(1)}, bf16[64,1536]{1,0:T(8,128)(2,1)S(1)}, bf16[64,1536]{1,0:T(8,128)(2,1)S(1)}) custom-call(s32[4]{0:T(128)} %fc_in.5, bf16[128,1536]{1,0:T(8,128)(2,1)} %bitcast.9, bf16[96,1536]{1,0:T(8,128)(2,1)S(1)} %collective-permute-done.recv_a, ...), custom_call_target="tpu_custom_call" | custom-call | flops 10000000000 | bytes 4000000 | tf_op jit(solution)/shard_map/main/pallas_call | solution.py:481
  49.4 0.1 collective-permute-start.7
  49.5 2.4 %collective-permute-start.8 = (bf16[64,1536]{1,0:T(8,128)(2,1)S(1)}, bf16[64,1536]{1,0:T(8,128)(2,1)S(1)}, u32[]{:S(2)}, u32[]{:S(2)}) collective-permute-start(bf16[64,1536]{1,0:T(8,128)(2,1)S(1)} %get-tuple-element.24), channel_id=1, source_target_pairs={{0,1},{1,0},{2,3},{3,2},{4,8},{5,9},{6,10},{7,11},{8,4},{9,5},{10,... | collective-permute-start | bytes 589832 | tf_op jit(solution)/shard_map/ppermute | solution.py:444
  51.9 0.4 collective-permute-start.11
  52.3 0.6 collective-permute-start.10
  52.9 2.2 %collective-permute-start.9 = (bf16[32,1536]{1,0:T(8,128)(2,1)S(1)}, bf16[32,1536]{1,0:T(8,128)(2,1)S(1)}, u32[]{:S(2)}, u32[]{:S(2)}) collective-permute-start(bf16[32,1536]{1,0:T(8,128)(2,1)S(1)} %get-tuple-element.25.l0), channel_id=1, source_target_pairs={{0,1},{1,0},{2,3},{3,2},{4,5},{5,4},{6,7},{7,6},{8,9},{9,8},{10,11... | collective-permute-start | bytes 294920 | tf_op jit(solution)/shard_map/ppermute | solution.py:449
  55.1 3.1 %collective-permute-done.11.l3 = bf16[32,1536]{1,0:T(8,128)(2,1)S(1)} collective-permute-done((bf16[32,1536]{1,0:T(8,128)(2,1)S(1)}, bf16[32,1536]{1,0:T(8,128)(2,1)S(1)}, u32[]{:S(2)}, u32[]{:S(2)}) %collective-permute-start.11) | collective-permute-done | bytes 98336 | tf_op jit(solution)/shard_map/ppermute | solution.py:449
  58.2 0.1 collective-permute-done.10.l2
  58.3 0.9 %collective-permute-done.9.l1 = bf16[32,1536]{1,0:T(8,128)(2,1)S(1)} collective-permute-done((bf16[32,1536]{1,0:T(8,128)(2,1)S(1)}, bf16[32,1536]{1,0:T(8,128)(2,1)S(1)}, u32[]{:S(2)}, u32[]{:S(2)}) %collective-permute-start.9) | collective-permute-done | bytes 98336 | tf_op jit(solution)/shard_map/ppermute | solution.py:449
  59.1 0.0 collective-permute-done.7.recv_a
  59.1 0.0 collective-permute-done.8.recv_b
  59.1 3.0 %finish.1 = (bf16[64,1536]{1,0:T(8,128)(2,1)}, bf16[128,1536]{1,0:T(8,128)(2,1)}) custom-call(s32[4]{0:T(128)} %fc_in.5, s32[4,32]{1,0:T(4,128)} %bitcast.15, bf16[128,1536]{1,0:T(8,128)(2,1)} %bitcast.10, bf16[128,1536]{1,0:T(8,128)(2,1)S(1)} %get-tuple-element.21.dhid, f32[128,1536]{1,0:T(8,128)S(1)} %get-tuple-element.22.dn, ...), custom_call_target="tpu_custom_call" | custom-call | flops 10000000 | bytes 4000000 | tf_op jit(solution)/shard_map/finish/pallas_call | solution.py:538
  (2 shorter events, 0.0 us)
Async XLA Ops:
  2.8 6.9 %collective-permute-start.2 = (bf16[32,1536]{1,0:T(8,128)(2,1)S(1)}, bf16[32,1536]{1,0:T(8,128)(2,1)S(1)}, u32[]{:S(2)}, u32[]{:S(2)}) collective-permute-start(bf16[32,1536]{1,0:T(8,128)(2,1)S(1)} %get-tuple-element.18), channel_id=1, source_target_pairs={{0,1},{1,0},{2,3},{3,2},{4,5},{5,4},{6,7},{7,6},{8,9},{9,8},{10,11... | collective-permute-start | bytes 294920 | tf_op jit(solution)/shard_map/ppermute | solution.py:449
  4.1 6.6 %collective-permute-start.3 = (bf16[32,1536]{1,0:T(8,128)(2,1)S(1)}, bf16[32,1536]{1,0:T(8,128)(2,1)S(1)}, u32[]{:S(2)}, u32[]{:S(2)}) collective-permute-start(bf16[32,1536]{1,0:T(8,128)(2,1)S(1)} %get-tuple-element.19), channel_id=1, source_target_pairs={{0,2},{1,3},{2,0},{3,1},{4,6},{5,7},{6,4},{7,5},{8,10},{9,11},{10,... | collective-permute-start | bytes 294920 | tf_op jit(solution)/shard_map/ppermute | solution.py:449
  6.8 6.8 %collective-permute-start.4 = (bf16[32,1536]{1,0:T(8,128)(2,1)S(1)}, bf16[32,1536]{1,0:T(8,128)(2,1)S(1)}, u32[]{:S(2)}, u32[]{:S(2)}) collective-permute-start(bf16[32,1536]{1,0:T(8,128)(2,1)S(1)} %get-tuple-element.20), channel_id=1, source_target_pairs={{0,3},{1,2},{2,1},{3,0},{4,7},{5,6},{6,5},{7,4},{8,11},{9,10},{10,... | collective-permute-start | bytes 294920 | tf_op jit(solution)/shard_map/ppermute | solution.py:449
  6.8 12.5 %collective-permute-start = (bf16[96,1536]{1,0:T(8,128)(2,1)S(1)}, bf16[96,1536]{1,0:T(8,128)(2,1)S(1)}, u32[]{:S(2)}, u32[]{:S(2)}) collective-permute-start(bf16[96,1536]{1,0:T(8,128)(2,1)S(1)} %get-tuple-element.15), channel_id=1, source_target_pairs={{0,4},{4,0},{8,12},{12,8},{16,20},{20,16},{24,28},{28,24},{32,36},... | collective-permute-start | bytes 884744 | tf_op jit(solution)/shard_map/ppermute | solution.py:444
  8.2 11.1 %collective-permute-start.1 = (bf16[96,1536]{1,0:T(8,128)(2,1)S(1)}, bf16[96,1536]{1,0:T(8,128)(2,1)S(1)}, u32[]{:S(2)}, u32[]{:S(2)}) collective-permute-start(bf16[96,1536]{1,0:T(8,128)(2,1)S(1)} %get-tuple-element.16), channel_id=1, source_target_pairs={{0,1},{1,0},{2,3},{3,2},{4,8},{5,9},{6,10},{7,11},{8,4},{9,5},{10,... | collective-permute-start | bytes 884744 | tf_op jit(solution)/shard_map/ppermute | solution.py:444
  13.6 5.7 %collective-permute-start.6 = (bf16[16,1536]{1,0:T(8,128)(2,1)S(1)}, bf16[16,1536]{1,0:T(8,128)(2,1)S(1)}, u32[]{:S(2)}, u32[]{:S(2)}) collective-permute-start(bf16[16,1536]{1,0:T(8,128)(2,1)S(1)} %get-tuple-element.28), channel_id=1, source_target_pairs={{0,1},{1,0},{2,3},{3,2},{4,8},{5,9},{6,10},{7,11},{8,4},{9,5},{10,... | collective-permute-start | bytes 147464 | tf_op jit(solution)/shard_map/ppermute | solution.py:444
  16.0 3.3 %collective-permute-start.5 = (bf16[16,1536]{1,0:T(8,128)(2,1)S(1)}, bf16[16,1536]{1,0:T(8,128)(2,1)S(1)}, u32[]{:S(2)}, u32[]{:S(2)}) collective-permute-start(bf16[16,1536]{1,0:T(8,128)(2,1)S(1)} %get-tuple-element.29), channel_id=1, source_target_pairs={{0,4},{4,0},{8,12},{12,8},{16,20},{20,16},{24,28},{28,24},{32,36},... | collective-permute-start | bytes 147464 | tf_op jit(solution)/shard_map/ppermute | solution.py:444
  49.4 9.8 %collective-permute-start.7 = (bf16[64,1536]{1,0:T(8,128)(2,1)S(1)}, bf16[64,1536]{1,0:T(8,128)(2,1)S(1)}, u32[]{:S(2)}, u32[]{:S(2)}) collective-permute-start(bf16[64,1536]{1,0:T(8,128)(2,1)S(1)} %get-tuple-element.23), channel_id=1, source_target_pairs={{0,4},{4,0},{8,12},{12,8},{16,20},{20,16},{24,28},{28,24},{32,36},... | collective-permute-start | bytes 589832 | tf_op jit(solution)/shard_map/ppermute | solution.py:444
  49.5 9.7 %collective-permute-start.8 = (bf16[64,1536]{1,0:T(8,128)(2,1)S(1)}, bf16[64,1536]{1,0:T(8,128)(2,1)S(1)}, u32[]{:S(2)}, u32[]{:S(2)}) collective-permute-start(bf16[64,1536]{1,0:T(8,128)(2,1)S(1)} %get-tuple-element.24), channel_id=1, source_target_pairs={{0,1},{1,0},{2,3},{3,2},{4,8},{5,9},{6,10},{7,11},{8,4},{9,5},{10,... | collective-permute-start | bytes 589832 | tf_op jit(solution)/shard_map/ppermute | solution.py:444
  51.9 6.3 %collective-permute-start.11 = (bf16[32,1536]{1,0:T(8,128)(2,1)S(1)}, bf16[32,1536]{1,0:T(8,128)(2,1)S(1)}, u32[]{:S(2)}, u32[]{:S(2)}) collective-permute-start(bf16[32,1536]{1,0:T(8,128)(2,1)S(1)} %get-tuple-element.25.l0), channel_id=1, source_target_pairs={{0,3},{1,2},{2,1},{3,0},{4,7},{5,6},{6,5},{7,4},{8,11},{9,10},{10,... | collective-permute-start | bytes 294920 | tf_op jit(solution)/shard_map/ppermute | solution.py:449
  52.3 5.9 %collective-permute-start.10 = (bf16[32,1536]{1,0:T(8,128)(2,1)S(1)}, bf16[32,1536]{1,0:T(8,128)(2,1)S(1)}, u32[]{:S(2)}, u32[]{:S(2)}) collective-permute-start(bf16[32,1536]{1,0:T(8,128)(2,1)S(1)} %get-tuple-element.25.l0), channel_id=1, source_target_pairs={{0,2},{1,3},{2,0},{3,1},{4,6},{5,7},{6,4},{7,5},{8,10},{9,11},{10,... | collective-permute-start | bytes 294920 | tf_op jit(solution)/shard_map/ppermute | solution.py:449
  52.9 6.2 %collective-permute-start.9 = (bf16[32,1536]{1,0:T(8,128)(2,1)S(1)}, bf16[32,1536]{1,0:T(8,128)(2,1)S(1)}, u32[]{:S(2)}, u32[]{:S(2)}) collective-permute-start(bf16[32,1536]{1,0:T(8,128)(2,1)S(1)} %get-tuple-element.25.l0), channel_id=1, source_target_pairs={{0,1},{1,0},{2,3},{3,2},{4,5},{5,4},{6,7},{7,6},{8,9},{9,8},{10,11... | collective-permute-start | bytes 294920 | tf_op jit(solution)/shard_map/ppermute | solution.py:449

commit v3 on v2

v3 whole, which is shorter than its diff:
```python
import jax
import jax.numpy as jnp
from jax import lax
from jax.experimental import pallas as pl
from jax.experimental.pallas import tpu as pltpu
from jax.sharding import PartitionSpec as P

D = 1536
REACH = 64
KERN = 32
FR = 128
HALO = 96
EXT = FR + 2 * HALO
QR = FR + 64
SR = FR + 32
PR = SR // 4
LR = FR // 4
SLOTS = 64
NREC = 4
HEAD = 96
LANE = 128
NB = D // LANE
COL = 1536
NC = D // COL
GROUP = 4 * HEAD
EPSILON = 1e-06
SCALE = HEAD ** (-0.5)
BF = jnp.bfloat16
F32 = jnp.float32
WINDOWS = ((0, 1), (0, 2), (1, 3), (2, 3))

VMEM = pl.BlockSpec(memory_space=pltpu.VMEM)
ANY = pl.BlockSpec(memory_space=pl.ANY)


def dot(a, b):
    return lax.dot_general(a, b, (((1,), (0,)), ((), ())), preferred_element_type=F32)


def dot_t(a, b):
    return lax.dot_general(a, b, (((1,), (1,)), ((), ())), preferred_element_type=F32)


def t_dot(a, b):
    return lax.dot_general(a, b, (((0,), (0,)), ((), ())), preferred_element_type=F32)


def lanes(c, width=LANE):
    return pl.ds(pl.multiple_of(c * width, width), width)


def routes(fc, tl, slice_index):
    starts, lives = [], []
    total = 0
    for b in range(NREC):
        live = jnp.clip(fc[b] // 4 - slice_index * LR, 0, LR)
        total = total + tl[b, slice_index]
        starts.append(total)
        lives.append(live)
        total = total + live
    return starts, lives


def pick(values, index):
    out = values[0]
    for b in range(1, NREC):
        out = jnp.where(index == b, values[b], out)
    return out


def prepare(fc_in, tl_in, audio, grads, send_a, send_b, own, pair, mate, fc, tl, g_buf, sems):
    cf = pltpu.make_async_copy(fc_in, fc, sems.at[0])
    ct = pltpu.make_async_copy(tl_in, tl, sems.at[1])
    cf.start()
    ct.start()
    tm = lax.axis_index("tm")
    llm = lax.axis_index("llm")
    off_a = (1 - tm % 2) * (FR - HALO)
    off_b = (FR - HALO) - off_a
    cg = pltpu.make_async_copy(grads, g_buf, sems.at[2])
    ca = pltpu.make_async_copy(audio.at[pl.ds(pl.multiple_of(off_a, 32), HALO)], send_a, sems.at[3])
    cb = pltpu.make_async_copy(audio.at[pl.ds(pl.multiple_of(off_b, 32), HALO)], send_b, sems.at[4])
    cg.start()
    ca.start()
    cb.start()
    cf.wait()
    ct.wait()
    starts, lives = routes(fc, tl, tm)
    row = lax.broadcasted_iota(jnp.int32, (LR, SLOTS), 0)
    slot = lax.broadcasted_iota(jnp.int32, (LR, SLOTS), 1) + llm * SLOTS
    picked = []
    for j in range(NREC):
        b = llm ^ j
        chosen = (row < pick(lives, b)) & (slot == row + pick(starts, b))
        picked.append(jnp.where(chosen, 1.0, 0.0).astype(BF))
    cg.wait()
    moved = dot(jnp.concatenate(picked, axis=0), g_buf[...]).astype(BF)
    own[...] = moved[:LR]
    pair[...] = moved[LR : 3 * LR]
    mate[...] = moved[3 * LR :]
    ca.wait()
    cb.wait()


def norm_rows(x, gains, out, rows):
    inv = lax.rsqrt(jnp.mean(x * x, axis=-1, keepdims=True) + EPSILON)
    for c in range(NB):
        cols = slice(c * LANE, (c + 1) * LANE)
        out[rows, cols] = (x[:, cols] * inv * gains[c : c + 1, :]).astype(BF)


def project_own(
    after, audio, gains_in, w_key, w_value, w_query, w_out,
    x_o, gain_o, k_o, v_o, q_o, wk_o, wv_o, wq_o, wo_o, n_s, w_sems, sems,
):
    cx = pltpu.make_async_copy(audio, x_o, sems.at[0])
    cg = pltpu.make_async_copy(gains_in, gain_o, sems.at[1])
    cx.start()
    cg.start()

    def w_copy(n, j):
        src = (w_key, w_value, w_query, w_out)[n]
        dst = (wk_o, wv_o, wq_o, wo_o)[n]
        return pltpu.make_async_copy(src.at[:, lanes(j, COL)], dst.at[:, lanes(j, COL)], w_sems.at[n, j])

    for n in range(4):
        for j in range(NC):
            w_copy(n, j).start()
    cx.wait()
    cg.wait()
    for r in range(2):
        rows = slice(r * 64, r * 64 + 64)
        norm_rows(x_o[rows, :].astype(F32), gain_o, n_s, rows)
    for n, (w_s, out_s) in enumerate(((wk_o, k_o), (wv_o, v_o), (wq_o, q_o))):
        for j in range(NC):
            w_copy(n, j).wait()
            cols = slice(j * COL, (j + 1) * COL)
            out_s[:, cols] = dot(n_s[...], w_s[:, cols]).astype(BF)
    for j in range(NC):
        w_copy(3, j).wait()


def combine(after, mate, got_pair, out):
    out[...] = mate[...] + got_pair[LR:, :]


def split_edges(after, own, got_pair, got_mate, grad_o, send_a, send_b):
    grads = own[...] + got_pair[:LR, :] + got_mate[...]
    grad_o[...] = grads
    even = lax.axis_index("tm") % 2 == 0

    @pl.when(even)
    def _():
        send_a[...] = grads[16:]
        send_b[...] = grads[:16]

    @pl.when(jnp.logical_not(even))
    def _():
        send_a[...] = grads[:16]
        send_b[...] = grads[16:]


def head_mask(j, lo, hi):
    lane = lax.broadcasted_iota(jnp.int32, (1, (hi - lo) * LANE), 1) + lo * LANE
    return jnp.where((lane >= j * HEAD) & (lane < (j + 1) * HEAD), 1.0, 0.0).astype(BF)


def window(g, lo, hi):
    return pl.ds(pl.multiple_of(g * GROUP + lo * LANE, LANE), (hi - lo) * LANE)


def add_tiles(tiles, lo, value):
    for t in range(value.shape[1] // LANE):
        part = value[:, t * LANE : (t + 1) * LANE]
        tiles[lo + t] = part if tiles[lo + t] is None else tiles[lo + t] + part


def attend(
    fc_in, recv_a, recv_b, x_own, gains, k_own, v_own, q_own, wk_s, wv_s, wq_s,
    xq_o, q_s, k_s, v_s, p_s, att_s, fc, n_s, bias_s, sems,
):
    fc_copy = pltpu.make_async_copy(fc_in, fc, sems.at[0])
    fc_copy.start()
    tm = lax.axis_index("tm")
    llm = lax.axis_index("llm")
    even = tm % 2 == 0
    first = tm * FR
    total = lax.axis_size("tm") * FR

    @pl.when(even)
    def _():
        norm_rows(recv_b[...].astype(F32), gains, n_s, slice(0, HALO))
        norm_rows(recv_a[...].astype(F32), gains, n_s, slice(HALO, 2 * HALO))
        xq_o[0:32, :] = recv_b[64:96, :]
        xq_o[160:192, :] = recv_a[0:32, :]

    @pl.when(jnp.logical_not(even))
    def _():
        norm_rows(recv_a[...].astype(F32), gains, n_s, slice(0, HALO))
        norm_rows(recv_b[...].astype(F32), gains, n_s, slice(HALO, 2 * HALO))
        xq_o[0:32, :] = recv_a[64:96, :]
        xq_o[160:192, :] = recv_b[0:32, :]

    xq_o[32:160, :] = x_own[...]
    k_s[96:224, :] = k_own[...]
    v_s[96:224, :] = v_own[...]
    q_s[32:160, :] = q_own[...]
    for w_s, out_s in ((wk_s, k_s), (wv_s, v_s)):
        @pl.loop(0, NC)
        def _(j, w_s=w_s, out_s=out_s):
            cols = lanes(j, COL)
            new = dot(n_s[...], w_s[:, cols]).astype(BF)
            out_s[0:96, cols] = new[0:96]
            out_s[224:320, cols] = new[96:192]

    @pl.loop(0, NC)
    def _(j):
        cols = lanes(j, COL)
        new = dot(n_s[64:128, :], wq_s[:, cols]).astype(BF)
        q_s[0:32, cols] = new[0:32]
        q_s[160:192, cols] = new[32:64]

    fc_copy.wait()
    limit = fc[llm]

    def bias_of(rows, q_first, k_first):
        qe = lax.broadcasted_iota(jnp.int32, (rows, 256), 0) + q_first
        ke = lax.broadcasted_iota(jnp.int32, (rows, 256), 1) + k_first
        kt = ke + (first - HALO)
        ok = (ke >= qe - REACH) & (ke < qe + REACH) & (kt >= 0) & (kt < total) & ((kt < limit) | (ke == qe))
        return jnp.where(ok, 0.0, -1e30)

    bias_s[0:32, :] = bias_of(32, 64, 0)
    bias_s[32:160, :] = bias_of(FR, HALO, 32)
    bias_s[160:192, :] = bias_of(32, 224, 64)

    @pl.loop(0, 4)
    def _(g):
        heads = []
        for j, (lo, hi) in enumerate(WINDOWS):
            win = window(g, lo, hi)
            q = q_s[:, win] * head_mask(j, lo, hi)
            k = k_s[:, win]
            heads.append(
                jnp.concatenate(
                    [dot_t(q[0:32], k[0:256]), dot_t(q[32:160], k[32:288]), dot_t(q[160:192], k[64:320])], axis=0
                )
            )
        heads = [scores * SCALE + bias_s[...] for scores in heads]
        highest = [jnp.max(scores, axis=-1, keepdims=True) for scores in heads]
        heads = [jnp.exp(scores - top) for scores, top in zip(heads, highest)]
        inverse = [1.0 / jnp.sum(powers, axis=-1, keepdims=True) for powers in heads]
        heads = [(powers * inv).astype(BF) for powers, inv in zip(heads, inverse)]
        parts = [[None] * 3 for _ in range(3)]
        for j, (lo, hi) in enumerate(WINDOWS):
            v = v_s[:, window(g, lo, hi)] * head_mask(j, lo, hi)
            p = heads[j]
            p_s[g * 4 + j] = p[32:160]
            add_tiles(parts[0], lo, dot(p[0:32], v[0:256]))
            add_tiles(parts[1], lo, dot(p[32:160], v[32:288]))
            add_tiles(parts[2], lo, dot(p[160:192], v[64:320]))
        for t in range(3):
            at = window(g, t, t + 1)
            att_s[0:32, at] = parts[0][t].astype(BF)
            att_s[32:160, at] = parts[1][t].astype(BF)
            att_s[160:192, at] = parts[2][t].astype(BF)


def spoken_rows(fc, tm, llm):
    frame = lax.broadcasted_iota(jnp.int32, (QR, 1), 0) + (tm * FR - 32)
    return jnp.where((frame >= 0) & (frame < fc[llm]), 1.0, 0.0)


def convolve(
    fc_in, xq, att_s, wo_s, cg_in, lg_in, taps_in,
    lat_o, h_s, dsilu_s, pool_s, inv_o, cg_s, lg_s, tap_s, fc, ci_s, up_s, norm_t, sems,
):
    copies = [
        pltpu.make_async_copy(source, into, sems.at[i])
        for i, (source, into) in enumerate(((fc_in, fc), (cg_in, cg_s), (lg_in, lg_s), (taps_in, tap_s)))
    ]
    for copy in copies:
        copy.start()
    tm = lax.axis_index("tm")
    llm = lax.axis_index("llm")

    def hidden_step(j, squares):
        cols = lanes(j, COL)
        h = dot(att_s[...], wo_s[:, cols]) + xq[:, cols].astype(F32)
        h = h.astype(BF).astype(F32)
        for t in range(COL // LANE):
            part = h[:, t * LANE : (t + 1) * LANE]
            h_s[j * (COL // LANE) + t] = part
            squares = squares + part * part
        return squares

    squares = lax.fori_loop(0, NC, hidden_step, jnp.zeros((QR, LANE), F32))
    inv_h = lax.rsqrt(jnp.sum(squares, axis=-1, keepdims=True) * (1.0 / D) + EPSILON)
    inv_o[...] = jnp.broadcast_to(inv_h, (QR, LANE))
    for copy in copies:
        copy.wait()
    inv_spoken = inv_h * spoken_rows(fc, tm, llm)

    def conv_step(c, squares):
        cols = lanes(c)
        ci_s[...] = (h_s[c] * inv_spoken * cg_s[pl.ds(c, 1), :]).astype(BF).astype(F32)
        kern = tap_s[:, cols]
        acc = jnp.zeros((SR, LANE), F32)
        for s in range(8):
            xs = ci_s[s : s + SR + 24, :]
            for u in range(4):
                m = s + 8 * u
                acc = acc + kern[m : m + 1, :] * xs[8 * u : 8 * u + SR]
        sig = 1.0 / (1.0 + jnp.exp(-acc))
        silu = acc * sig
        dsilu_s[c] = sig + silu * (1.0 - sig)
        up_s[...] = h_s[c, 16 : 16 + SR, :] + silu
        pooled = up_s[pl.ds(0, PR, 4), :]
        for u in range(1, 4):
            pooled = pooled + up_s[pl.ds(u, PR, 4), :]
        pooled = pooled * 0.25
        pool_s[c] = pooled
        return squares + pooled * pooled

    squares = lax.fori_loop(0, NB, conv_step, jnp.zeros((PR, LANE), F32))
    inv_p = lax.rsqrt(jnp.sum(squares, axis=-1, keepdims=True) * (1.0 / D) + EPSILON)
    for c in range(NB):
        norm_t[...] = pool_s[c] * inv_p * lg_s[c : c + 1, :]
        lat_o[:, c * LANE : (c + 1) * LANE] = norm_t[4:36, :].astype(BF)


def convolve_back(
    fc_in, lat_grad, edge_a, edge_b, h_s, dsilu_s, pool_s, inv_s, cg_s, lg_s, tap_s, wo_s,
    dhid_s, datt_s, fc, g_s, up_s, ds_s, us_s, dnc_s, sems,
):
    copy = pltpu.make_async_copy(fc_in, fc, sems.at[0])
    copy.start()
    tm = lax.axis_index("tm")
    llm = lax.axis_index("llm")
    even = tm % 2 == 0

    row = lax.broadcasted_iota(jnp.int32, (PR, 64), 0)
    col = lax.broadcasted_iota(jnp.int32, (PR, 64), 1)
    at = tm * LR + row - 4
    chosen = (col == row + 12) & (at >= 0) & (at < lax.axis_size("tm") * LR)
    chosen = jnp.where(chosen, 1.0, 0.0).astype(BF)
    left = jnp.where(even, 0.0, 1.0).astype(BF)
    right = jnp.where(even, 1.0, 0.0).astype(BF)
    stacked = jnp.concatenate(
        [
            edge_a[...] * left + edge_b[...] * right,
            lat_grad[...],
            edge_a[...] * right + edge_b[...] * left,
        ],
        axis=0,
    )
    g_s[...] = dot(chosen, stacked)

    def sums(c, carry):
        squares, along = carry
        pooled = pool_s[c]
        return squares + pooled * pooled, along + g_s[:, lanes(c)] * lg_s[pl.ds(c, 1), :] * pooled

    zero = jnp.zeros((PR, LANE), F32)
    squares, along = lax.fori_loop(0, NB, sums, (zero, zero))
    inv_p = lax.rsqrt(jnp.sum(squares, axis=-1, keepdims=True) * (1.0 / D) + EPSILON)
    back_p = inv_p * inv_p * inv_p * (jnp.sum(along, axis=-1, keepdims=True) * (1.0 / D))
    inv_own = inv_s[32:160, :]
    copy.wait()
    spoken_own = spoken_rows(fc, tm, llm)[32:160]

    def conv_back(c, along):
        cols = lanes(c)
        gain = lg_s[pl.ds(c, 1), :]
        dpool = (g_s[:, cols] * gain * inv_p - pool_s[c] * back_p) * 0.25
        for u in range(4):
            up_s[pl.ds(u, PR, 4), :] = dpool
        ds_s[...] = up_s[...] * dsilu_s[c]
        us_s[c] = up_s[16 : 16 + FR, :]
        kern = tap_s[:, cols]
        acc = jnp.zeros((FR, LANE), F32)
        for s in range(8):
            base = 8 if s == 0 else s
            xs = ds_s[base : base + FR + 24, :]
            for u in range(4):
                m = 32 - base - 8 * u
                acc = acc + kern[m : m + 1, :] * xs[8 * u : 8 * u + FR]
        dn = acc.astype(BF).astype(F32) * spoken_own * cg_s[pl.ds(c, 1), :]
        dnc_s[c] = dn
        return along + dn * h_s[c, 32:160, :]

    along = lax.fori_loop(0, NB, conv_back, jnp.zeros((FR, LANE), F32))
    back_h = inv_own * inv_own * inv_own * (jnp.sum(along, axis=-1, keepdims=True) * (1.0 / D))

    @pl.loop(0, NB)
    def _(c):
        dhid_s[:, lanes(c)] = (us_s[c] + dnc_s[c] * inv_own - h_s[c, 32:160, :] * back_h).astype(BF)

    @pl.loop(0, NC)
    def _(j):
        datt_s[:, lanes(j, COL)] = dot_t(dhid_s[...], wo_s[lanes(j, COL), :]).astype(BF)


def attend_back(q_s, k_s, v_s, p_s, datt_s, wk_s, wv_s, send_a, send_b, dq_s, dk_s, dv_s, ek_s, ev_s):
    @pl.loop(0, 4)
    def _(g):
        heads = []
        for j, (lo, hi) in enumerate(WINDOWS):
            win = window(g, lo, hi)
            heads.append(dot_t(datt_s[:, win] * head_mask(j, lo, hi), v_s[32:288, win]))
        weights = [p_s[g * 4 + j].astype(F32) for j in range(4)]
        heads = [w * dp for w, dp in zip(weights, heads)]
        sums = [jnp.sum(pd, axis=-1, keepdims=True) for pd in heads]
        heads = [((pd - w * total) * SCALE).astype(BF) for pd, w, total in zip(heads, weights, sums)]
        dq, dk, dv = [None] * 3, [None] * 3, [None] * 3
        for j, (lo, hi) in enumerate(WINDOWS):
            win = window(g, lo, hi)
            mask = head_mask(j, lo, hi)
            add_tiles(dq, lo, dot(heads[j], k_s[32:288, win] * mask))
            add_tiles(dk, lo, t_dot(heads[j], q_s[32:160, win] * mask))
            add_tiles(dv, lo, t_dot(p_s[g * 4 + j], datt_s[:, win] * mask))
        for t in range(3):
            at = window(g, t, t + 1)
            dq_s[:, at] = dq[t].astype(BF)
            for out, edge, tiles in ((dk_s, ek_s, dk), (dv_s, ev_s, dv)):
                new = tiles[t].astype(BF)
                edge[0:64, at] = new[0:64]
                out[:, at] = new[64:192]
                edge[64:128, at] = new[192:256]

    even = lax.axis_index("tm") % 2 == 0

    @pl.loop(0, NC)
    def _(j):
        cols = lanes(j, COL)
        both = (dot_t(ek_s[...], wk_s[cols, :]) + dot_t(ev_s[...], wv_s[cols, :])).astype(BF)

        @pl.when(even)
        def _():
            send_a[:, cols] = both[64:128]
            send_b[:, cols] = both[0:64]

        @pl.when(jnp.logical_not(even))
        def _():
            send_a[:, cols] = both[0:64]
            send_b[:, cols] = both[64:128]


def project_back(after, dq, dk, dv, wq_s, wk_s, wv_s, dn_o):
    @pl.loop(0, NC)
    def _(j):
        cols = lanes(j, COL)
        dn_o[:, cols] = (
            dot_t(dk[...], wk_s[cols, :]) + dot_t(dv[...], wv_s[cols, :]) + dot_t(dq[...], wq_s[cols, :])
        )


def finish(
    fc_in, tl_in, x_s, dh_s, dn_s, recv_a, recv_b, l0, l1, l23, gains,
    rows_out, grad_out, fc, tl, r_s, g_s, out_s, rows_s, sems,
):
    cf = pltpu.make_async_copy(fc_in, fc, sems.at[0])
    ct = pltpu.make_async_copy(tl_in, tl, sems.at[1])
    cf.start()
    ct.start()
    tm = lax.axis_index("tm")
    llm = lax.axis_index("llm")
    even = tm % 2 == 0

    @pl.when(even)
    def _():
        r_s[0:64, :] = recv_b[...]
        r_s[64:128, :] = recv_a[...]

    @pl.when(jnp.logical_not(even))
    def _():
        r_s[0:64, :] = recv_a[...]
        r_s[64:128, :] = recv_b[...]

    copies = []
    for half in range(2):
        rows = slice(half * 64, half * 64 + 64)
        inside = (tm > 0) if half == 0 else (tm < lax.axis_size("tm") - 1)
        keep = jnp.where(inside, 1.0, 0.0)
        x = x_s[rows, :].astype(F32)
        inv = lax.rsqrt(jnp.mean(x * x, axis=-1, keepdims=True) + EPSILON)
        along = jnp.zeros((64, LANE), F32)
        for c in range(NB):
            cols = slice(c * LANE, (c + 1) * LANE)
            g = (dn_s[rows, cols] + r_s[rows, cols].astype(F32) * keep).astype(BF).astype(F32) * gains[c : c + 1, :]
            g_s[rows, cols] = g
            along = along + g * x[:, cols]
        back = inv * inv * inv * (jnp.sum(along, axis=-1, keepdims=True) * (1.0 / D))
        out_s[rows, :] = (dh_s[rows, :].astype(F32) + g_s[rows, :] * inv - x * back).astype(BF)
        copy = pltpu.make_async_copy(out_s.at[rows], grad_out.at[rows], sems.at[2 + half])
        copy.start()
        copies.append(copy)
    cf.wait()
    ct.wait()
    starts, lives = routes(fc, tl, tm)
    slot = lax.broadcasted_iota(jnp.int32, (SLOTS, NREC * LR), 0) + llm * SLOTS
    col = lax.broadcasted_iota(jnp.int32, (SLOTS, NREC * LR), 1)
    chosen = jnp.zeros((SLOTS, NREC * LR), F32)
    for j, apart in enumerate((0, 1, 3, 2)):
        b = llm ^ apart
        r = col - j * LR
        hit = (r >= 0) & (r < pick(lives, b)) & (slot == r + pick(starts, b))
        chosen = jnp.where(hit, 1.0, chosen)
    latents = jnp.concatenate([l0[...], l1[...], l23[...]], axis=0)
    rows_s[...] = dot(chosen.astype(BF), latents).astype(BF)
    copy = pltpu.make_async_copy(rows_s, rows_out, sems.at[4])
    copy.start()
    for copy in copies + [copy]:
        copy.wait()


def swap(count, cells_a, cells_b):
    pairs_a = [(i, i ^ 1) for i in range(count)]
    n = lax.axis_size("llm")
    full_b = []
    for i in range(count):
        partner = ((i + 1) ^ 1) - 1
        end = partner < 0 or partner >= count
        full_b += [(i * n + y, i * n + (y ^ 1) if end else partner * n + y) for y in range(n)]
    return lax.ppermute(cells_a, "tm", pairs_a), lax.ppermute(cells_b, ("tm", "llm"), full_b)


def trade(cells, apart):
    n = lax.axis_size("llm")
    return lax.ppermute(cells, "llm", [(i, i ^ apart) for i in range(n)])


def hbm(array):
    return pltpu.with_memory_space_constraint(array, pltpu.HBM)


def vmem(array):
    return pltpu.with_memory_space_constraint(array, pltpu.VMEM)


def call(kernel, ins, outs, scratch, flops, outs_in_hbm=False):
    place = {"h": hbm, "v": vmem, "n": lambda array: array}
    spec = {"h": ANY, "v": VMEM, "n": ANY}
    if outs_in_hbm:
        shapes = [jax.ShapeDtypeStruct(s, d) for s, d in outs]
    else:
        shapes = [pltpu.VMEM(s, d) for s, d in outs]
    return pl.pallas_call(
        kernel,
        out_shape=shapes,
        in_specs=[spec[kind] for kind, _ in ins],
        out_specs=[ANY if outs_in_hbm else VMEM] * len(outs),
        scratch_shapes=scratch,
        compiler_params=pltpu.CompilerParams(vmem_limit_bytes=12 * 1024 * 1024),
        cost_estimate=pl.CostEstimate(flops=flops, bytes_accessed=1_000_000, transcendentals=0),
        name=kernel.__name__,
    )(*[place[kind](array) for kind, array in ins])


def mark(kind, *arrays):
    return [(kind, array) for array in arrays]


def on_device(
    audio, frame_counts, text_lengths, norm_gain, w_query, w_key, w_value, w_out,
    conv_gain, conv_kernel, latent_gain, llm_grads,
):
    signal = audio[0]
    n_tm = lax.axis_size("tm")
    norm_row, conv_row, latent_row = (g.reshape(NB, LANE) for g in (norm_gain, conv_gain, latent_gain))
    tl_in = text_lengths.T
    V = pltpu.VMEM
    fc = pltpu.SMEM((NREC,), jnp.int32)
    tl = pltpu.SMEM((NREC, n_tm), jnp.int32)
    gain = ((NB, LANE), F32)
    weight = ((D, D), BF)

    def rows(n, dtype=BF):
        return ((n, D), dtype)

    def sems(*dims):
        return pltpu.SemaphoreType.DMA(dims)

    send_a, send_b, own, pair, mate = call(
        prepare,
        mark("h", frame_counts, tl_in, signal, llm_grads[0]),
        [rows(HALO), rows(HALO), rows(LR), rows(2 * LR), rows(LR)],
        [fc, tl, V((SLOTS, D), BF), sems(5)],
        100_000_000,
    )
    got_pair = trade(pair, 1)
    recv_a, recv_b = swap(n_tm, send_a, send_b)
    x, gains, k_own, v_own, q_own, wk, wv, wq, wo = call(
        project_own,
        mark("v", own) + mark("h", signal, norm_row, w_key, w_value, w_query, w_out),
        [rows(FR), gain, rows(FR), rows(FR), rows(FR), weight, weight, weight, weight],
        [V((FR, D), BF), sems(4, NC), sems(2)],
        6_000_000_000,
    )
    (both,) = call(combine, mark("v", gains, mate, got_pair), [rows(LR)], [], 1_000_000)
    got_mate = trade(both, 3)
    xq, q, k, v, p, att = call(
        attend,
        mark("h", frame_counts) + mark("v", recv_a, recv_b, x, gains, k_own, v_own, q_own, wk, wv, wq),
        [rows(QR), rows(QR), rows(EXT), rows(EXT), ((16, FR, 256), BF), rows(QR)],
        [fc, V((2 * HALO, D), BF), V((QR, 256), F32), sems(1)],
        8_000_000_000,
    )
    lat_grad, first_a, first_b = call(
        split_edges, mark("v", xq, own, got_pair, got_mate), [rows(LR), rows(16), rows(16)], [], 1_000_000
    )
    edge_a, edge_b = swap(n_tm, first_a, first_b)
    latent, h, dsilu, pool, inv, cgain, lgain, taps = call(
        convolve,
        mark("h", frame_counts) + mark("v", xq, att, wo) + mark("h", conv_row, latent_row, conv_kernel),
        [
            rows(LR), ((NB, QR, LANE), F32), ((NB, SR, LANE), F32), ((NB, PR, LANE), F32), ((QR, LANE), F32),
            gain, gain, rows(KERN, F32),
        ],
        [fc, V((QR, LANE), F32), V((SR, LANE), F32), V((PR, LANE), F32), sems(4)],
        5_000_000_000,
    )
    latent_1 = trade(latent, 1)
    dhid, datt = call(
        convolve_back,
        mark("h", frame_counts)
        + mark("v", lat_grad, edge_a, edge_b, h, dsilu, pool, inv, cgain, lgain, taps, wo),
        [rows(FR), rows(FR)],
        [
            fc, V((PR, D), F32), V((SR, LANE), F32), V((SR, LANE), F32), V((NB, FR, LANE), F32),
            V((NB, FR, LANE), F32), sems(1),
        ],
        5_000_000_000,
    )
    latent_23 = trade(jnp.concatenate([latent, latent_1], axis=0), 3)
    back_a, back_b, dq, dk, dv = call(
        attend_back,
        mark("v", q, k, v, p, datt, wk, wv),
        [rows(64), rows(64), rows(FR), rows(FR), rows(FR)],
        [V((FR, D), BF), V((FR, D), BF)],
        6_000_000_000,
    )
    ret_a, ret_b = swap(n_tm, back_a, back_b)
    (dn,) = call(
        project_back,
        mark("v", back_a, dq, dk, dv, wq, wk, wv),
        [rows(FR, F32)],
        [],
        3_000_000_000,
    )
    out_rows, grad = call(
        finish,
        mark("h", frame_counts, tl_in)
        + mark("v", x, dhid, dn, ret_a, ret_b, latent, latent_1, latent_23, gains),
        [rows(SLOTS), rows(FR)],
        [fc, tl, V((FR, D), BF), V((FR, D), F32), V((FR, D), BF), V((SLOTS, D), BF), sems(5)],
        1_000_000_000,
        outs_in_hbm=True,
    )
    return (out_rows[None], grad[None])


def solution(mesh):
    placed = (P("llm", "tm", None),) + (P(),) * 10 + (P("tm", "llm", None),)
    return jax.shard_map(
        on_device,
        mesh=mesh,
        in_specs=placed,
        out_specs=(P("tm", "llm", None), P("llm", "tm", None)),
        check_vma=False,
    )
```

time: 62.5 us -> 53.8 us (0.86)
  the two profiles are of different devices: /device:TPU:39 before, /device:TPU:96 now
where the time goes in v3:
time: 53.8 us; the launch traced here: 53.6 us
  Pallas kernels  37.2 us (69%)
  starting transfers between devices  12.1 us (22%)
  waiting for transfers between devices  3.29 us (6%)
  between operations  0.91 us (2%)
    pallas_call x10, Pallas kernels, call(): pl.pallas_call(kernel, out_shape=shapes, in_specs=[spec[kind] for kind, _...  37.2 us
    ppermute x3, starting transfers between devices, swap(): lax.ppermute(cells_b, ('tm', 'llm'), full_b)  6.6 us
    ppermute x4, starting transfers between devices, trade(): return lax.ppermute(cells, 'llm', [(i, i ^ apart) for i in range(n)])  5.45 us
    ppermute x4, waiting for transfers between devices, trade(): return lax.ppermute(cells, 'llm', [(i, i ^ apart) for i in range(n)])  3.28 us
  transfers between devices with their start and end apart: 10, of which 1 were waited for; matrix products, arithmetic and copies ran while one was open for 0% of the time, Pallas kernels for 64%

profile of v3, /device:TPU:96, one launch (start us, length us, event | category | flops | bytes accessed | tf_op | source)
XLA Modules:
  0.0 53.6 jit_solution(7357622621224359832)
XLA Ops:
  0.6 1.2 %prepare.1 = (bf16[96,1536]{1,0:T(8,128)(2,1)S(1)}, bf16[96,1536]{1,0:T(8,128)(2,1)S(1)}, bf16[32,1536]{1,0:T(8,128)(2,1)S(1)}, bf16[64,1536]{1,0:T(8,128)(2,1)S(1)}, bf16[32,1536]{1,0:T(8,128)(2,1)S(1)}) custom-call(s32[4]{0:T(128)} %fc_in.9, s32[4,32]{1,0:T(4,128)} %bitcast.11, bf16[128,1536]{1,0:T(8,128)(2,1)} %bitcast.8, bf16[64,1536]{1,0:T(8,128)(2,1)} %bitcast.10), custom_call_target="tpu_custom_call" | custom-call | flops 100000000 | bytes 1000000 | tf_op jit(solution)/shard_map/prepare/pallas_call | solution.py:548
  1.9 1.7 %collective-permute-start.2 = (bf16[64,1536]{1,0:T(8,128)(2,1)S(1)}, bf16[64,1536]{1,0:T(8,128)(2,1)S(1)}, u32[]{:S(2)}, u32[]{:S(2)}) collective-permute-start(bf16[64,1536]{1,0:T(8,128)(2,1)S(1)} %get-tuple-element.54), channel_id=1, source_target_pairs={{0,1},{1,0},{2,3},{3,2},{4,5},{5,4},{6,7},{7,6},{8,9},{9,8},{10,11... | collective-permute-start | bytes 589832 | tf_op jit(solution)/shard_map/ppermute | solution.py:530
  3.5 0.0 collective-permute-start
  3.5 2.7 %collective-permute-start.1 = (bf16[96,1536]{1,0:T(8,128)(2,1)S(1)}, bf16[96,1536]{1,0:T(8,128)(2,1)S(1)}, u32[]{:S(2)}, u32[]{:S(2)}) collective-permute-start(bf16[96,1536]{1,0:T(8,128)(2,1)S(1)} %get-tuple-element.45), channel_id=1, source_target_pairs={{0,1},{1,0},{2,3},{3,2},{4,8},{5,9},{6,10},{7,11},{8,4},{9,5},{10,... | collective-permute-start | bytes 884744 | tf_op jit(solution)/shard_map/ppermute | solution.py:525
  6.2 7.5 %project_own.1 = (bf16[128,1536]{1,0:T(8,128)(2,1)S(1)}, f32[12,128]{1,0:T(8,128)S(1)}, bf16[128,1536]{1,0:T(8,128)(2,1)S(1)}, bf16[128,1536]{1,0:T(8,128)(2,1)S...) custom-call(bf16[32,1536]{1,0:T(8,128)(2,1)S(1)} %get-tuple-element., ...), custom_call_target="tpu_custom_call" | custom-call | flops 6000000000 | bytes 1000000 | tf_op jit(solution)/shard_map/project_own/pallas_call | solution.py:548
  13.7 0.0 collective-permute-done.2.got_pair
  13.8 2.3 %collective-permute-start.3 = (bf16[32,1536]{1,0:T(8,128)(2,1)S(1)}, bf16[32,1536]{1,0:T(8,128)(2,1)S(1)}, u32[]{:S(2)}, u32[]{:S(2)}) collective-permute-start(bf16[32,1536]{1,0:T(8,128)(2,1)S(1)} %combine.1), channel_id=1, source_target_pairs={{0,3},{1,2},{2,1},{3,0},{4,7},{5,6},{6,5},{7,4},{8,11},{9,10},{10,... | collective-permute-start | bytes 294920 | tf_op jit(solution)/shard_map/ppermute | solution.py:530
  16.0 0.0 collective-permute-done.recv_a
  16.1 0.0 collective-permute-done.1.recv_b
  16.1 6.5 %attend.1 = (bf16[192,1536]{1,0:T(8,128)(2,1)S(1)}, bf16[192,1536]{1,0:T(8,128)(2,1)S(1)}, bf16[320,1536]{1,0:T(8,128)(2,1)S(1)}, bf16[320,1536]{1,0:T(8,128)(2,...) custom-call(s32[4]{0:T(128)} %fc_in.9, bf16[96,1536]{1,0:T(8,128)(2,1)S(1)} %collective-permute-done.recv_a, ...), custom_call_target="tpu_custom_call" | custom-call | flops 8000000000 | bytes 1000000 | tf_op jit(solution)/shard_map/attend/pallas_call | solution.py:548
  22.6 0.0 collective-permute-done.3.got_mate
  22.7 0.1 collective-permute-start.4
  22.7 0.9 %collective-permute-start.5 = (bf16[16,1536]{1,0:T(8,128)(2,1)S(1)}, bf16[16,1536]{1,0:T(8,128)(2,1)S(1)}, u32[]{:S(2)}, u32[]{:S(2)}) collective-permute-start(bf16[16,1536]{1,0:T(8,128)(2,1)S(1)} %get-tuple-element.58), channel_id=1, source_target_pairs={{0,1},{1,0},{2,3},{3,2},{4,8},{5,9},{6,10},{7,11},{8,4},{9,5},{10,... | collective-permute-start | bytes 147464 | tf_op jit(solution)/shard_map/ppermute | solution.py:525
  23.7 4.9 %convolve.1 = (bf16[32,1536]{1,0:T(8,128)(2,1)S(1)}, f32[12,192,128]{2,1,0:T(8,128)S(1)}, f32[12,160,128]{2,1,0:T(8,128)S(1)}, f32[12,40,128]{2,1,0:T(8,128)S(1)...) custom-call(s32[4]{0:T(128)} %fc_in.9, ...), custom_call_target="tpu_custom_call" | custom-call | flops 5000000000 | bytes 1000000 | tf_op jit(solution)/shard_map/convolve/pallas_call | solution.py:548
  28.6 0.8 %collective-permute-start.8 = (bf16[32,1536]{1,0:T(8,128)(2,1)S(1)}, bf16[32,1536]{1,0:T(8,128)(2,1)S(1)}, u32[]{:S(2)}, u32[]{:S(2)}) collective-permute-start(bf16[32,1536]{1,0:T(8,128)(2,1)S(1)} %get-tuple-element.79.l0), channel_id=1, source_target_pairs={{0,1},{1,0},{2,3},{3,2},{4,5},{5,4},{6,7},{7,6},{8,9},{9,8},{10,11... | collective-permute-start | bytes 294920 | tf_op jit(solution)/shard_map/ppermute | solution.py:530
  29.4 0.0 collective-permute-done.4.edge_a
  29.4 0.0 collective-permute-done.5.edge_b
  29.4 4.7 %convolve_back.1 = (bf16[128,1536]{1,0:T(8,128)(2,1)S(1)}, bf16[128,1536]{1,0:T(8,128)(2,1)S(1)}) custom-call(s32[4]{0:T(128)} %fc_in.9, bf16[32,1536]{1,0:T(8,128)(2,1)S(1)} %get-tuple-element.56.lat_grad, bf16[16,1536]{1,0:T(8,128)(2,1)S(1)} %collective-permute-done.4.edge_a, bf16[16,1536]{1,0:T(8,128)(2,1)S(1)} %collective-permute-done.5.edge_b, ...), custom_call_target="tpu_custom_call" | custom-call | flops 5000000000 | bytes 1000000 | tf_op jit(solution)/shard_map/convolve_back/pallas_call | solution.py:548
  34.1 6.1 %attend_back.1 = (bf16[64,1536]{1,0:T(8,128)(2,1)S(1)}, bf16[64,1536]{1,0:T(8,128)(2,1)S(1)}, bf16[128,1536]{1,0:T(8,128)(2,1)S(1)}, bf16[128,1536]{1,0:T(8,128)(2,1)S(1)}, bf16[128,1536]{1,0:T(8,128)(2,1)S(1)}) custom-call(bf16[192,1536]{1,0:T(8,128)(2,1)S(1)} %get-tuple-element.69.q_s, bf16[320,1536]{1,0:T(8,128)(2,1)S(1)} %get-tuple-element.70.k_s, ...), custom_call_target="tpu_custom_call" | custom-call | flops 6000000000 | bytes 1000000 | tf_op jit(solution)/shard_map/attend_back/pallas_call | solution.py:548
  40.2 3.0 %collective-permute-start.7 = (bf16[64,1536]{1,0:T(8,128)(2,1)S(1)}, bf16[64,1536]{1,0:T(8,128)(2,1)S(1)}, u32[]{:S(2)}, u32[]{:S(2)}) collective-permute-start(bf16[64,1536]{1,0:T(8,128)(2,1)S(1)} %get-tuple-element.78), channel_id=1, source_target_pairs={{0,1},{1,0},{2,3},{3,2},{4,8},{5,9},{6,10},{7,11},{8,4},{9,5},{10,... | collective-permute-start | bytes 589832 | tf_op jit(solution)/shard_map/ppermute | solution.py:525
  43.2 0.0 collective-permute-start.6
  43.2 0.0 collective-permute-done.8.l1
  43.2 0.8 %collective-permute-start.9 = (bf16[64,1536]{1,0:T(8,128)(2,1)S(1)}, bf16[64,1536]{1,0:T(8,128)(2,1)S(1)}, u32[]{:S(2)}, u32[]{:S(2)}) collective-permute-start(bf16[64,1536]{1,0:T(8,128)(2,1)S(1)} %pad_maximum_fusion), channel_id=1, source_target_pairs={{0,3},{1,2},{2,1},{3,0},{4,7},{5,6},{6,5},{7,4},{8,11},{9,10},{10,... | collective-permute-start | bytes 589832 | tf_op jit(solution)/shard_map/ppermute | solution.py:530
  43.9 4.5 %project_back.1.dn_s = f32[128,1536]{1,0:T(8,128)S(1)} custom-call(bf16[64,1536]{1,0:T(8,128)(2,1)S(1)} %get-tuple-element.74.after, bf16[128,1536]{1,0:T(8,128)(2,1)S(1)} %get-tuple-element.75.dq, bf16[128,1536]{1,0:T(8,128)(2,1)S(1)} %get-tuple-element.76.dk, bf16[128,1536]{1,0:T(8,128)(2,1)S(1)} %get-tuple-element.77.dv, ...), custom_call_target="tpu_custom_call" | custom-call | flops 3000000000 | bytes 1000000 | tf_op jit(solution)/shard_map/project_back/pallas_call | solution.py:548
  48.5 0.0 collective-permute-done.7.recv_b
  48.5 0.0 collective-permute-done.6.recv_a
  48.5 3.3 %collective-permute-done.9.l23 = bf16[64,1536]{1,0:T(8,128)(2,1)S(1)} collective-permute-done((bf16[64,1536]{1,0:T(8,128)(2,1)S(1)}, bf16[64,1536]{1,0:T(8,128)(2,1)S(1)}, u32[]{:S(2)}, u32[]{:S(2)}) %collective-permute-start.9) | collective-permute-done | bytes 196640 | tf_op jit(solution)/shard_map/ppermute | solution.py:530
  51.8 1.6 %finish.1 = (bf16[64,1536]{1,0:T(8,128)(2,1)}, bf16[128,1536]{1,0:T(8,128)(2,1)}) custom-call(s32[4]{0:T(128)} %fc_in.9, s32[4,32]{1,0:T(4,128)} %bitcast.12, bf16[128,1536]{1,0:T(8,128)(2,1)S(1)} %get-tuple-element.43.x_own.x_s, bf16[128,1536]{1,0:T(8,128)(2,1)S(1)} %get-tuple-element.68.dh_s, f32[128,1536]{1,0:T(8,128)S(1)} %project_back.1.dn_s, ...), custom_call_target="tpu_custom_call" | custom-call | flops 1000000000 | bytes 1000000 | tf_op jit(solution)/shard_map/finish/pallas_call | solution.py:548
  (3 shorter events, 0.1 us)
Async XLA Ops:
  1.9 11.9 %collective-permute-start.2 = (bf16[64,1536]{1,0:T(8,128)(2,1)S(1)}, bf16[64,1536]{1,0:T(8,128)(2,1)S(1)}, u32[]{:S(2)}, u32[]{:S(2)}) collective-permute-start(bf16[64,1536]{1,0:T(8,128)(2,1)S(1)} %get-tuple-element.54), channel_id=1, source_target_pairs={{0,1},{1,0},{2,3},{3,2},{4,5},{5,4},{6,7},{7,6},{8,9},{9,8},{10,11... | collective-permute-start | bytes 589832 | tf_op jit(solution)/shard_map/ppermute | solution.py:530
  3.5 12.5 %collective-permute-start = (bf16[96,1536]{1,0:T(8,128)(2,1)S(1)}, bf16[96,1536]{1,0:T(8,128)(2,1)S(1)}, u32[]{:S(2)}, u32[]{:S(2)}) collective-permute-start(bf16[96,1536]{1,0:T(8,128)(2,1)S(1)} %get-tuple-element.44), channel_id=1, source_target_pairs={{0,4},{4,0},{8,12},{12,8},{16,20},{20,16},{24,28},{28,24},{32,36},... | collective-permute-start | bytes 884744 | tf_op jit(solution)/shard_map/ppermute | solution.py:525
  3.5 12.5 %collective-permute-start.1 = (bf16[96,1536]{1,0:T(8,128)(2,1)S(1)}, bf16[96,1536]{1,0:T(8,128)(2,1)S(1)}, u32[]{:S(2)}, u32[]{:S(2)}) collective-permute-start(bf16[96,1536]{1,0:T(8,128)(2,1)S(1)} %get-tuple-element.45), channel_id=1, source_target_pairs={{0,1},{1,0},{2,3},{3,2},{4,8},{5,9},{6,10},{7,11},{8,4},{9,5},{10,... | collective-permute-start | bytes 884744 | tf_op jit(solution)/shard_map/ppermute | solution.py:525
  13.8 8.8 %collective-permute-start.3 = (bf16[32,1536]{1,0:T(8,128)(2,1)S(1)}, bf16[32,1536]{1,0:T(8,128)(2,1)S(1)}, u32[]{:S(2)}, u32[]{:S(2)}) collective-permute-start(bf16[32,1536]{1,0:T(8,128)(2,1)S(1)} %combine.1), channel_id=1, source_target_pairs={{0,3},{1,2},{2,1},{3,0},{4,7},{5,6},{6,5},{7,4},{8,11},{9,10},{10,... | collective-permute-start | bytes 294920 | tf_op jit(solution)/shard_map/ppermute | solution.py:530
  22.7 6.7 %collective-permute-start.4 = (bf16[16,1536]{1,0:T(8,128)(2,1)S(1)}, bf16[16,1536]{1,0:T(8,128)(2,1)S(1)}, u32[]{:S(2)}, u32[]{:S(2)}) collective-permute-start(bf16[16,1536]{1,0:T(8,128)(2,1)S(1)} %get-tuple-element.57), channel_id=1, source_target_pairs={{0,4},{4,0},{8,12},{12,8},{16,20},{20,16},{24,28},{28,24},{32,36},... | collective-permute-start | bytes 147464 | tf_op jit(solution)/shard_map/ppermute | solution.py:525
  22.7 6.6 %collective-permute-start.5 = (bf16[16,1536]{1,0:T(8,128)(2,1)S(1)}, bf16[16,1536]{1,0:T(8,128)(2,1)S(1)}, u32[]{:S(2)}, u32[]{:S(2)}) collective-permute-start(bf16[16,1536]{1,0:T(8,128)(2,1)S(1)} %get-tuple-element.58), channel_id=1, source_target_pairs={{0,1},{1,0},{2,3},{3,2},{4,8},{5,9},{6,10},{7,11},{8,4},{9,5},{10,... | collective-permute-start | bytes 147464 | tf_op jit(solution)/shard_map/ppermute | solution.py:525
  28.6 14.6 %collective-permute-start.8 = (bf16[32,1536]{1,0:T(8,128)(2,1)S(1)}, bf16[32,1536]{1,0:T(8,128)(2,1)S(1)}, u32[]{:S(2)}, u32[]{:S(2)}) collective-permute-start(bf16[32,1536]{1,0:T(8,128)(2,1)S(1)} %get-tuple-element.79.l0), channel_id=1, source_target_pairs={{0,1},{1,0},{2,3},{3,2},{4,5},{5,4},{6,7},{7,6},{8,9},{9,8},{10,11... | collective-permute-start | bytes 294920 | tf_op jit(solution)/shard_map/ppermute | solution.py:530
  40.2 8.3 %collective-permute-start.7 = (bf16[64,1536]{1,0:T(8,128)(2,1)S(1)}, bf16[64,1536]{1,0:T(8,128)(2,1)S(1)}, u32[]{:S(2)}, u32[]{:S(2)}) collective-permute-start(bf16[64,1536]{1,0:T(8,128)(2,1)S(1)} %get-tuple-element.78), channel_id=1, source_target_pairs={{0,1},{1,0},{2,3},{3,2},{4,8},{5,9},{6,10},{7,11},{8,4},{9,5},{10,... | collective-permute-start | bytes 589832 | tf_op jit(solution)/shard_map/ppermute | solution.py:525
  43.2 5.4 %collective-permute-start.6 = (bf16[64,1536]{1,0:T(8,128)(2,1)S(1)}, bf16[64,1536]{1,0:T(8,128)(2,1)S(1)}, u32[]{:S(2)}, u32[]{:S(2)}) collective-permute-start(bf16[64,1536]{1,0:T(8,128)(2,1)S(1)} %get-tuple-element.74.after), channel_id=1, source_target_pairs={{0,4},{4,0},{8,12},{12,8},{16,20},{20,16},{24,28},{28,24},{32,36},... | collective-permute-start | bytes 589832 | tf_op jit(solution)/shard_map/ppermute | solution.py:525
  43.2 8.6 %collective-permute-start.9 = (bf16[64,1536]{1,0:T(8,128)(2,1)S(1)}, bf16[64,1536]{1,0:T(8,128)(2,1)S(1)}, u32[]{:S(2)}, u32[]{:S(2)}) collective-permute-start(bf16[64,1536]{1,0:T(8,128)(2,1)S(1)} %pad_maximum_fusion), channel_id=1, source_target_pairs={{0,3},{1,2},{2,1},{3,0},{4,7},{5,6},{6,5},{7,4},{8,11},{9,10},{10,... | collective-permute-start | bytes 589832 | tf_op jit(solution)/shard_map/ppermute | solution.py:530

commit v4 on v3

--- a/solution.py
+++ b/solution.py
@@ -78,8 +78,12 @@
     off_a = (1 - tm % 2) * (FR - HALO)
     off_b = (FR - HALO) - off_a
     cg = pltpu.make_async_copy(grads, g_buf, sems.at[2])
-    ca = pltpu.make_async_copy(audio.at[pl.ds(pl.multiple_of(off_a, 32), HALO)], send_a, sems.at[3])
-    cb = pltpu.make_async_copy(audio.at[pl.ds(pl.multiple_of(off_b, 32), HALO)], send_b, sems.at[4])
+    ca = pltpu.make_async_copy(
+        audio.at[pl.ds(pl.multiple_of(off_a, 32), HALO)], send_a.at[pl.ds(0, HALO)], sems.at[3]
+    )
+    cb = pltpu.make_async_copy(
+        audio.at[pl.ds(pl.multiple_of(off_b, 32), HALO)], send_b.at[pl.ds(0, HALO)], sems.at[4]
+    )
     cg.start()
     ca.start()
     cb.start()
@@ -88,16 +92,28 @@
     starts, lives = routes(fc, tl, tm)
     row = lax.broadcasted_iota(jnp.int32, (LR, SLOTS), 0)
     slot = lax.broadcasted_iota(jnp.int32, (LR, SLOTS), 1) + llm * SLOTS
+    starts = [pick(starts, llm ^ j) for j in range(NREC)]
+    lives = [pick(lives, llm ^ j) for j in range(NREC)]
     picked = []
     for j in range(NREC):
-        b = llm ^ j
-        chosen = (row < pick(lives, b)) & (slot == row + pick(starts, b))
+        chosen = (row < lives[j]) & (slot == row + starts[j])
         picked.append(jnp.where(chosen, 1.0, 0.0).astype(BF))
+    place = lax.broadcasted_iota(jnp.int32, (16, SLOTS), 0)
+    slot = lax.broadcasted_iota(jnp.int32, (16, SLOTS), 1) + llm * SLOTS
+    for offset in ((1 - tm % 2) * (LR - 4), (tm % 2) * (LR - 4)):
+        r = place % 4 + offset
+        chosen = jnp.zeros((16, SLOTS), F32)
+        for j in range(NREC):
+            hit = (place // 4 == (j + 3) % 4) & (r < lives[j]) & (slot == r + starts[j])
+            chosen = jnp.where(hit, 1.0, chosen)
+        picked.append(chosen.astype(BF))
     cg.wait()
     moved = dot(jnp.concatenate(picked, axis=0), g_buf[...]).astype(BF)
     own[...] = moved[:LR]
     pair[...] = moved[LR : 3 * LR]
-    mate[...] = moved[3 * LR :]
+    mate[...] = moved[3 * LR : 4 * LR]
+    send_a[HALO:, :] = moved[4 * LR : 4 * LR + 16]
+    send_b[HALO:, :] = moved[4 * LR + 16 :]
     ca.wait()
     cb.wait()
 
@@ -110,54 +126,46 @@
 
 
 def project_own(
-    after, audio, gains_in, w_key, w_value, w_query, w_out,
-    x_o, gain_o, k_o, v_o, q_o, wk_o, wv_o, wq_o, wo_o, n_s, w_sems, sems,
+    after, audio, gains_in, w_key, w_value, x_o, gain_o, n_s, k_o, v_o, wk_o, wv_o, wkt_o, wvt_o, sems
 ):
     cx = pltpu.make_async_copy(audio, x_o, sems.at[0])
     cg = pltpu.make_async_copy(gains_in, gain_o, sems.at[1])
-    cx.start()
-    cg.start()
-
-    def w_copy(n, j):
-        src = (w_key, w_value, w_query, w_out)[n]
-        dst = (wk_o, wv_o, wq_o, wo_o)[n]
-        return pltpu.make_async_copy(src.at[:, lanes(j, COL)], dst.at[:, lanes(j, COL)], w_sems.at[n, j])
-
-    for n in range(4):
-        for j in range(NC):
-            w_copy(n, j).start()
+    loads = [
+        pltpu.make_async_copy(w_key, wk_o, sems.at[2]),
+        pltpu.make_async_copy(w_value, wv_o, sems.at[3]),
+    ]
+    for copy in [cx, cg] + loads:
+        copy.start()
     cx.wait()
     cg.wait()
     for r in range(2):
         rows = slice(r * 64, r * 64 + 64)
         norm_rows(x_o[rows, :].astype(F32), gain_o, n_s, rows)
-    for n, (w_s, out_s) in enumerate(((wk_o, k_o), (wv_o, v_o), (wq_o, q_o))):
-        for j in range(NC):
-            w_copy(n, j).wait()
-            cols = slice(j * COL, (j + 1) * COL)
-            out_s[:, cols] = dot(n_s[...], w_s[:, cols]).astype(BF)
-    for j in range(NC):
-        w_copy(3, j).wait()
-
-
-def combine(after, mate, got_pair, out):
-    out[...] = mate[...] + got_pair[LR:, :]
-
-
-def split_edges(after, own, got_pair, got_mate, grad_o, send_a, send_b):
-    grads = own[...] + got_pair[:LR, :] + got_mate[...]
-    grad_o[...] = grads
-    even = lax.axis_index("tm") % 2 == 0
-
-    @pl.when(even)
-    def _():
-        send_a[...] = grads[16:]
-        send_b[...] = grads[:16]
-
-    @pl.when(jnp.logical_not(even))
-    def _():
-        send_a[...] = grads[:16]
-        send_b[...] = grads[16:]
+    for load, w_s, wt_s, out_s in zip(loads, (wk_o, wv_o), (wkt_o, wvt_o), (k_o, v_o)):
+        load.wait()
+        out_s[...] = dot(n_s[...], w_s[...]).astype(BF)
+        wt_s[...] = w_s[...].T
+
+
+def halves(first, second, lo):
+    pair = [part.astype(F32)[lo : lo + 8] for part in (first, second)]
+    return jnp.concatenate(pair, axis=0).astype(BF)
+
+
+def stack_pair(after, pair, recv_a, recv_b, out):
+    out[: 2 * LR, :] = pair[...]
+    out[2 * LR :, :] = halves(recv_a[HALO:, :], recv_b[HALO:, :], 0)
+
+
+def stack_mate(after, mate, got_pair, recv_a, recv_b, out):
+    out[:LR, :] = mate[...] + got_pair[LR : 2 * LR, :]
+    out[LR : LR + 16, :] = halves(recv_a[HALO:, :], recv_b[HALO:, :], 8)
+    out[LR + 16 :, :] = got_pair[2 * LR :, :]
+
+
+def stack_latents(after, first, second, out):
+    out[:LR, :] = first[...]
+    out[LR:, :] = second[...]
 
 
 def head_mask(j, lo, hi):
@@ -166,7 +174,8 @@
 
 
 def window(g, lo, hi):
-    return pl.ds(pl.multiple_of(g * GROUP + lo * LANE, LANE), (hi - lo) * LANE)
+    start = g * GROUP + lo * LANE
+    return pl.ds(start if isinstance(start, int) else pl.multiple_of(start, LANE), (hi - lo) * LANE)
 
 
 def add_tiles(tiles, lo, value):
@@ -176,11 +185,15 @@
 
 
 def attend(
-    fc_in, recv_a, recv_b, x_own, gains, k_own, v_own, q_own, wk_s, wv_s, wq_s,
-    xq_o, q_s, k_s, v_s, p_s, att_s, fc, n_s, bias_s, sems,
+    fc_in, w_query, w_out, recv_a, recv_b, x_own, n_own, gains, k_own, v_own, wk_s, wv_s,
+    xq_o, q_s, k_s, v_s, p_s, att_s, wq_s, wo_s, fc, n_s, bias_s, sems,
 ):
     fc_copy = pltpu.make_async_copy(fc_in, fc, sems.at[0])
     fc_copy.start()
+    load_q = pltpu.make_async_copy(w_query, wq_s, sems.at[1])
+    load_q.start()
+    load_o = pltpu.make_async_copy(w_out, wo_s, sems.at[2])
+    load_o.start()
     tm = lax.axis_index("tm")
     llm = lax.axis_index("llm")
     even = tm % 2 == 0
@@ -189,22 +202,21 @@
 
     @pl.when(even)
     def _():
-        norm_rows(recv_b[...].astype(F32), gains, n_s, slice(0, HALO))
-        norm_rows(recv_a[...].astype(F32), gains, n_s, slice(HALO, 2 * HALO))
+        norm_rows(recv_b[:HALO, :].astype(F32), gains, n_s, slice(0, HALO))
+        norm_rows(recv_a[:HALO, :].astype(F32), gains, n_s, slice(HALO, 2 * HALO))
         xq_o[0:32, :] = recv_b[64:96, :]
         xq_o[160:192, :] = recv_a[0:32, :]
 
     @pl.when(jnp.logical_not(even))
     def _():
-        norm_rows(recv_a[...].astype(F32), gains, n_s, slice(0, HALO))
-        norm_rows(recv_b[...].astype(F32), gains, n_s, slice(HALO, 2 * HALO))
+        norm_rows(recv_a[:HALO, :].astype(F32), gains, n_s, slice(0, HALO))
+        norm_rows(recv_b[:HALO, :].astype(F32), gains, n_s, slice(HALO, 2 * HALO))
         xq_o[0:32, :] = recv_a[64:96, :]
         xq_o[160:192, :] = recv_b[0:32, :]
 
     xq_o[32:160, :] = x_own[...]
     k_s[96:224, :] = k_own[...]
     v_s[96:224, :] = v_own[...]
-    q_s[32:160, :] = q_own[...]
     for w_s, out_s in ((wk_s, k_s), (wv_s, v_s)):
         @pl.loop(0, NC)
         def _(j, w_s=w_s, out_s=out_s):
@@ -213,12 +225,9 @@
             out_s[0:96, cols] = new[0:96]
             out_s[224:320, cols] = new[96:192]
 
-    @pl.loop(0, NC)
-    def _(j):
-        cols = lanes(j, COL)
-        new = dot(n_s[64:128, :], wq_s[:, cols]).astype(BF)
-        q_s[0:32, cols] = new[0:32]
-        q_s[160:192, cols] = new[32:64]
+    queried = jnp.concatenate([n_s[64:96, :], n_own[...], n_s[96:128, :]], axis=0)
+    load_q.wait()
+    q_s[...] = dot(queried, wq_s[...]).astype(BF)
 
     fc_copy.wait()
     limit = fc[llm]
@@ -265,6 +274,8 @@
             att_s[32:160, at] = parts[1][t].astype(BF)
             att_s[160:192, at] = parts[2][t].astype(BF)
 
+    load_o.wait()
+
 
 def spoken_rows(fc, tm, llm):
     frame = lax.broadcasted_iota(jnp.int32, (QR, 1), 0) + (tm * FR - 32)
@@ -273,7 +284,7 @@
 
 def convolve(
     fc_in, xq, att_s, wo_s, cg_in, lg_in, taps_in,
-    lat_o, h_s, dsilu_s, pool_s, inv_o, cg_s, lg_s, tap_s, fc, ci_s, up_s, norm_t, sems,
+    lat_o, h_s, dsilu_s, pool_s, inv_o, cg_s, lg_s, tap_s, wot_s, fc, ci_s, up_s, norm_t, sems,
 ):
     copies = [
         pltpu.make_async_copy(source, into, sems.at[i])
@@ -303,18 +314,21 @@
 
     def conv_step(c, squares):
         cols = lanes(c)
+        wot_s[cols, :] = wo_s[:, cols].T
         ci_s[...] = (h_s[c] * inv_spoken * cg_s[pl.ds(c, 1), :]).astype(BF).astype(F32)
         kern = tap_s[:, cols]
-        acc = jnp.zeros((SR, LANE), F32)
-        for s in range(8):
-            xs = ci_s[s : s + SR + 24, :]
-            for u in range(4):
-                m = s + 8 * u
-                acc = acc + kern[m : m + 1, :] * xs[8 * u : 8 * u + SR]
-        sig = 1.0 / (1.0 + jnp.exp(-acc))
-        silu = acc * sig
-        dsilu_s[c] = sig + silu * (1.0 - sig)
-        up_s[...] = h_s[c, 16 : 16 + SR, :] + silu
+        part = SR // 4
+        for at in range(0, SR, part):
+            acc = jnp.zeros((part, LANE), F32)
+            for s in range(8):
+                xs = ci_s[at + s : at + s + part + 24, :]
+                for u in range(4):
+                    m = s + 8 * u
+                    acc = acc + kern[m : m + 1, :] * xs[8 * u : 8 * u + part]
+            sig = 0.5 * jnp.tanh(0.5 * acc) + 0.5
+            silu = acc * sig
+            dsilu_s[c, at : at + part, :] = sig + silu * (1.0 - sig)
+            up_s[at : at + part, :] = h_s[c, 16 + at : 16 + at + part, :] + silu
         pooled = up_s[pl.ds(0, PR, 4), :]
         for u in range(1, 4):
             pooled = pooled + up_s[pl.ds(u, PR, 4), :]
@@ -330,7 +344,7 @@
 
 
 def convolve_back(
-    fc_in, lat_grad, edge_a, edge_b, h_s, dsilu_s, pool_s, inv_s, cg_s, lg_s, tap_s, wo_s,
+    fc_in, own, got_pair, got_mate, recv_a, recv_b, h_s, dsilu_s, pool_s, inv_s, cg_s, lg_s, tap_s, wot_s,
     dhid_s, datt_s, fc, g_s, up_s, ds_s, us_s, dnc_s, sems,
 ):
     copy = pltpu.make_async_copy(fc_in, fc, sems.at[0])
@@ -339,18 +353,27 @@
     llm = lax.axis_index("llm")
     even = tm % 2 == 0
 
-    row = lax.broadcasted_iota(jnp.int32, (PR, 64), 0)
-    col = lax.broadcasted_iota(jnp.int32, (PR, 64), 1)
+    row = lax.broadcasted_iota(jnp.int32, (PR, LR + 80), 0)
+    col = lax.broadcasted_iota(jnp.int32, (PR, LR + 80), 1)
+    is_left = row < 4
+    is_right = row >= PR - 4
+    r = jnp.where(is_left, row, row - (PR - 4))
+    label = jnp.where(is_left, 1 - tm % 2, tm % 2)
+    side = (
+        (col == 44 + 16 * label + r) | (col == 64 + 8 * label + r)
+        | (col == 80 + 8 * label + r) | (col == 100 + 8 * label + r)
+    ) & (is_left | is_right)
+    middle = (col < LR) & (col == row - 4)
     at = tm * LR + row - 4
-    chosen = (col == row + 12) & (at >= 0) & (at < lax.axis_size("tm") * LR)
+    chosen = (side | middle) & (at >= 0) & (at < lax.axis_size("tm") * LR)
     chosen = jnp.where(chosen, 1.0, 0.0).astype(BF)
-    left = jnp.where(even, 0.0, 1.0).astype(BF)
-    right = jnp.where(even, 1.0, 0.0).astype(BF)
     stacked = jnp.concatenate(
         [
-            edge_a[...] * left + edge_b[...] * right,
-            lat_grad[...],
-            edge_a[...] * right + edge_b[...] * left,
+            own[...] + got_pair[:LR, :] + got_mate[:LR, :],
+            recv_a[HALO:, :],
+            recv_b[HALO:, :],
+            got_pair[2 * LR :, :],
+            got_mate[LR:, :],
         ],
         axis=0,
     )
@@ -378,16 +401,20 @@
         ds_s[...] = up_s[...] * dsilu_s[c]
         us_s[c] = up_s[16 : 16 + FR, :]
         kern = tap_s[:, cols]
-        acc = jnp.zeros((FR, LANE), F32)
-        for s in range(8):
-            base = 8 if s == 0 else s
-            xs = ds_s[base : base + FR + 24, :]
-            for u in range(4):
-                m = 32 - base - 8 * u
-                acc = acc + kern[m : m + 1, :] * xs[8 * u : 8 * u + FR]
-        dn = acc.astype(BF).astype(F32) * spoken_own * cg_s[pl.ds(c, 1), :]
-        dnc_s[c] = dn
-        return along + dn * h_s[c, 32:160, :]
+        part = FR // 4
+        sums = []
+        for at in range(0, FR, part):
+            acc = jnp.zeros((part, LANE), F32)
+            for s in range(8):
+                base = 8 if s == 0 else s
+                xs = ds_s[at + base : at + base + part + 24, :]
+                for u in range(4):
+                    m = 32 - base - 8 * u
+                    acc = acc + kern[m : m + 1, :] * xs[8 * u : 8 * u + part]
+            dn = acc.astype(BF).astype(F32) * spoken_own[at : at + part] * cg_s[pl.ds(c, 1), :]
+            dnc_s[c, at : at + part, :] = dn
+            sums.append(along[at : at + part] + dn * h_s[c, 32 + at : 32 + at + part, :])
+        return jnp.concatenate(sums, axis=0)
 
     along = lax.fori_loop(0, NB, conv_back, jnp.zeros((FR, LANE), F32))
     back_h = inv_own * inv_own * inv_own * (jnp.sum(along, axis=-1, keepdims=True) * (1.0 / D))
@@ -398,10 +425,10 @@
 
     @pl.loop(0, NC)
     def _(j):
-        datt_s[:, lanes(j, COL)] = dot_t(dhid_s[...], wo_s[lanes(j, COL), :]).astype(BF)
-
-
-def attend_back(q_s, k_s, v_s, p_s, datt_s, wk_s, wv_s, send_a, send_b, dq_s, dk_s, dv_s, ek_s, ev_s):
+        datt_s[:, lanes(j, COL)] = dot(dhid_s[...], wot_s[:, lanes(j, COL)]).astype(BF)
+
+
+def attend_back(after, q_s, v_s, p_s, datt_s, wkt_s, wvt_s, send_a, send_b, ds_o, dk_s, dv_s, ek_s, ev_s):
     @pl.loop(0, 4)
     def _(g):
         heads = []
@@ -412,16 +439,15 @@
         heads = [w * dp for w, dp in zip(weights, heads)]
         sums = [jnp.sum(pd, axis=-1, keepdims=True) for pd in heads]
         heads = [((pd - w * total) * SCALE).astype(BF) for pd, w, total in zip(heads, weights, sums)]
-        dq, dk, dv = [None] * 3, [None] * 3, [None] * 3
+        dk, dv = [None] * 3, [None] * 3
         for j, (lo, hi) in enumerate(WINDOWS):
             win = window(g, lo, hi)
             mask = head_mask(j, lo, hi)
-            add_tiles(dq, lo, dot(heads[j], k_s[32:288, win] * mask))
+            ds_o[g * 4 + j] = heads[j]
             add_tiles(dk, lo, t_dot(heads[j], q_s[32:160, win] * mask))
             add_tiles(dv, lo, t_dot(p_s[g * 4 + j], datt_s[:, win] * mask))
         for t in range(3):
             at = window(g, t, t + 1)
-            dq_s[:, at] = dq[t].astype(BF)
             for out, edge, tiles in ((dk_s, ek_s, dk), (dv_s, ev_s, dv)):
                 new = tiles[t].astype(BF)
                 edge[0:64, at] = new[0:64]
@@ -433,7 +459,7 @@
     @pl.loop(0, NC)
     def _(j):
         cols = lanes(j, COL)
-        both = (dot_t(ek_s[...], wk_s[cols, :]) + dot_t(ev_s[...], wv_s[cols, :])).astype(BF)
+        both = (dot(ek_s[...], wkt_s[:, cols]) + dot(ev_s[...], wvt_s[:, cols])).astype(BF)
 
         @pl.when(even)
         def _():
@@ -446,13 +472,14 @@
             send_b[:, cols] = both[64:128]
 
 
-def project_back(after, dq, dk, dv, wq_s, wk_s, wv_s, dn_o):
-    @pl.loop(0, NC)
-    def _(j):
-        cols = lanes(j, COL)
-        dn_o[:, cols] = (
-            dot_t(dk[...], wk_s[cols, :]) + dot_t(dv[...], wv_s[cols, :]) + dot_t(dq[...], wq_s[cols, :])
-        )
+def project_back(after, ds_s, k_s, dk, dv, wq_s, wkt_s, wvt_s, dn_o, dq_s):
+    for g in range(4):
+        dq = [None] * 3
+        for j, (lo, hi) in enumerate(WINDOWS):
+            add_tiles(dq, lo, dot(ds_s[g * 4 + j], k_s[32:288, window(g, lo, hi)] * head_mask(j, lo, hi)))
+        for t in range(3):
+            dq_s[:, window(g, t, t + 1)] = dq[t].astype(BF)
+    dn_o[...] = dot(dk[...], wkt_s[...]) + dot(dv[...], wvt_s[...]) + dot_t(dq_s[...], wq_s[...])
 
 
 def finish(
@@ -584,38 +611,36 @@
     send_a, send_b, own, pair, mate = call(
         prepare,
         mark("h", frame_counts, tl_in, signal, llm_grads[0]),
-        [rows(HALO), rows(HALO), rows(LR), rows(2 * LR), rows(LR)],
+        [rows(HALO + 16), rows(HALO + 16), rows(LR), rows(2 * LR), rows(LR)],
         [fc, tl, V((SLOTS, D), BF), sems(5)],
         100_000_000,
     )
-    got_pair = trade(pair, 1)
     recv_a, recv_b = swap(n_tm, send_a, send_b)
-    x, gains, k_own, v_own, q_own, wk, wv, wq, wo = call(
+    x, gains, normed, k_own, v_own, wk, wv, wkt, wvt = call(
         project_own,
-        mark("v", own) + mark("h", signal, norm_row, w_key, w_value, w_query, w_out),
+        mark("v", own) + mark("h", signal, norm_row, w_key, w_value),
         [rows(FR), gain, rows(FR), rows(FR), rows(FR), weight, weight, weight, weight],
-        [V((FR, D), BF), sems(4, NC), sems(2)],
+        [sems(4)],
         6_000_000_000,
     )
-    (both,) = call(combine, mark("v", gains, mate, got_pair), [rows(LR)], [], 1_000_000)
-    got_mate = trade(both, 3)
-    xq, q, k, v, p, att = call(
+    (pairs,) = call(stack_pair, mark("v", gains, pair, recv_a, recv_b), [rows(2 * LR + 16)], [], 1_000_000)
+    got_pair = trade(pairs, 1)
+    xq, q, k, v, p, att, wq, wo = call(
         attend,
-        mark("h", frame_counts) + mark("v", recv_a, recv_b, x, gains, k_own, v_own, q_own, wk, wv, wq),
-        [rows(QR), rows(QR), rows(EXT), rows(EXT), ((16, FR, 256), BF), rows(QR)],
-        [fc, V((2 * HALO, D), BF), V((QR, 256), F32), sems(1)],
+        mark("h", frame_counts, w_query, w_out)
+        + mark("v", recv_a, recv_b, x, normed, gains, k_own, v_own, wk, wv),
+        [rows(QR), rows(QR), rows(EXT), rows(EXT), ((16, FR, 256), BF), rows(QR), weight, weight],
+        [fc, V((2 * HALO, D), BF), V((QR, 256), F32), sems(3)],
         8_000_000_000,
     )
-    lat_grad, first_a, first_b = call(
-        split_edges, mark("v", xq, own, got_pair, got_mate), [rows(LR), rows(16), rows(16)], [], 1_000_000
-    )
-    edge_a, edge_b = swap(n_tm, first_a, first_b)
-    latent, h, dsilu, pool, inv, cgain, lgain, taps = call(
+    (mates,) = call(stack_mate, mark("v", xq, mate, got_pair, recv_a, recv_b), [rows(LR + 32)], [], 1_000_000)
+    got_mate = trade(mates, 3)
+    latent, h, dsilu, pool, inv, cgain, lgain, taps, wot = call(
         convolve,
         mark("h", frame_counts) + mark("v", xq, att, wo) + mark("h", conv_row, latent_row, conv_kernel),
         [
             rows(LR), ((NB, QR, LANE), F32), ((NB, SR, LANE), F32), ((NB, PR, LANE), F32), ((QR, LANE), F32),
-            gain, gain, rows(KERN, F32),
+            gain, gain, rows(KERN, F32), weight,
         ],
         [fc, V((QR, LANE), F32), V((SR, LANE), F32), V((PR, LANE), F32), sems(4)],
         5_000_000_000,
@@ -624,7 +649,7 @@
     dhid, datt = call(
         convolve_back,
         mark("h", frame_counts)
-        + mark("v", lat_grad, edge_a, edge_b, h, dsilu, pool, inv, cgain, lgain, taps, wo),
+        + mark("v", own, got_pair, got_mate, recv_a, recv_b, h, dsilu, pool, inv, cgain, lgain, taps, wot),
         [rows(FR), rows(FR)],
         [
             fc, V((PR, D), F32), V((SR, LANE), F32), V((SR, LANE), F32), V((NB, FR, LANE), F32),
@@ -632,20 +657,21 @@
         ],
         5_000_000_000,
     )
-    latent_23 = trade(jnp.concatenate([latent, latent_1], axis=0), 3)
-    back_a, back_b, dq, dk, dv = call(
+    (latents,) = call(stack_latents, mark("v", dhid, latent, latent_1), [rows(2 * LR)], [], 1_000_000)
+    latent_23 = trade(latents, 3)
+    back_a, back_b, ds, dk, dv = call(
         attend_back,
-        mark("v", q, k, v, p, datt, wk, wv),
-        [rows(64), rows(64), rows(FR), rows(FR), rows(FR)],
+        mark("v", latents, q, v, p, datt, wkt, wvt),
+        [rows(64), rows(64), ((16, FR, 256), BF), rows(FR), rows(FR)],
         [V((FR, D), BF), V((FR, D), BF)],
         6_000_000_000,
     )
     ret_a, ret_b = swap(n_tm, back_a, back_b)
     (dn,) = call(
         project_back,
-        mark("v", back_a, dq, dk, dv, wq, wk, wv),
+        mark("v", back_a, ds, k, dk, dv, wq, wkt, wvt),
         [rows(FR, F32)],
-        [],
+        [V((FR, D), BF)],
         3_000_000_000,
     )
     out_rows, grad = call(

time: 53.8 us -> 46.6 us (0.87)
  the two profiles are of different devices: /device:TPU:96 before, /device:TPU:39 now
where the time goes in v4:
time: 46.6 us; the launch traced here: 46 us
  Pallas kernels  31.5 us (68%)
  starting transfers between devices  9.85 us (21%)
  waiting for transfers between devices  3.73 us (8%)
  between operations  0.9 us (2%)
    pallas_call x11, Pallas kernels, call(): pl.pallas_call(kernel, out_shape=shapes, in_specs=[spec[kind] for kind, _...  31.5 us
    ppermute x4, starting transfers between devices, trade(): return lax.ppermute(cells, 'llm', [(i, i ^ apart) for i in range(n)])  4.86 us
    ppermute x2, starting transfers between devices, swap(): lax.ppermute(cells_b, ('tm', 'llm'), full_b)  4.16 us
    ppermute x2, waiting for transfers between devices, swap(): lax.ppermute(cells_b, ('tm', 'llm'), full_b)  3.72 us
  transfers between devices with their start and end apart: 8, of which 2 were waited for; matrix products, arithmetic and copies ran while one was open for 0% of the time, Pallas kernels for 62%

profile of v4, /device:TPU:39, one launch (start us, length us, event | category | flops | bytes accessed | tf_op | source)
XLA Modules:
  0.0 46.0 jit_solution(9858815683396131582)
XLA Ops:
  0.6 1.2 %prepare.1 = (bf16[112,1536]{1,0:T(8,128)(2,1)S(1)}, bf16[112,1536]{1,0:T(8,128)(2,1)S(1)}, bf16[32,1536]{1,0:T(8,128)(2,1)S(1)}, bf16[64,1536]{1,0:T(8,128)(2,1)S(1)}, bf16[32,1536]{1,0:T(8,128)(2,1)S(1)}) custom-call(s32[4]{0:T(128)} %fc_in.9, s32[4,32]{1,0:T(4,128)} %bitcast.11, bf16[128,1536]{1,0:T(8,128)(2,1)} %bitcast.8, bf16[64,1536]{1,0:T(8,128)(2,1)} %bitcast.10), custom_call_target="tpu_custom_call" | custom-call | flops 100000000 | bytes 1000000 | tf_op jit(solution)/shard_map/prepare/pallas_call | solution.py:575
  1.9 0.8 %collective-permute-start = (bf16[112,1536]{1,0:T(8,128)(2,1)S(1)}, bf16[112,1536]{1,0:T(8,128)(2,1)S(1)}, u32[]{:S(2)}, u32[]{:S(2)}) collective-permute-start(bf16[112,1536]{1,0:T(8,128)(2,1)S(1)} %get-tuple-element.46), channel_id=1, source_target_pairs={{0,4},{4,0},{8,12},{12,8},{16,20},{20,16},{24,28},{28,24},{32,36},... | collective-permute-start | bytes 1032200 | tf_op jit(solution)/shard_map/ppermute | solution.py:552
  2.6 1.5 %collective-permute-start.1 = (bf16[112,1536]{1,0:T(8,128)(2,1)S(1)}, bf16[112,1536]{1,0:T(8,128)(2,1)S(1)}, u32[]{:S(2)}, u32[]{:S(2)}) collective-permute-start(bf16[112,1536]{1,0:T(8,128)(2,1)S(1)} %get-tuple-element.47), channel_id=1, source_target_pairs={{0,1},{1,0},{2,3},{3,2},{4,8},{5,9},{6,10},{7,11},{8,4},{9,5},{10,... | collective-permute-start | bytes 1032200 | tf_op jit(solution)/shard_map/ppermute | solution.py:552
  4.2 5.2 %project_own.1 = (bf16[128,1536]{1,0:T(8,128)(2,1)S(1)}, f32[12,128]{1,0:T(8,128)S(1)}, bf16[128,1536]{1,0:T(8,128)(2,1)S(1)}, bf16[128,1536]{1,0:T(8,128)(2,1)S...) custom-call(bf16[32,1536]{1,0:T(8,128)(2,1)S(1)} %get-tuple-element., ...), custom_call_target="tpu_custom_call" | custom-call | flops 6000000000 | bytes 1000000 | tf_op jit(solution)/shard_map/project_own/pallas_call | solution.py:575
  9.4 0.0 collective-permute-done.recv_a
  9.4 2.0 %collective-permute-done.1.recv_b = bf16[112,1536]{1,0:T(8,128)(2,1)S(1)} collective-permute-done((bf16[112,1536]{1,0:T(8,128)(2,1)S(1)}, bf16[112,1536]{1,0:T(8,128)(2,1)S(1)}, u32[]{:S(2)}, u32[]{:S(2)}) %collective-permute-start.1) | collective-permute-done | bytes 344096 | tf_op jit(solution)/shard_map/ppermute | solution.py:552
  11.4 1.4 %collective-permute-start.2 = (bf16[80,1536]{1,0:T(8,128)(2,1)S(1)}, bf16[80,1536]{1,0:T(8,128)(2,1)S(1)}, u32[]{:S(2)}, u32[]{:S(2)}) collective-permute-start(bf16[80,1536]{1,0:T(8,128)(2,1)S(1)} %stack_pair.1), channel_id=1, source_target_pairs={{0,1},{1,0},{2,3},{3,2},{4,5},{5,4},{6,7},{7,6},{8,9},{9,8},{10,11... | collective-permute-start | bytes 737288 | tf_op jit(solution)/shard_map/ppermute | solution.py:557
  12.8 6.8 %attend.1 = (bf16[192,1536]{1,0:T(8,128)(2,1)S(1)}, bf16[192,1536]{1,0:T(8,128)(2,1)S(1)}, bf16[320,1536]{1,0:T(8,128)(2,1)S(1)}, bf16[320,1536]{1,0:T(8,128)(2,...) custom-call(s32[4]{0:T(128)} %fc_in.9, ...), custom_call_target="tpu_custom_call" | custom-call | flops 8000000000 | bytes 1000000 | tf_op jit(solution)/shard_map/attend/pallas_call | solution.py:575
  19.7 0.0 collective-permute-done.2.got_pair
  19.7 2.0 %collective-permute-start.3 = (bf16[64,1536]{1,0:T(8,128)(2,1)S(1)}, bf16[64,1536]{1,0:T(8,128)(2,1)S(1)}, u32[]{:S(2)}, u32[]{:S(2)}) collective-permute-start(bf16[64,1536]{1,0:T(8,128)(2,1)S(1)} %stack_mate.1), channel_id=1, source_target_pairs={{0,3},{1,2},{2,1},{3,0},{4,7},{5,6},{6,5},{7,4},{8,11},{9,10},{10,... | collective-permute-start | bytes 589832 | tf_op jit(solution)/shard_map/ppermute | solution.py:557
  21.7 5.3 %convolve.1 = (bf16[32,1536]{1,0:T(8,128)(2,1)S(1)}, f32[12,192,128]{2,1,0:T(8,128)S(1)}, f32[12,160,128]{2,1,0:T(8,128)S(1)}, f32[12,40,128]{2,1,0:T(8,128)S(1)...) custom-call(s32[4]{0:T(128)} %fc_in.9, ...), custom_call_target="tpu_custom_call" | custom-call | flops 5000000000 | bytes 1000000 | tf_op jit(solution)/shard_map/convolve/pallas_call | solution.py:575
  27.0 0.5 %collective-permute-start.4 = (bf16[32,1536]{1,0:T(8,128)(2,1)S(1)}, bf16[32,1536]{1,0:T(8,128)(2,1)S(1)}, u32[]{:S(2)}, u32[]{:S(2)}) collective-permute-start(bf16[32,1536]{1,0:T(8,128)(2,1)S(1)} %get-tuple-element.66.first.l0), channel_id=1, source_target_pairs={{0,1},{1,0},{2,3},{3,2},{4,5},{5,4},{6,7},{7,6},{8,9},{9,8},{10,11... | collective-permute-start | bytes 294920 | tf_op jit(solution)/shard_map/ppermute | solution.py:557
  27.5 0.0 collective-permute-done.3.got_mate
  27.5 4.0 %convolve_back.1 = (bf16[128,1536]{1,0:T(8,128)(2,1)S(1)}, bf16[128,1536]{1,0:T(8,128)(2,1)S(1)}) custom-call(s32[4]{0:T(128)} %fc_in.9, bf16[32,1536]{1,0:T(8,128)(2,1)S(1)} %get-tuple-element.42.after.own, bf16[80,1536]{1,0:T(8,128)(2,1)S(1)} %collective-permute-done.2.got_pair, bf16[64,1536]{1,0:T(8,128)(2,1)S(1)} %collective-permute-done.3.got_mate, ...), custom_call_target="tpu_custom_call" | custom-call | flops 5000000000 | bytes 1000000 | tf_op jit(solution)/shard_map/convolve_back/pallas_call | solution.py:575
  31.5 0.0 collective-permute-done.4.second.l1
  31.6 1.0 %collective-permute-start.7 = (bf16[64,1536]{1,0:T(8,128)(2,1)S(1)}, bf16[64,1536]{1,0:T(8,128)(2,1)S(1)}, u32[]{:S(2)}, u32[]{:S(2)}) collective-permute-start(bf16[64,1536]{1,0:T(8,128)(2,1)S(1)} %stack_latents.1.after), channel_id=1, source_target_pairs={{0,3},{1,2},{2,1},{3,0},{4,7},{5,6},{6,5},{7,4},{8,11},{9,10},{10,... | collective-permute-start | bytes 589832 | tf_op jit(solution)/shard_map/ppermute | solution.py:557
  32.6 4.2 %attend_back.1 = (bf16[64,1536]{1,0:T(8,128)(2,1)S(1)}, bf16[64,1536]{1,0:T(8,128)(2,1)S(1)}, bf16[16,128,256]{2,1,0:T(8,128)(2,1)S(1)}, bf16[128,1536]{1,0:T(8,128)(2,1)S(1)}, bf16[128,1536]{1,0:T(8,128)(2,1)S(1)}) custom-call(bf16[64,1536]{1,0:T(8,128)(2,1)S(1)} %stack_latents.1.after, bf16[192,1536]{1,0:T(8,128)(2,1)S(1)} %get-tuple-element.67.q_s, ...), custom_call_target="tpu_custom_call" | custom-call | flops 6000000000 | bytes 1000000 | tf_op jit(solution)/shard_map/attend_back/pallas_call | solution.py:575
  36.8 0.1 collective-permute-start.5
  36.9 2.6 %collective-permute-start.6 = (bf16[64,1536]{1,0:T(8,128)(2,1)S(1)}, bf16[64,1536]{1,0:T(8,128)(2,1)S(1)}, u32[]{:S(2)}, u32[]{:S(2)}) collective-permute-start(bf16[64,1536]{1,0:T(8,128)(2,1)S(1)} %get-tuple-element.79), channel_id=1, source_target_pairs={{0,1},{1,0},{2,3},{3,2},{4,8},{5,9},{6,10},{7,11},{8,4},{9,5},{10,... | collective-permute-start | bytes 589832 | tf_op jit(solution)/shard_map/ppermute | solution.py:552
  39.5 2.9 %project_back.1.dn_s = f32[128,1536]{1,0:T(8,128)S(1)} custom-call(bf16[64,1536]{1,0:T(8,128)(2,1)S(1)} %get-tuple-element.73.after, bf16[16,128,256]{2,1,0:T(8,128)(2,1)S(1)} %get-tuple-element.74.ds_s, bf16[320,1536]{1,0:T(8,128)(2,1)S(1)} %get-tuple-element.75.k_s, bf16[128,1536]{1,0:T(8,128)(2,1)S(1)} %get-tuple-element.76.dk, ...), custom_call_target="tpu_custom_call" | custom-call | flops 3000000000 | bytes 1000000 | tf_op jit(solution)/shard_map/project_back/pallas_call | solution.py:575
  42.5 0.0 collective-permute-done.5.recv_a
  42.5 1.7 %collective-permute-done.6.recv_b = bf16[64,1536]{1,0:T(8,128)(2,1)S(1)} collective-permute-done((bf16[64,1536]{1,0:T(8,128)(2,1)S(1)}, bf16[64,1536]{1,0:T(8,128)(2,1)S(1)}, u32[]{:S(2)}, u32[]{:S(2)}) %collective-permute-start.6) | collective-permute-done | bytes 196640 | tf_op jit(solution)/shard_map/ppermute | solution.py:552
  44.2 0.0 collective-permute-done.7.l23
  44.2 1.6 %finish.1 = (bf16[64,1536]{1,0:T(8,128)(2,1)}, bf16[128,1536]{1,0:T(8,128)(2,1)}) custom-call(s32[4]{0:T(128)} %fc_in.9, s32[4,32]{1,0:T(4,128)} %bitcast.12, bf16[128,1536]{1,0:T(8,128)(2,1)S(1)} %get-tuple-element.43.x_own.x_s, bf16[128,1536]{1,0:T(8,128)(2,1)S(1)} %get-tuple-element.65.after.dh_s, f32[128,1536]{1,0:T(8,128)S(1)} %project_back.1.dn_s, ...), custom_call_target="tpu_custom_call" | custom-call | flops 1000000000 | bytes 1000000 | tf_op jit(solution)/shard_map/finish/pallas_call | solution.py:575
  (3 shorter events, 0.1 us)
Async XLA Ops:
  1.9 7.5 %collective-permute-start = (bf16[112,1536]{1,0:T(8,128)(2,1)S(1)}, bf16[112,1536]{1,0:T(8,128)(2,1)S(1)}, u32[]{:S(2)}, u32[]{:S(2)}) collective-permute-start(bf16[112,1536]{1,0:T(8,128)(2,1)S(1)} %get-tuple-element.46), channel_id=1, source_target_pairs={{0,4},{4,0},{8,12},{12,8},{16,20},{20,16},{24,28},{28,24},{32,36},... | collective-permute-start | bytes 1032200 | tf_op jit(solution)/shard_map/ppermute | solution.py:552
  2.6 8.8 %collective-permute-start.1 = (bf16[112,1536]{1,0:T(8,128)(2,1)S(1)}, bf16[112,1536]{1,0:T(8,128)(2,1)S(1)}, u32[]{:S(2)}, u32[]{:S(2)}) collective-permute-start(bf16[112,1536]{1,0:T(8,128)(2,1)S(1)} %get-tuple-element.47), channel_id=1, source_target_pairs={{0,1},{1,0},{2,3},{3,2},{4,8},{5,9},{6,10},{7,11},{8,4},{9,5},{10,... | collective-permute-start | bytes 1032200 | tf_op jit(solution)/shard_map/ppermute | solution.py:552
  11.4 8.2 %collective-permute-start.2 = (bf16[80,1536]{1,0:T(8,128)(2,1)S(1)}, bf16[80,1536]{1,0:T(8,128)(2,1)S(1)}, u32[]{:S(2)}, u32[]{:S(2)}) collective-permute-start(bf16[80,1536]{1,0:T(8,128)(2,1)S(1)} %stack_pair.1), channel_id=1, source_target_pairs={{0,1},{1,0},{2,3},{3,2},{4,5},{5,4},{6,7},{7,6},{8,9},{9,8},{10,11... | collective-permute-start | bytes 737288 | tf_op jit(solution)/shard_map/ppermute | solution.py:557
  19.7 7.8 %collective-permute-start.3 = (bf16[64,1536]{1,0:T(8,128)(2,1)S(1)}, bf16[64,1536]{1,0:T(8,128)(2,1)S(1)}, u32[]{:S(2)}, u32[]{:S(2)}) collective-permute-start(bf16[64,1536]{1,0:T(8,128)(2,1)S(1)} %stack_mate.1), channel_id=1, source_target_pairs={{0,3},{1,2},{2,1},{3,0},{4,7},{5,6},{6,5},{7,4},{8,11},{9,10},{10,... | collective-permute-start | bytes 589832 | tf_op jit(solution)/shard_map/ppermute | solution.py:557
  27.0 4.5 %collective-permute-start.4 = (bf16[32,1536]{1,0:T(8,128)(2,1)S(1)}, bf16[32,1536]{1,0:T(8,128)(2,1)S(1)}, u32[]{:S(2)}, u32[]{:S(2)}) collective-permute-start(bf16[32,1536]{1,0:T(8,128)(2,1)S(1)} %get-tuple-element.66.first.l0), channel_id=1, source_target_pairs={{0,1},{1,0},{2,3},{3,2},{4,5},{5,4},{6,7},{7,6},{8,9},{9,8},{10,11... | collective-permute-start | bytes 294920 | tf_op jit(solution)/shard_map/ppermute | solution.py:557
  31.6 12.6 %collective-permute-start.7 = (bf16[64,1536]{1,0:T(8,128)(2,1)S(1)}, bf16[64,1536]{1,0:T(8,128)(2,1)S(1)}, u32[]{:S(2)}, u32[]{:S(2)}) collective-permute-start(bf16[64,1536]{1,0:T(8,128)(2,1)S(1)} %stack_latents.1.after), channel_id=1, source_target_pairs={{0,3},{1,2},{2,1},{3,0},{4,7},{5,6},{6,5},{7,4},{8,11},{9,10},{10,... | collective-permute-start | bytes 589832 | tf_op jit(solution)/shard_map/ppermute | solution.py:557
  36.8 5.7 %collective-permute-start.5 = (bf16[64,1536]{1,0:T(8,128)(2,1)S(1)}, bf16[64,1536]{1,0:T(8,128)(2,1)S(1)}, u32[]{:S(2)}, u32[]{:S(2)}) collective-permute-start(bf16[64,1536]{1,0:T(8,128)(2,1)S(1)} %get-tuple-element.73.after), channel_id=1, source_target_pairs={{0,4},{4,0},{8,12},{12,8},{16,20},{20,16},{24,28},{28,24},{32,36},... | collective-permute-start | bytes 589832 | tf_op jit(solution)/shard_map/ppermute | solution.py:552
  36.9 7.3 %collective-permute-start.6 = (bf16[64,1536]{1,0:T(8,128)(2,1)S(1)}, bf16[64,1536]{1,0:T(8,128)(2,1)S(1)}, u32[]{:S(2)}, u32[]{:S(2)}) collective-permute-start(bf16[64,1536]{1,0:T(8,128)(2,1)S(1)} %get-tuple-element.79), channel_id=1, source_target_pairs={{0,1},{1,0},{2,3},{3,2},{4,8},{5,9},{6,10},{7,11},{8,4},{9,5},{10,... | collective-permute-start | bytes 589832 | tf_op jit(solution)/shard_map/ppermute | solution.py:552

commit v5 on v4

--- a/solution.py
+++ b/solution.py
@@ -18,6 +18,7 @@
 SLOTS = 64
 NREC = 4
 HEAD = 96
+HEADS = 16
 LANE = 128
 NB = D // LANE
 COL = 1536
@@ -193,7 +194,6 @@
     load_q = pltpu.make_async_copy(w_query, wq_s, sems.at[1])
     load_q.start()
     load_o = pltpu.make_async_copy(w_out, wo_s, sems.at[2])
-    load_o.start()
     tm = lax.axis_index("tm")
     llm = lax.axis_index("llm")
     even = tm % 2 == 0
@@ -227,6 +227,7 @@
 
     queried = jnp.concatenate([n_s[64:96, :], n_own[...], n_s[96:128, :]], axis=0)
     load_q.wait()
+    load_o.start()
     q_s[...] = dot(queried, wq_s[...]).astype(BF)
 
     fc_copy.wait()
@@ -243,13 +244,12 @@
     bias_s[32:160, :] = bias_of(FR, HALO, 32)
     bias_s[160:192, :] = bias_of(32, 224, 64)
 
-    @pl.loop(0, 4)
-    def _(g):
+    for base in range(0, HEADS, 16):
+        some = [(h, h // 4, WINDOWS[h % 4]) for h in range(base, base + 16)]
         heads = []
-        for j, (lo, hi) in enumerate(WINDOWS):
-            win = window(g, lo, hi)
-            q = q_s[:, win] * head_mask(j, lo, hi)
-            k = k_s[:, win]
+        for h, g, (lo, hi) in some:
+            q = q_s[:, window(g, lo, hi)] * head_mask(h % 4, lo, hi)
+            k = k_s[:, window(g, lo, hi)]
             heads.append(
                 jnp.concatenate(
                     [dot_t(q[0:32], k[0:256]), dot_t(q[32:160], k[32:288]), dot_t(q[160:192], k[64:320])], axis=0
@@ -260,19 +260,21 @@
         heads = [jnp.exp(scores - top) for scores, top in zip(heads, highest)]
         inverse = [1.0 / jnp.sum(powers, axis=-1, keepdims=True) for powers in heads]
         heads = [(powers * inv).astype(BF) for powers, inv in zip(heads, inverse)]
-        parts = [[None] * 3 for _ in range(3)]
-        for j, (lo, hi) in enumerate(WINDOWS):
-            v = v_s[:, window(g, lo, hi)] * head_mask(j, lo, hi)
-            p = heads[j]
-            p_s[g * 4 + j] = p[32:160]
-            add_tiles(parts[0], lo, dot(p[0:32], v[0:256]))
-            add_tiles(parts[1], lo, dot(p[32:160], v[32:288]))
-            add_tiles(parts[2], lo, dot(p[160:192], v[64:320]))
-        for t in range(3):
-            at = window(g, t, t + 1)
-            att_s[0:32, at] = parts[0][t].astype(BF)
-            att_s[32:160, at] = parts[1][t].astype(BF)
-            att_s[160:192, at] = parts[2][t].astype(BF)
+        for g in range(base // 4, (base + 16) // 4):
+            parts = [[None] * 3 for _ in range(3)]
+            for (h, of, (lo, hi)), p in zip(some, heads):
+                if of != g:
+                    continue
+                v = v_s[:, window(g, lo, hi)] * head_mask(h % 4, lo, hi)
+                p_s[h] = p[32:160]
+                add_tiles(parts[0], lo, dot(p[0:32], v[0:256]))
+                add_tiles(parts[1], lo, dot(p[32:160], v[32:288]))
+                add_tiles(parts[2], lo, dot(p[160:192], v[64:320]))
+            for t in range(3):
+                at = window(g, t, t + 1)
+                att_s[0:32, at] = parts[0][t].astype(BF)
+                att_s[32:160, at] = parts[1][t].astype(BF)
+                att_s[160:192, at] = parts[2][t].astype(BF)
 
     load_o.wait()
 
@@ -416,7 +418,7 @@
             sums.append(along[at : at + part] + dn * h_s[c, 32 + at : 32 + at + part, :])
         return jnp.concatenate(sums, axis=0)
 
-    along = lax.fori_loop(0, NB, conv_back, jnp.zeros((FR, LANE), F32))
+    along = lax.fori_loop(0, NB, conv_back, jnp.zeros((FR, LANE), F32), unroll=2)
     back_h = inv_own * inv_own * inv_own * (jnp.sum(along, axis=-1, keepdims=True) * (1.0 / D))
 
     @pl.loop(0, NB)
@@ -429,30 +431,33 @@
 
 
 def attend_back(after, q_s, v_s, p_s, datt_s, wkt_s, wvt_s, send_a, send_b, ds_o, dk_s, dv_s, ek_s, ev_s):
-    @pl.loop(0, 4)
-    def _(g):
+    for base in range(0, HEADS, 16):
+        some = [(h, h // 4, WINDOWS[h % 4]) for h in range(base, base + 16)]
         heads = []
-        for j, (lo, hi) in enumerate(WINDOWS):
+        for h, g, (lo, hi) in some:
             win = window(g, lo, hi)
-            heads.append(dot_t(datt_s[:, win] * head_mask(j, lo, hi), v_s[32:288, win]))
-        weights = [p_s[g * 4 + j].astype(F32) for j in range(4)]
+            heads.append(dot_t(datt_s[:, win] * head_mask(h % 4, lo, hi), v_s[32:288, win]))
+        weights = [p_s[h].astype(F32) for h, _, _ in some]
         heads = [w * dp for w, dp in zip(weights, heads)]
         sums = [jnp.sum(pd, axis=-1, keepdims=True) for pd in heads]
         heads = [((pd - w * total) * SCALE).astype(BF) for pd, w, total in zip(heads, weights, sums)]
-        dk, dv = [None] * 3, [None] * 3
-        for j, (lo, hi) in enumerate(WINDOWS):
-            win = window(g, lo, hi)
-            mask = head_mask(j, lo, hi)
-            ds_o[g * 4 + j] = heads[j]
-            add_tiles(dk, lo, t_dot(heads[j], q_s[32:160, win] * mask))
-            add_tiles(dv, lo, t_dot(p_s[g * 4 + j], datt_s[:, win] * mask))
-        for t in range(3):
-            at = window(g, t, t + 1)
-            for out, edge, tiles in ((dk_s, ek_s, dk), (dv_s, ev_s, dv)):
-                new = tiles[t].astype(BF)
-                edge[0:64, at] = new[0:64]
-                out[:, at] = new[64:192]
-                edge[64:128, at] = new[192:256]
+        for g in range(base // 4, (base + 16) // 4):
+            dk, dv = [None] * 3, [None] * 3
+            for (h, of, (lo, hi)), ds in zip(some, heads):
+                if of != g:
+                    continue
+                win = window(g, lo, hi)
+                mask = head_mask(h % 4, lo, hi)
+                ds_o[h] = ds
+                add_tiles(dk, lo, t_dot(ds, q_s[32:160, win] * mask))
+                add_tiles(dv, lo, t_dot(p_s[h], datt_s[:, win] * mask))
+            for t in range(3):
+                at = window(g, t, t + 1)
+                for out, edge, tiles in ((dk_s, ek_s, dk), (dv_s, ev_s, dv)):
+                    new = tiles[t].astype(BF)
+                    edge[0:64, at] = new[0:64]
+                    out[:, at] = new[64:192]
+                    edge[64:128, at] = new[192:256]
 
     even = lax.axis_index("tm") % 2 == 0
 
@@ -472,56 +477,36 @@
             send_b[:, cols] = both[64:128]
 
 
-def project_back(after, ds_s, k_s, dk, dv, wq_s, wkt_s, wvt_s, dn_o, dq_s):
+def project_back(
+    fc_in, tl_in, after, ds_s, k_s, dk, dv, wq_s, wkt_s, wvt_s, x_s, gains, l0, l1, l23,
+    g_o, along_o, inv_o, rows_o, fc, tl, dq_s, sems,
+):
+    cf = pltpu.make_async_copy(fc_in, fc, sems.at[0])
+    ct = pltpu.make_async_copy(tl_in, tl, sems.at[1])
+    cf.start()
+    ct.start()
     for g in range(4):
         dq = [None] * 3
         for j, (lo, hi) in enumerate(WINDOWS):
             add_tiles(dq, lo, dot(ds_s[g * 4 + j], k_s[32:288, window(g, lo, hi)] * head_mask(j, lo, hi)))
         for t in range(3):
             dq_s[:, window(g, t, t + 1)] = dq[t].astype(BF)
-    dn_o[...] = dot(dk[...], wkt_s[...]) + dot(dv[...], wvt_s[...]) + dot_t(dq_s[...], wq_s[...])
-
-
-def finish(
-    fc_in, tl_in, x_s, dh_s, dn_s, recv_a, recv_b, l0, l1, l23, gains,
-    rows_out, grad_out, fc, tl, r_s, g_s, out_s, rows_s, sems,
-):
-    cf = pltpu.make_async_copy(fc_in, fc, sems.at[0])
-    ct = pltpu.make_async_copy(tl_in, tl, sems.at[1])
-    cf.start()
-    ct.start()
+    dn = dot(dk[...], wkt_s[...]) + dot(dv[...], wvt_s[...]) + dot_t(dq_s[...], wq_s[...])
+    squares = jnp.zeros((FR, LANE), F32)
+    along = jnp.zeros((FR, LANE), F32)
+    for c in range(NB):
+        cols = slice(c * LANE, (c + 1) * LANE)
+        x = x_s[:, cols].astype(F32)
+        g = dn[:, cols] * gains[c : c + 1, :]
+        g_o[:, cols] = g
+        squares = squares + x * x
+        along = along + g * x
+    along_o[...] = along
+    inv = lax.rsqrt(jnp.sum(squares, axis=-1, keepdims=True) * (1.0 / D) + EPSILON)
+    inv_o[...] = jnp.broadcast_to(inv, (FR, LANE))
+
     tm = lax.axis_index("tm")
     llm = lax.axis_index("llm")
-    even = tm % 2 == 0
-
-    @pl.when(even)
-    def _():
-        r_s[0:64, :] = recv_b[...]
-        r_s[64:128, :] = recv_a[...]
-
-    @pl.when(jnp.logical_not(even))
-    def _():
-        r_s[0:64, :] = recv_a[...]
-        r_s[64:128, :] = recv_b[...]
-
-    copies = []
-    for half in range(2):
-        rows = slice(half * 64, half * 64 + 64)
-        inside = (tm > 0) if half == 0 else (tm < lax.axis_size("tm") - 1)
-        keep = jnp.where(inside, 1.0, 0.0)
-        x = x_s[rows, :].astype(F32)
-        inv = lax.rsqrt(jnp.mean(x * x, axis=-1, keepdims=True) + EPSILON)
-        along = jnp.zeros((64, LANE), F32)
-        for c in range(NB):
-            cols = slice(c * LANE, (c + 1) * LANE)
-            g = (dn_s[rows, cols] + r_s[rows, cols].astype(F32) * keep).astype(BF).astype(F32) * gains[c : c + 1, :]
-            g_s[rows, cols] = g
-            along = along + g * x[:, cols]
-        back = inv * inv * inv * (jnp.sum(along, axis=-1, keepdims=True) * (1.0 / D))
-        out_s[rows, :] = (dh_s[rows, :].astype(F32) + g_s[rows, :] * inv - x * back).astype(BF)
-        copy = pltpu.make_async_copy(out_s.at[rows], grad_out.at[rows], sems.at[2 + half])
-        copy.start()
-        copies.append(copy)
     cf.wait()
     ct.wait()
     starts, lives = routes(fc, tl, tm)
@@ -531,13 +516,43 @@
     for j, apart in enumerate((0, 1, 3, 2)):
         b = llm ^ apart
         r = col - j * LR
-        hit = (r >= 0) & (r < pick(lives, b)) & (slot == r + pick(starts, b))
+        hit = (r >= 0) & (r < LR) & (r < pick(lives, b)) & (slot == r + pick(starts, b))
         chosen = jnp.where(hit, 1.0, chosen)
     latents = jnp.concatenate([l0[...], l1[...], l23[...]], axis=0)
-    rows_s[...] = dot(chosen.astype(BF), latents).astype(BF)
-    copy = pltpu.make_async_copy(rows_s, rows_out, sems.at[4])
-    copy.start()
-    for copy in copies + [copy]:
+    rows_o[...] = dot(chosen.astype(BF), latents).astype(BF)
+
+
+def finish(
+    rows, x_s, dh_s, g_own, along_own, inv_s, recv_a, recv_b, gains, rows_out, grad_out, g_s, out_s, sems
+):
+    rows_copy = pltpu.make_async_copy(rows, rows_out, sems.at[2])
+    rows_copy.start()
+    tm = lax.axis_index("tm")
+    odd = tm % 2
+    one, none = jnp.float32(1.0), jnp.float32(0.0)
+    copies = []
+    for half in range(2):
+        at = slice(half * 64, half * 64 + 64)
+        keep_a = jnp.where(odd == 1 - half, one, none)
+        inside = (tm > 0) & (tm < lax.axis_size("tm") - 1)
+        keep_b = jnp.where((odd == half) & inside, one, none)
+        along = along_own[at, :]
+        for c in range(NB):
+            cols = slice(c * LANE, (c + 1) * LANE)
+            new = recv_a[:, cols].astype(F32) * keep_a + recv_b[:, cols].astype(F32) * keep_b
+            new = new * gains[c : c + 1, :]
+            g_s[at, cols] = g_own[at, cols] + new
+            along = along + new * x_s[at, cols].astype(F32)
+        inv = inv_s[at, :]
+        back = inv * inv * inv * (jnp.sum(along, axis=-1, keepdims=True) * (1.0 / D))
+        for c in range(NB):
+            cols = slice(c * LANE, (c + 1) * LANE)
+            x = x_s[at, cols].astype(F32)
+            out_s[at, cols] = (dh_s[at, cols].astype(F32) + g_s[at, cols] * inv - x * back).astype(BF)
+        copy = pltpu.make_async_copy(out_s.at[at], grad_out.at[at], sems.at[half])
+        copy.start()
+        copies.append(copy)
+    for copy in copies + [rows_copy]:
         copy.wait()
 
 
@@ -667,19 +682,19 @@
         6_000_000_000,
     )
     ret_a, ret_b = swap(n_tm, back_a, back_b)
-    (dn,) = call(
+    g_own, along, inv_x, placed = call(
         project_back,
-        mark("v", back_a, ds, k, dk, dv, wq, wkt, wvt),
-        [rows(FR, F32)],
-        [V((FR, D), BF)],
+        mark("h", frame_counts, tl_in)
+        + mark("v", back_a, ds, k, dk, dv, wq, wkt, wvt, x, gains, latent, latent_1, latent_23),
+        [rows(FR, F32), ((FR, LANE), F32), ((FR, LANE), F32), rows(SLOTS)],
+        [fc, tl, V((FR, D), BF), sems(2)],
         3_000_000_000,
     )
     out_rows, grad = call(
         finish,
-        mark("h", frame_counts, tl_in)
-        + mark("v", x, dhid, dn, ret_a, ret_b, latent, latent_1, latent_23, gains),
+        mark("v", placed, x, dhid, g_own, along, inv_x, ret_a, ret_b, gains),
         [rows(SLOTS), rows(FR)],
-        [fc, tl, V((FR, D), BF), V((FR, D), F32), V((FR, D), BF), V((SLOTS, D), BF), sems(5)],
+        [V((FR, D), F32), V((FR, D), BF), sems(3)],
         1_000_000_000,
         outs_in_hbm=True,
     )

time: 46.6 us -> 44.3 us (0.951)
  Pallas kernels: 31.5 us -> 29 us
  waiting for transfers between devices: 3.73 us -> 4.28 us
    pallas_call x11, Pallas kernels: 31.5 us -> 29 us  [call(): pl.pallas_call(kernel, out_shape=shapes, in_specs=[spec[kind] for kind, _...]
    ppermute x4, waiting for transfers between devices: 0.01 us -> 1.17 us  [trade(): return lax.ppermute(cells, 'llm', [(i, i ^ apart) for i in range(n)])]
    ppermute x2, starting transfers between devices: 4.16 us -> 3.2 us  [swap(): lax.ppermute(cells_b, ('tm', 'llm'), full_b)]
    ppermute x4, starting transfers between devices: 4.86 us -> 5.52 us  [trade(): return lax.ppermute(cells, 'llm', [(i, i ^ apart) for i in range(n)])]
    ppermute x2, waiting for transfers between devices: 3.72 us -> 3.11 us  [swap(): lax.ppermute(cells_b, ('tm', 'llm'), full_b)]
  transfers between devices with their start and end apart: 8 -> 8, of which waited for: 2 -> 3; matrix products, arithmetic and copies ran while one was open for 0% -> 0% of each run, Pallas kernels for 62% -> 60%
where the time goes in v5:
time: 44.3 us; the launch traced here: 44.1 us
  Pallas kernels  29 us (65%)
  starting transfers between devices  9.91 us (22%)
  waiting for transfers between devices  4.28 us (10%)
  between operations  0.9 us (2%)
    pallas_call x11, Pallas kernels, call(): pl.pallas_call(kernel, out_shape=shapes, in_specs=[spec[kind] for kind, _...  29 us
    ppermute x4, starting transfers between devices, trade(): return lax.ppermute(cells, 'llm', [(i, i ^ apart) for i in range(n)])  5.52 us
    ppermute x2, starting transfers between devices, swap(): lax.ppermute(cells_b, ('tm', 'llm'), full_b)  3.2 us
    ppermute x2, waiting for transfers between devices, swap(): lax.ppermute(cells_b, ('tm', 'llm'), full_b)  3.11 us
    ppermute x2, starting transfers between devices, swap(): lax.ppermute(cells_a, 'tm', pairs_a)  1.19 us
    ppermute x4, waiting for transfers between devices, trade(): return lax.ppermute(cells, 'llm', [(i, i ^ apart) for i in range(n)])  1.17 us
  transfers between devices with their start and end apart: 8, of which 3 were waited for; matrix products, arithmetic and copies ran while one was open for 0% of the time, Pallas kernels for 60%

profile of v5, /device:TPU:39, one launch (start us, length us, event | category | flops | bytes accessed | tf_op | source)
XLA Modules:
  0.0 44.1 jit_solution(3570259158854947514)
XLA Ops:
  0.6 1.2 %prepare.1 = (bf16[112,1536]{1,0:T(8,128)(2,1)S(1)}, bf16[112,1536]{1,0:T(8,128)(2,1)S(1)}, bf16[32,1536]{1,0:T(8,128)(2,1)S(1)}, bf16[64,1536]{1,0:T(8,128)(2,1)S(1)}, bf16[32,1536]{1,0:T(8,128)(2,1)S(1)}) custom-call(s32[4]{0:T(128)} %fc_in.9, s32[4,32]{1,0:T(4,128)} %bitcast.11, bf16[128,1536]{1,0:T(8,128)(2,1)} %bitcast.8, bf16[64,1536]{1,0:T(8,128)(2,1)} %bitcast.10), custom_call_target="tpu_custom_call" | custom-call | flops 100000000 | bytes 1000000 | tf_op jit(solution)/shard_map/prepare/pallas_call | solution.py:590
  1.9 0.8 %collective-permute-start = (bf16[112,1536]{1,0:T(8,128)(2,1)S(1)}, bf16[112,1536]{1,0:T(8,128)(2,1)S(1)}, u32[]{:S(2)}, u32[]{:S(2)}) collective-permute-start(bf16[112,1536]{1,0:T(8,128)(2,1)S(1)} %get-tuple-element.49), channel_id=1, source_target_pairs={{0,4},{4,0},{8,12},{12,8},{16,20},{20,16},{24,28},{28,24},{32,36},... | collective-permute-start | bytes 1032200 | tf_op jit(solution)/shard_map/ppermute | solution.py:567
  2.6 1.5 %collective-permute-start.1 = (bf16[112,1536]{1,0:T(8,128)(2,1)S(1)}, bf16[112,1536]{1,0:T(8,128)(2,1)S(1)}, u32[]{:S(2)}, u32[]{:S(2)}) collective-permute-start(bf16[112,1536]{1,0:T(8,128)(2,1)S(1)} %get-tuple-element.50), channel_id=1, source_target_pairs={{0,1},{1,0},{2,3},{3,2},{4,8},{5,9},{6,10},{7,11},{8,4},{9,5},{10,... | collective-permute-start | bytes 1032200 | tf_op jit(solution)/shard_map/ppermute | solution.py:567
  4.2 5.2 %project_own.1 = (bf16[128,1536]{1,0:T(8,128)(2,1)S(1)}, f32[12,128]{1,0:T(8,128)S(1)}, bf16[128,1536]{1,0:T(8,128)(2,1)S(1)}, bf16[128,1536]{1,0:T(8,128)(2,1)S...) custom-call(bf16[32,1536]{1,0:T(8,128)(2,1)S(1)} %get-tuple-element., ...), custom_call_target="tpu_custom_call" | custom-call | flops 6000000000 | bytes 1000000 | tf_op jit(solution)/shard_map/project_own/pallas_call | solution.py:590
  9.4 0.0 collective-permute-done.recv_a
  9.4 2.0 %collective-permute-done.1.recv_b = bf16[112,1536]{1,0:T(8,128)(2,1)S(1)} collective-permute-done((bf16[112,1536]{1,0:T(8,128)(2,1)S(1)}, bf16[112,1536]{1,0:T(8,128)(2,1)S(1)}, u32[]{:S(2)}, u32[]{:S(2)}) %collective-permute-start.1) | collective-permute-done | bytes 344096 | tf_op jit(solution)/shard_map/ppermute | solution.py:567
  11.4 1.4 %collective-permute-start.2 = (bf16[80,1536]{1,0:T(8,128)(2,1)S(1)}, bf16[80,1536]{1,0:T(8,128)(2,1)S(1)}, u32[]{:S(2)}, u32[]{:S(2)}) collective-permute-start(bf16[80,1536]{1,0:T(8,128)(2,1)S(1)} %stack_pair.1), channel_id=1, source_target_pairs={{0,1},{1,0},{2,3},{3,2},{4,5},{5,4},{6,7},{7,6},{8,9},{9,8},{10,11... | collective-permute-start | bytes 737288 | tf_op jit(solution)/shard_map/ppermute | solution.py:572
  12.8 5.8 %attend.1 = (bf16[192,1536]{1,0:T(8,128)(2,1)S(1)}, bf16[192,1536]{1,0:T(8,128)(2,1)S(1)}, bf16[320,1536]{1,0:T(8,128)(2,1)S(1)}, bf16[320,1536]{1,0:T(8,128)(2,...) custom-call(s32[4]{0:T(128)} %fc_in.9, ...), custom_call_target="tpu_custom_call" | custom-call | flops 8000000000 | bytes 1000000 | tf_op jit(solution)/shard_map/attend/pallas_call | solution.py:590
  18.6 0.0 collective-permute-done.2.got_pair
  18.7 2.0 %collective-permute-start.3 = (bf16[64,1536]{1,0:T(8,128)(2,1)S(1)}, bf16[64,1536]{1,0:T(8,128)(2,1)S(1)}, u32[]{:S(2)}, u32[]{:S(2)}) collective-permute-start(bf16[64,1536]{1,0:T(8,128)(2,1)S(1)} %stack_mate.1), channel_id=1, source_target_pairs={{0,3},{1,2},{2,1},{3,0},{4,7},{5,6},{6,5},{7,4},{8,11},{9,10},{10,... | collective-permute-start | bytes 589832 | tf_op jit(solution)/shard_map/ppermute | solution.py:572
  20.6 5.3 %convolve.1 = (bf16[32,1536]{1,0:T(8,128)(2,1)S(1)}, f32[12,192,128]{2,1,0:T(8,128)S(1)}, f32[12,160,128]{2,1,0:T(8,128)S(1)}, f32[12,40,128]{2,1,0:T(8,128)S(1)...) custom-call(s32[4]{0:T(128)} %fc_in.9, ...), custom_call_target="tpu_custom_call" | custom-call | flops 5000000000 | bytes 1000000 | tf_op jit(solution)/shard_map/convolve/pallas_call | solution.py:590
  26.0 0.5 %collective-permute-start.4 = (bf16[32,1536]{1,0:T(8,128)(2,1)S(1)}, bf16[32,1536]{1,0:T(8,128)(2,1)S(1)}, u32[]{:S(2)}, u32[]{:S(2)}) collective-permute-start(bf16[32,1536]{1,0:T(8,128)(2,1)S(1)} %get-tuple-element.70.first.l0), channel_id=1, source_target_pairs={{0,1},{1,0},{2,3},{3,2},{4,5},{5,4},{6,7},{7,6},{8,9},{9,8},{10,11... | collective-permute-start | bytes 294920 | tf_op jit(solution)/shard_map/ppermute | solution.py:572
  26.5 0.0 collective-permute-done.3.got_mate
  26.5 4.0 %convolve_back.1 = (bf16[128,1536]{1,0:T(8,128)(2,1)S(1)}, bf16[128,1536]{1,0:T(8,128)(2,1)S(1)}) custom-call(s32[4]{0:T(128)} %fc_in.9, bf16[32,1536]{1,0:T(8,128)(2,1)S(1)} %get-tuple-element.46.after.own, bf16[80,1536]{1,0:T(8,128)(2,1)S(1)} %collective-permute-done.2.got_pair, bf16[64,1536]{1,0:T(8,128)(2,1)S(1)} %collective-permute-done.3.got_mate, ...), custom_call_target="tpu_custom_call" | custom-call | flops 5000000000 | bytes 1000000 | tf_op jit(solution)/shard_map/convolve_back/pallas_call | solution.py:590
  30.4 0.0 collective-permute-done.4.second.l1
  30.5 1.7 %collective-permute-start.5 = (bf16[64,1536]{1,0:T(8,128)(2,1)S(1)}, bf16[64,1536]{1,0:T(8,128)(2,1)S(1)}, u32[]{:S(2)}, u32[]{:S(2)}) collective-permute-start(bf16[64,1536]{1,0:T(8,128)(2,1)S(1)} %stack_latents.1.after), channel_id=1, source_target_pairs={{0,3},{1,2},{2,1},{3,0},{4,7},{5,6},{6,5},{7,4},{8,11},{9,10},{10,... | collective-permute-start | bytes 589832 | tf_op jit(solution)/shard_map/ppermute | solution.py:572
  32.1 2.9 %attend_back.1 = (bf16[64,1536]{1,0:T(8,128)(2,1)S(1)}, bf16[64,1536]{1,0:T(8,128)(2,1)S(1)}, bf16[16,128,256]{2,1,0:T(8,128)(2,1)S(1)}, bf16[128,1536]{1,0:T(8,128)(2,1)S(1)}, bf16[128,1536]{1,0:T(8,128)(2,1)S(1)}) custom-call(bf16[64,1536]{1,0:T(8,128)(2,1)S(1)} %stack_latents.1.after, bf16[192,1536]{1,0:T(8,128)(2,1)S(1)} %get-tuple-element.71.q_s, ...), custom_call_target="tpu_custom_call" | custom-call | flops 6000000000 | bytes 1000000 | tf_op jit(solution)/shard_map/attend_back/pallas_call | solution.py:590
  35.0 0.4 collective-permute-start.6
  35.5 1.7 %collective-permute-start.7 = (bf16[64,1536]{1,0:T(8,128)(2,1)S(1)}, bf16[64,1536]{1,0:T(8,128)(2,1)S(1)}, u32[]{:S(2)}, u32[]{:S(2)}) collective-permute-start(bf16[64,1536]{1,0:T(8,128)(2,1)S(1)} %get-tuple-element.87), channel_id=1, source_target_pairs={{0,1},{1,0},{2,3},{3,2},{4,8},{5,9},{6,10},{7,11},{8,4},{9,5},{10,... | collective-permute-start | bytes 589832 | tf_op jit(solution)/shard_map/ppermute | solution.py:567
  37.1 1.2 %collective-permute-done.5.l23 = bf16[64,1536]{1,0:T(8,128)(2,1)S(1)} collective-permute-done((bf16[64,1536]{1,0:T(8,128)(2,1)S(1)}, bf16[64,1536]{1,0:T(8,128)(2,1)S(1)}, u32[]{:S(2)}, u32[]{:S(2)}) %collective-permute-start.5) | collective-permute-done | bytes 196640 | tf_op jit(solution)/shard_map/ppermute | solution.py:572
  38.3 3.2 %project_back.1 = (f32[128,1536]{1,0:T(8,128)S(1)}, f32[128,128]{1,0:T(8,128)S(1)}, f32[128,128]{1,0:T(8,128)S(1)}, bf16[64,1536]{1,0:T(8,128)(2,1)S(1)}) custom-call(s32[4]{0:T(128)} %fc_in.9, s32[4,32]{1,0:T(4,128)} %bitcast.12, bf16[64,1536]{1,0:T(8,128)(2,1)S(1)} %get-tuple-element.77.after, bf16[16,128,256]{2,1,0:T(8,128)(2,1)S(1)} %get-tuple-element.78.ds_s, ...), custom_call_target="tpu_custom_call" | custom-call | flops 3000000000 | bytes 1000000 | tf_op jit(solution)/shard_map/project_back/pallas_call | solution.py:590
  41.5 0.0 collective-permute-done.6.recv_a
  41.6 1.1 %collective-permute-done.7.recv_b = bf16[64,1536]{1,0:T(8,128)(2,1)S(1)} collective-permute-done((bf16[64,1536]{1,0:T(8,128)(2,1)S(1)}, bf16[64,1536]{1,0:T(8,128)(2,1)S(1)}, u32[]{:S(2)}, u32[]{:S(2)}) %collective-permute-start.7) | collective-permute-done | bytes 196640 | tf_op jit(solution)/shard_map/ppermute | solution.py:567
  42.7 1.2 %finish.1 = (bf16[64,1536]{1,0:T(8,128)(2,1)}, bf16[128,1536]{1,0:T(8,128)(2,1)}) custom-call(bf16[64,1536]{1,0:T(8,128)(2,1)S(1)} %get-tuple-element.83.rows, bf16[128,1536]{1,0:T(8,128)(2,1)S(1)} %get-tuple-element.51.x_own.x_s, bf16[128,1536]{1,0:T(8,128)(2,1)S(1)} %get-tuple-element.69.after.dh_s, f32[128,1536]{1,0:T(8,128)S(1)} %get-tuple-element.84.g_own, ...), custom_call_target="tpu_custom_call" | custom-call | flops 1000000000 | bytes 1000000 | tf_op jit(solution)/shard_map/finish/pallas_call | solution.py:590
  (3 shorter events, 0.1 us)
Async XLA Ops:
  1.9 7.5 %collective-permute-start = (bf16[112,1536]{1,0:T(8,128)(2,1)S(1)}, bf16[112,1536]{1,0:T(8,128)(2,1)S(1)}, u32[]{:S(2)}, u32[]{:S(2)}) collective-permute-start(bf16[112,1536]{1,0:T(8,128)(2,1)S(1)} %get-tuple-element.49), channel_id=1, source_target_pairs={{0,4},{4,0},{8,12},{12,8},{16,20},{20,16},{24,28},{28,24},{32,36},... | collective-permute-start | bytes 1032200 | tf_op jit(solution)/shard_map/ppermute | solution.py:567
  2.6 8.8 %collective-permute-start.1 = (bf16[112,1536]{1,0:T(8,128)(2,1)S(1)}, bf16[112,1536]{1,0:T(8,128)(2,1)S(1)}, u32[]{:S(2)}, u32[]{:S(2)}) collective-permute-start(bf16[112,1536]{1,0:T(8,128)(2,1)S(1)} %get-tuple-element.50), channel_id=1, source_target_pairs={{0,1},{1,0},{2,3},{3,2},{4,8},{5,9},{6,10},{7,11},{8,4},{9,5},{10,... | collective-permute-start | bytes 1032200 | tf_op jit(solution)/shard_map/ppermute | solution.py:567
  11.4 7.2 %collective-permute-start.2 = (bf16[80,1536]{1,0:T(8,128)(2,1)S(1)}, bf16[80,1536]{1,0:T(8,128)(2,1)S(1)}, u32[]{:S(2)}, u32[]{:S(2)}) collective-permute-start(bf16[80,1536]{1,0:T(8,128)(2,1)S(1)} %stack_pair.1), channel_id=1, source_target_pairs={{0,1},{1,0},{2,3},{3,2},{4,5},{5,4},{6,7},{7,6},{8,9},{9,8},{10,11... | collective-permute-start | bytes 737288 | tf_op jit(solution)/shard_map/ppermute | solution.py:572
  18.7 7.8 %collective-permute-start.3 = (bf16[64,1536]{1,0:T(8,128)(2,1)S(1)}, bf16[64,1536]{1,0:T(8,128)(2,1)S(1)}, u32[]{:S(2)}, u32[]{:S(2)}) collective-permute-start(bf16[64,1536]{1,0:T(8,128)(2,1)S(1)} %stack_mate.1), channel_id=1, source_target_pairs={{0,3},{1,2},{2,1},{3,0},{4,7},{5,6},{6,5},{7,4},{8,11},{9,10},{10,... | collective-permute-start | bytes 589832 | tf_op jit(solution)/shard_map/ppermute | solution.py:572
  26.0 4.5 %collective-permute-start.4 = (bf16[32,1536]{1,0:T(8,128)(2,1)S(1)}, bf16[32,1536]{1,0:T(8,128)(2,1)S(1)}, u32[]{:S(2)}, u32[]{:S(2)}) collective-permute-start(bf16[32,1536]{1,0:T(8,128)(2,1)S(1)} %get-tuple-element.70.first.l0), channel_id=1, source_target_pairs={{0,1},{1,0},{2,3},{3,2},{4,5},{5,4},{6,7},{7,6},{8,9},{9,8},{10,11... | collective-permute-start | bytes 294920 | tf_op jit(solution)/shard_map/ppermute | solution.py:572
  30.5 7.8 %collective-permute-start.5 = (bf16[64,1536]{1,0:T(8,128)(2,1)S(1)}, bf16[64,1536]{1,0:T(8,128)(2,1)S(1)}, u32[]{:S(2)}, u32[]{:S(2)}) collective-permute-start(bf16[64,1536]{1,0:T(8,128)(2,1)S(1)} %stack_latents.1.after), channel_id=1, source_target_pairs={{0,3},{1,2},{2,1},{3,0},{4,7},{5,6},{6,5},{7,4},{8,11},{9,10},{10,... | collective-permute-start | bytes 589832 | tf_op jit(solution)/shard_map/ppermute | solution.py:572
  35.0 6.5 %collective-permute-start.6 = (bf16[64,1536]{1,0:T(8,128)(2,1)S(1)}, bf16[64,1536]{1,0:T(8,128)(2,1)S(1)}, u32[]{:S(2)}, u32[]{:S(2)}) collective-permute-start(bf16[64,1536]{1,0:T(8,128)(2,1)S(1)} %get-tuple-element.77.after), channel_id=1, source_target_pairs={{0,4},{4,0},{8,12},{12,8},{16,20},{20,16},{24,28},{28,24},{32,36},... | collective-permute-start | bytes 589832 | tf_op jit(solution)/shard_map/ppermute | solution.py:567
  35.5 7.2 %collective-permute-start.7 = (bf16[64,1536]{1,0:T(8,128)(2,1)S(1)}, bf16[64,1536]{1,0:T(8,128)(2,1)S(1)}, u32[]{:S(2)}, u32[]{:S(2)}) collective-permute-start(bf16[64,1536]{1,0:T(8,128)(2,1)S(1)} %get-tuple-element.87), channel_id=1, source_target_pairs={{0,1},{1,0},{2,3},{3,2},{4,8},{5,9},{6,10},{7,11},{8,4},{9,5},{10,... | collective-permute-start | bytes 589832 | tf_op jit(solution)/shard_map/ppermute | solution.py:567

commit v6 on v5

--- a/solution.py
+++ b/solution.py
@@ -69,7 +69,7 @@
     return out
 
 
-def prepare(fc_in, tl_in, audio, grads, send_a, send_b, own, pair, mate, fc, tl, g_buf, sems):
+def prepare(fc_in, tl_in, audio, grads, send_b, send_a, own, pair, mate, placing, fc, tl, g_buf, sems):
     cf = pltpu.make_async_copy(fc_in, fc, sems.at[0])
     ct = pltpu.make_async_copy(tl_in, tl, sems.at[1])
     cf.start()
@@ -108,6 +108,14 @@
             hit = (place // 4 == (j + 3) % 4) & (r < lives[j]) & (slot == r + starts[j])
             chosen = jnp.where(hit, 1.0, chosen)
         picked.append(chosen.astype(BF))
+    slot = lax.broadcasted_iota(jnp.int32, (SLOTS, NREC * LR), 0) + llm * SLOTS
+    col = lax.broadcasted_iota(jnp.int32, (SLOTS, NREC * LR), 1)
+    chosen = jnp.zeros((SLOTS, NREC * LR), F32)
+    for j, apart in enumerate((0, 1, 3, 2)):
+        r = col - j * LR
+        hit = (r >= 0) & (r < LR) & (r < lives[apart]) & (slot == r + starts[apart])
+        chosen = jnp.where(hit, 1.0, chosen)
+    placing[...] = chosen.astype(BF)
     cg.wait()
     moved = dot(jnp.concatenate(picked, axis=0), g_buf[...]).astype(BF)
     own[...] = moved[:LR]
@@ -153,7 +161,7 @@
     return jnp.concatenate(pair, axis=0).astype(BF)
 
 
-def stack_pair(after, pair, recv_a, recv_b, out):
+def stack_pair(after, pair, recv_b, recv_a, out):
     out[: 2 * LR, :] = pair[...]
     out[2 * LR :, :] = halves(recv_a[HALO:, :], recv_b[HALO:, :], 0)
 
@@ -187,7 +195,7 @@
 
 def attend(
     fc_in, w_query, w_out, recv_a, recv_b, x_own, n_own, gains, k_own, v_own, wk_s, wv_s,
-    xq_o, q_s, k_s, v_s, p_s, att_s, wq_s, wo_s, fc, n_s, bias_s, sems,
+    h_s, inv_o, q_s, k_s, v_s, p_s, wq_s, wo_s, fc, n_s, xq_o, att_s, bias_s, sems,
 ):
     fc_copy = pltpu.make_async_copy(fc_in, fc, sems.at[0])
     fc_copy.start()
@@ -278,6 +286,20 @@
 
     load_o.wait()
 
+    def hidden_step(j, squares):
+        cols = lanes(j, COL)
+        h = dot(att_s[...], wo_s[:, cols]) + xq_o[:, cols].astype(F32)
+        h = h.astype(BF).astype(F32)
+        for t in range(COL // LANE):
+            part = h[:, t * LANE : (t + 1) * LANE]
+            h_s[j * (COL // LANE) + t] = part
+            squares = squares + part * part
+        return squares
+
+    squares = lax.fori_loop(0, NC, hidden_step, jnp.zeros((QR, LANE), F32))
+    inv_h = lax.rsqrt(jnp.sum(squares, axis=-1, keepdims=True) * (1.0 / D) + EPSILON)
+    inv_o[...] = jnp.broadcast_to(inv_h, (QR, LANE))
+
 
 def spoken_rows(fc, tm, llm):
     frame = lax.broadcasted_iota(jnp.int32, (QR, 1), 0) + (tm * FR - 32)
@@ -285,8 +307,8 @@
 
 
 def convolve(
-    fc_in, xq, att_s, wo_s, cg_in, lg_in, taps_in,
-    lat_o, h_s, dsilu_s, pool_s, inv_o, cg_s, lg_s, tap_s, wot_s, fc, ci_s, up_s, norm_t, sems,
+    fc_in, h_s, inv_s, wo_s, cg_in, lg_in, taps_in,
+    lat_o, dsilu_s, pool_s, cg_s, lg_s, tap_s, wot_s, fc, ci_s, up_s, norm_t, sems,
 ):
     copies = [
         pltpu.make_async_copy(source, into, sems.at[i])
@@ -297,22 +319,9 @@
     tm = lax.axis_index("tm")
     llm = lax.axis_index("llm")
 
-    def hidden_step(j, squares):
-        cols = lanes(j, COL)
-        h = dot(att_s[...], wo_s[:, cols]) + xq[:, cols].astype(F32)
-        h = h.astype(BF).astype(F32)
-        for t in range(COL // LANE):
-            part = h[:, t * LANE : (t + 1) * LANE]
-            h_s[j * (COL // LANE) + t] = part
-            squares = squares + part * part
-        return squares
-
-    squares = lax.fori_loop(0, NC, hidden_step, jnp.zeros((QR, LANE), F32))
-    inv_h = lax.rsqrt(jnp.sum(squares, axis=-1, keepdims=True) * (1.0 / D) + EPSILON)
-    inv_o[...] = jnp.broadcast_to(inv_h, (QR, LANE))
     for copy in copies:
         copy.wait()
-    inv_spoken = inv_h * spoken_rows(fc, tm, llm)
+    inv_spoken = inv_s[...] * spoken_rows(fc, tm, llm)
 
     def conv_step(c, squares):
         cols = lanes(c)
@@ -478,13 +487,8 @@
 
 
 def project_back(
-    fc_in, tl_in, after, ds_s, k_s, dk, dv, wq_s, wkt_s, wvt_s, x_s, gains, l0, l1, l23,
-    g_o, along_o, inv_o, rows_o, fc, tl, dq_s, sems,
+    after, ds_s, k_s, dk, dv, wq_s, wkt_s, wvt_s, x_s, gains, g_o, along_o, inv_o, dq_s,
 ):
-    cf = pltpu.make_async_copy(fc_in, fc, sems.at[0])
-    ct = pltpu.make_async_copy(tl_in, tl, sems.at[1])
-    cf.start()
-    ct.start()
     for g in range(4):
         dq = [None] * 3
         for j, (lo, hi) in enumerate(WINDOWS):
@@ -505,21 +509,10 @@
     inv = lax.rsqrt(jnp.sum(squares, axis=-1, keepdims=True) * (1.0 / D) + EPSILON)
     inv_o[...] = jnp.broadcast_to(inv, (FR, LANE))
 
-    tm = lax.axis_index("tm")
-    llm = lax.axis_index("llm")
-    cf.wait()
-    ct.wait()
-    starts, lives = routes(fc, tl, tm)
-    slot = lax.broadcasted_iota(jnp.int32, (SLOTS, NREC * LR), 0) + llm * SLOTS
-    col = lax.broadcasted_iota(jnp.int32, (SLOTS, NREC * LR), 1)
-    chosen = jnp.zeros((SLOTS, NREC * LR), F32)
-    for j, apart in enumerate((0, 1, 3, 2)):
-        b = llm ^ apart
-        r = col - j * LR
-        hit = (r >= 0) & (r < LR) & (r < pick(lives, b)) & (slot == r + pick(starts, b))
-        chosen = jnp.where(hit, 1.0, chosen)
+
+def place_rows(after, chosen, l0, l1, l23, rows_o):
     latents = jnp.concatenate([l0[...], l1[...], l23[...]], axis=0)
-    rows_o[...] = dot(chosen.astype(BF), latents).astype(BF)
+    rows_o[...] = dot(chosen[...], latents).astype(BF)
 
 
 def finish(
@@ -564,7 +557,8 @@
         partner = ((i + 1) ^ 1) - 1
         end = partner < 0 or partner >= count
         full_b += [(i * n + y, i * n + (y ^ 1) if end else partner * n + y) for y in range(n)]
-    return lax.ppermute(cells_a, "tm", pairs_a), lax.ppermute(cells_b, ("tm", "llm"), full_b)
+    got_b = lax.ppermute(cells_b, ("tm", "llm"), full_b)
+    return lax.ppermute(cells_a, "tm", pairs_a), got_b
 
 
 def trade(cells, apart):
@@ -593,7 +587,7 @@
         in_specs=[spec[kind] for kind, _ in ins],
         out_specs=[ANY if outs_in_hbm else VMEM] * len(outs),
         scratch_shapes=scratch,
-        compiler_params=pltpu.CompilerParams(vmem_limit_bytes=12 * 1024 * 1024),
+        compiler_params=pltpu.CompilerParams(vmem_limit_bytes=14 * 1024 * 1024),
         cost_estimate=pl.CostEstimate(flops=flops, bytes_accessed=1_000_000, transcendentals=0),
         name=kernel.__name__,
     )(*[place[kind](array) for kind, array in ins])
@@ -623,10 +617,10 @@
     def sems(*dims):
         return pltpu.SemaphoreType.DMA(dims)
 
-    send_a, send_b, own, pair, mate = call(
+    send_b, send_a, own, pair, mate, placing = call(
         prepare,
         mark("h", frame_counts, tl_in, signal, llm_grads[0]),
-        [rows(HALO + 16), rows(HALO + 16), rows(LR), rows(2 * LR), rows(LR)],
+        [rows(HALO + 16), rows(HALO + 16), rows(LR), rows(2 * LR), rows(LR), ((SLOTS, NREC * LR), BF)],
         [fc, tl, V((SLOTS, D), BF), sems(5)],
         100_000_000,
     )
@@ -638,23 +632,26 @@
         [sems(4)],
         6_000_000_000,
     )
-    (pairs,) = call(stack_pair, mark("v", gains, pair, recv_a, recv_b), [rows(2 * LR + 16)], [], 1_000_000)
+    (pairs,) = call(stack_pair, mark("v", gains, pair, recv_b, recv_a), [rows(2 * LR + 16)], [], 1_000_000)
     got_pair = trade(pairs, 1)
-    xq, q, k, v, p, att, wq, wo = call(
+    h, inv, q, k, v, p, wq, wo = call(
         attend,
         mark("h", frame_counts, w_query, w_out)
         + mark("v", recv_a, recv_b, x, normed, gains, k_own, v_own, wk, wv),
-        [rows(QR), rows(QR), rows(EXT), rows(EXT), ((16, FR, 256), BF), rows(QR), weight, weight],
-        [fc, V((2 * HALO, D), BF), V((QR, 256), F32), sems(3)],
+        [
+            ((NB, QR, LANE), F32), ((QR, LANE), F32), rows(QR), rows(EXT), rows(EXT), ((16, FR, 256), BF),
+            weight, weight,
+        ],
+        [fc, V((2 * HALO, D), BF), V((QR, D), BF), V((QR, D), BF), V((QR, 256), F32), sems(3)],
         8_000_000_000,
     )
-    (mates,) = call(stack_mate, mark("v", xq, mate, got_pair, recv_a, recv_b), [rows(LR + 32)], [], 1_000_000)
+    (mates,) = call(stack_mate, mark("v", inv, mate, got_pair, recv_a, recv_b), [rows(LR + 32)], [], 1_000_000)
     got_mate = trade(mates, 3)
-    latent, h, dsilu, pool, inv, cgain, lgain, taps, wot = call(
+    latent, dsilu, pool, cgain, lgain, taps, wot = call(
         convolve,
-        mark("h", frame_counts) + mark("v", xq, att, wo) + mark("h", conv_row, latent_row, conv_kernel),
+        mark("h", frame_counts) + mark("v", h, inv, wo) + mark("h", conv_row, latent_row, conv_kernel),
         [
-            rows(LR), ((NB, QR, LANE), F32), ((NB, SR, LANE), F32), ((NB, PR, LANE), F32), ((QR, LANE), F32),
+            rows(LR), ((NB, SR, LANE), F32), ((NB, PR, LANE), F32),
             gain, gain, rows(KERN, F32), weight,
         ],
         [fc, V((QR, LANE), F32), V((SR, LANE), F32), V((PR, LANE), F32), sems(4)],
@@ -682,13 +679,19 @@
         6_000_000_000,
     )
     ret_a, ret_b = swap(n_tm, back_a, back_b)
-    g_own, along, inv_x, placed = call(
+    g_own, along, inv_x = call(
         project_back,
-        mark("h", frame_counts, tl_in)
-        + mark("v", back_a, ds, k, dk, dv, wq, wkt, wvt, x, gains, latent, latent_1, latent_23),
-        [rows(FR, F32), ((FR, LANE), F32), ((FR, LANE), F32), rows(SLOTS)],
-        [fc, tl, V((FR, D), BF), sems(2)],
+        mark("v", back_a, ds, k, dk, dv, wq, wkt, wvt, x, gains),
+        [rows(FR, F32), ((FR, LANE), F32), ((FR, LANE), F32)],
+        [V((FR, D), BF)],
         3_000_000_000,
+    )
+    (placed,) = call(
+        place_rows,
+        mark("v", along, placing, latent, latent_1, latent_23),
+        [rows(SLOTS)],
+        [],
+        50_000_000,
     )
     out_rows, grad = call(
         finish,

time: 44.3 us -> 46.1 us (1.041)
  waiting for transfers between devices: 4.28 us -> 5.67 us
    ppermute x4, waiting for transfers between devices: 3.11 us -> 4.6 us  [the longest x2 4.6 us: swap(): got_b = lax.ppermute(cells_b, ('tm', 'llm'), full_b)]
    pallas_call x11 -> x12, Pallas kernels: 29 us -> 29.2 us  [call(): pl.pallas_call(kernel, out_shape=shapes, in_specs=[spec[kind] for kind, _...]
  transfers between devices with their start and end apart: 8 -> 8, of which waited for: 3 -> 3; matrix products, arithmetic and copies ran while one was open for 0% -> 0% of each run, Pallas kernels for 60% -> 58%
where the time goes in v6:
time: 46.1 us; the launch traced here: 45.9 us
  Pallas kernels  29.2 us (63%)
  starting transfers between devices  10.1 us (22%)
  waiting for transfers between devices  5.67 us (12%)
  between operations  0.91 us (2%)
    pallas_call x12, Pallas kernels, call(): pl.pallas_call(kernel, out_shape=shapes, in_specs=[spec[kind] for kind, _...  29.2 us
    ppermute x4, starting transfers between devices, trade(): return lax.ppermute(cells, 'llm', [(i, i ^ apart) for i in range(n)])  5.84 us
    ppermute x2, waiting for transfers between devices, swap(): got_b = lax.ppermute(cells_b, ('tm', 'llm'), full_b)  4.6 us
    ppermute x2, starting transfers between devices, swap(): got_b = lax.ppermute(cells_b, ('tm', 'llm'), full_b)  3.03 us
    ppermute x2, starting transfers between devices, swap(): return (lax.ppermute(cells_a, 'tm', pairs_a), got_b)  1.2 us
    ppermute x4, waiting for transfers between devices, trade(): return lax.ppermute(cells, 'llm', [(i, i ^ apart) for i in range(n)])  1.07 us
  transfers between devices with their start and end apart: 8, of which 3 were waited for; matrix products, arithmetic and copies ran while one was open for 0% of the time, Pallas kernels for 58%

profile of v6, /device:TPU:39, one launch (start us, length us, event | category | flops | bytes accessed | tf_op | source)
XLA Modules:
  0.0 45.9 jit_solution(5934307264322368300)
XLA Ops:
  0.6 1.2 %prepare.1 = (bf16[112,1536]{1,0:T(8,128)(2,1)S(1)}, bf16[112,1536]{1,0:T(8,128)(2,1)S(1)}, bf16[32,1536]{1,0:T(8,128)(2,1)S(1)}, bf16[64,1536]{1,0:T(8,128)(2,1...) custom-call(s32[4]{0:T(128)} %fc_in.7, s32[4,32]{1,0:T(4,128)} %bitcast.11, bf16[128,1536]{1,0:T(8,128)(2,1)} %bitcast.8, ...), custom_call_target="tpu_custom_call" | custom-call | flops 100000000 | bytes 1000000 | tf_op jit(solution)/shard_map/prepare/pallas_call | solution.py:584
  1.9 2.2 %collective-permute-start = (bf16[112,1536]{1,0:T(8,128)(2,1)S(1)}, bf16[112,1536]{1,0:T(8,128)(2,1)S(1)}, u32[]{:S(2)}, u32[]{:S(2)}) collective-permute-start(bf16[112,1536]{1,0:T(8,128)(2,1)S(1)} %get-tuple-element.47), channel_id=1, source_target_pairs={{0,1},{1,0},{2,3},{3,2},{4,8},{5,9},{6,10},{7,11},{8,4},{9,5},{10,... | collective-permute-start | bytes 1032200 | tf_op jit(solution)/shard_map/ppermute | solution.py:560
  4.1 0.0 collective-permute-start.1
  4.1 5.2 %project_own.1 = (bf16[128,1536]{1,0:T(8,128)(2,1)S(1)}, f32[12,128]{1,0:T(8,128)S(1)}, bf16[128,1536]{1,0:T(8,128)(2,1)S(1)}, bf16[128,1536]{1,0:T(8,128)(2,1)S...) custom-call(bf16[32,1536]{1,0:T(8,128)(2,1)S(1)} %get-tuple-element., ...), custom_call_target="tpu_custom_call" | custom-call | flops 6000000000 | bytes 1000000 | tf_op jit(solution)/shard_map/project_own/pallas_call | solution.py:584
  9.3 1.4 %collective-permute-done.recv_b = bf16[112,1536]{1,0:T(8,128)(2,1)S(1)} collective-permute-done((bf16[112,1536]{1,0:T(8,128)(2,1)S(1)}, bf16[112,1536]{1,0:T(8,128)(2,1)S(1)}, u32[]{:S(2)}, u32[]{:S(2)}) %collective-permute-start) | collective-permute-done | bytes 344096 | tf_op jit(solution)/shard_map/ppermute | solution.py:560
  10.8 0.0 collective-permute-done.1.recv_a
  10.8 1.4 %collective-permute-start.2 = (bf16[80,1536]{1,0:T(8,128)(2,1)S(1)}, bf16[80,1536]{1,0:T(8,128)(2,1)S(1)}, u32[]{:S(2)}, u32[]{:S(2)}) collective-permute-start(bf16[80,1536]{1,0:T(8,128)(2,1)S(1)} %stack_pair.1), channel_id=1, source_target_pairs={{0,1},{1,0},{2,3},{3,2},{4,5},{5,4},{6,7},{7,6},{8,9},{9,8},{10,11... | collective-permute-start | bytes 737288 | tf_op jit(solution)/shard_map/ppermute | solution.py:566
  12.2 7.0 %attend.1 = (f32[12,192,128]{2,1,0:T(8,128)S(1)}, f32[192,128]{1,0:T(8,128)S(1)}, bf16[192,1536]{1,0:T(8,128)(2,1)S(1)}, bf16[320,1536]{1,0:T(8,128)(2,1)S(1)}, ...) custom-call(s32[4]{0:T(128)} %fc_in.7, ...), custom_call_target="tpu_custom_call" | custom-call | flops 8000000000 | bytes 1000000 | tf_op jit(solution)/shard_map/attend/pallas_call | solution.py:584
  19.2 0.0 collective-permute-done.2.got_pair
  19.2 2.0 %collective-permute-start.3 = (bf16[64,1536]{1,0:T(8,128)(2,1)S(1)}, bf16[64,1536]{1,0:T(8,128)(2,1)S(1)}, u32[]{:S(2)}, u32[]{:S(2)}) collective-permute-start(bf16[64,1536]{1,0:T(8,128)(2,1)S(1)} %stack_mate.1), channel_id=1, source_target_pairs={{0,3},{1,2},{2,1},{3,0},{4,7},{5,6},{6,5},{7,4},{8,11},{9,10},{10,... | collective-permute-start | bytes 589832 | tf_op jit(solution)/shard_map/ppermute | solution.py:566
  21.2 4.4 %convolve.1 = (bf16[32,1536]{1,0:T(8,128)(2,1)S(1)}, f32[12,160,128]{2,1,0:T(8,128)S(1)}, f32[12,40,128]{2,1,0:T(8,128)S(1)}, f32[12,128]{1,0:T(8,128)S(1)}, f32...) custom-call(s32[4]{0:T(128)} %fc_in.7, f32[12,192,128]{2,1,0:T(8,128)S(1)} %get-tuple-element.57.h_s, ...), custom_call_target="tpu_custom_call" | custom-call | flops 5000000000 | bytes 1000000 | tf_op jit(solution)/shard_map/convolve/pallas_call | solution.py:584
  25.6 0.5 %collective-permute-start.4 = (bf16[32,1536]{1,0:T(8,128)(2,1)S(1)}, bf16[32,1536]{1,0:T(8,128)(2,1)S(1)}, u32[]{:S(2)}, u32[]{:S(2)}) collective-permute-start(bf16[32,1536]{1,0:T(8,128)(2,1)S(1)} %get-tuple-element.66.first.l0), channel_id=1, source_target_pairs={{0,1},{1,0},{2,3},{3,2},{4,5},{5,4},{6,7},{7,6},{8,9},{9,8},{10,11... | collective-permute-start | bytes 294920 | tf_op jit(solution)/shard_map/ppermute | solution.py:566
  26.1 1.1 %collective-permute-done.3.got_mate = bf16[64,1536]{1,0:T(8,128)(2,1)S(1)} collective-permute-done((bf16[64,1536]{1,0:T(8,128)(2,1)S(1)}, bf16[64,1536]{1,0:T(8,128)(2,1)S(1)}, u32[]{:S(2)}, u32[]{:S(2)}) %collective-permute-start.3) | collective-permute-done | bytes 196640 | tf_op jit(solution)/shard_map/ppermute | solution.py:566
  27.1 4.0 %convolve_back.1 = (bf16[128,1536]{1,0:T(8,128)(2,1)S(1)}, bf16[128,1536]{1,0:T(8,128)(2,1)S(1)}) custom-call(s32[4]{0:T(128)} %fc_in.7, bf16[32,1536]{1,0:T(8,128)(2,1)S(1)} %get-tuple-element.44.after.own, bf16[80,1536]{1,0:T(8,128)(2,1)S(1)} %collective-permute-done.2.got_pair, bf16[64,1536]{1,0:T(8,128)(2,1)S(1)} %collective-permute-done.3.got_mate, ...), custom_call_target="tpu_custom_call" | custom-call | flops 5000000000 | bytes 1000000 | tf_op jit(solution)/shard_map/convolve_back/pallas_call | solution.py:584
  31.1 0.0 collective-permute-done.4.second.l1
  31.1 2.0 %collective-permute-start.5 = (bf16[64,1536]{1,0:T(8,128)(2,1)S(1)}, bf16[64,1536]{1,0:T(8,128)(2,1)S(1)}, u32[]{:S(2)}, u32[]{:S(2)}) collective-permute-start(bf16[64,1536]{1,0:T(8,128)(2,1)S(1)} %stack_latents.1.after), channel_id=1, source_target_pairs={{0,3},{1,2},{2,1},{3,0},{4,7},{5,6},{6,5},{7,4},{8,11},{9,10},{10,... | collective-permute-start | bytes 589832 | tf_op jit(solution)/shard_map/ppermute | solution.py:566
  33.2 2.9 %attend_back.1 = (bf16[64,1536]{1,0:T(8,128)(2,1)S(1)}, bf16[64,1536]{1,0:T(8,128)(2,1)S(1)}, bf16[16,128,256]{2,1,0:T(8,128)(2,1)S(1)}, bf16[128,1536]{1,0:T(8,128)(2,1)S(1)}, bf16[128,1536]{1,0:T(8,128)(2,1)S(1)}) custom-call(bf16[64,1536]{1,0:T(8,128)(2,1)S(1)} %stack_latents.1.after, bf16[192,1536]{1,0:T(8,128)(2,1)S(1)} %get-tuple-element.67.q_s, ...), custom_call_target="tpu_custom_call" | custom-call | flops 6000000000 | bytes 1000000 | tf_op jit(solution)/shard_map/attend_back/pallas_call | solution.py:584
  36.1 1.2 %collective-permute-start.6 = (bf16[64,1536]{1,0:T(8,128)(2,1)S(1)}, bf16[64,1536]{1,0:T(8,128)(2,1)S(1)}, u32[]{:S(2)}, u32[]{:S(2)}) collective-permute-start(bf16[64,1536]{1,0:T(8,128)(2,1)S(1)} %get-tuple-element.73.after), channel_id=1, source_target_pairs={{0,4},{4,0},{8,12},{12,8},{16,20},{20,16},{24,28},{28,24},{32,36},... | collective-permute-start | bytes 589832 | tf_op jit(solution)/shard_map/ppermute | solution.py:561
  37.3 0.8 %collective-permute-start.7 = (bf16[64,1536]{1,0:T(8,128)(2,1)S(1)}, bf16[64,1536]{1,0:T(8,128)(2,1)S(1)}, u32[]{:S(2)}, u32[]{:S(2)}) collective-permute-start(bf16[64,1536]{1,0:T(8,128)(2,1)S(1)} %get-tuple-element.83), channel_id=1, source_target_pairs={{0,1},{1,0},{2,3},{3,2},{4,8},{5,9},{6,10},{7,11},{8,4},{9,5},{10,... | collective-permute-start | bytes 589832 | tf_op jit(solution)/shard_map/ppermute | solution.py:560
  38.1 3.0 %project_back.1 = (f32[128,1536]{1,0:T(8,128)S(1)}, f32[128,128]{1,0:T(8,128)S(1)}, f32[128,128]{1,0:T(8,128)S(1)}) custom-call(bf16[64,1536]{1,0:T(8,128)(2,1)S(1)} %get-tuple-element.73.after, bf16[16,128,256]{2,1,0:T(8,128)(2,1)S(1)} %get-tuple-element.74.ds_s, bf16[320,1536]{1,0:T(8,128)(2,1)S(1)} %get-tuple-element.75.k_s, ...), custom_call_target="tpu_custom_call" | custom-call | flops 3000000000 | bytes 1000000 | tf_op jit(solution)/shard_map/project_back/pallas_call | solution.py:584
  41.1 0.0 collective-permute-done.5.l23
  41.1 0.2 place_rows.1.rows
  41.3 0.0 collective-permute-done.6.recv_a
  41.3 3.2 %collective-permute-done.7.recv_b = bf16[64,1536]{1,0:T(8,128)(2,1)S(1)} collective-permute-done((bf16[64,1536]{1,0:T(8,128)(2,1)S(1)}, bf16[64,1536]{1,0:T(8,128)(2,1)S(1)}, u32[]{:S(2)}, u32[]{:S(2)}) %collective-permute-start.7) | collective-permute-done | bytes 196640 | tf_op jit(solution)/shard_map/ppermute | solution.py:560
  44.5 1.2 %finish.1 = (bf16[64,1536]{1,0:T(8,128)(2,1)}, bf16[128,1536]{1,0:T(8,128)(2,1)}) custom-call(bf16[64,1536]{1,0:T(8,128)(2,1)S(1)} %place_rows.1.rows, bf16[128,1536]{1,0:T(8,128)(2,1)S(1)} %get-tuple-element.49.x_own.x_s, bf16[128,1536]{1,0:T(8,128)(2,1)S(1)} %get-tuple-element.65.after.dh_s, f32[128,1536]{1,0:T(8,128)S(1)} %get-tuple-element.81.g_own, ...), custom_call_target="tpu_custom_call" | custom-call | flops 1000000000 | bytes 1000000 | tf_op jit(solution)/shard_map/finish/pallas_call | solution.py:584
  (3 shorter events, 0.1 us)
Async XLA Ops:
  1.9 8.9 %collective-permute-start = (bf16[112,1536]{1,0:T(8,128)(2,1)S(1)}, bf16[112,1536]{1,0:T(8,128)(2,1)S(1)}, u32[]{:S(2)}, u32[]{:S(2)}) collective-permute-start(bf16[112,1536]{1,0:T(8,128)(2,1)S(1)} %get-tuple-element.47), channel_id=1, source_target_pairs={{0,1},{1,0},{2,3},{3,2},{4,8},{5,9},{6,10},{7,11},{8,4},{9,5},{10,... | collective-permute-start | bytes 1032200 | tf_op jit(solution)/shard_map/ppermute | solution.py:560
  4.1 6.7 %collective-permute-start.1 = (bf16[112,1536]{1,0:T(8,128)(2,1)S(1)}, bf16[112,1536]{1,0:T(8,128)(2,1)S(1)}, u32[]{:S(2)}, u32[]{:S(2)}) collective-permute-start(bf16[112,1536]{1,0:T(8,128)(2,1)S(1)} %get-tuple-element.48), channel_id=1, source_target_pairs={{0,4},{4,0},{8,12},{12,8},{16,20},{20,16},{24,28},{28,24},{32,36},... | collective-permute-start | bytes 1032200 | tf_op jit(solution)/shard_map/ppermute | solution.py:561
  10.8 8.4 %collective-permute-start.2 = (bf16[80,1536]{1,0:T(8,128)(2,1)S(1)}, bf16[80,1536]{1,0:T(8,128)(2,1)S(1)}, u32[]{:S(2)}, u32[]{:S(2)}) collective-permute-start(bf16[80,1536]{1,0:T(8,128)(2,1)S(1)} %stack_pair.1), channel_id=1, source_target_pairs={{0,1},{1,0},{2,3},{3,2},{4,5},{5,4},{6,7},{7,6},{8,9},{9,8},{10,11... | collective-permute-start | bytes 737288 | tf_op jit(solution)/shard_map/ppermute | solution.py:566
  19.2 7.9 %collective-permute-start.3 = (bf16[64,1536]{1,0:T(8,128)(2,1)S(1)}, bf16[64,1536]{1,0:T(8,128)(2,1)S(1)}, u32[]{:S(2)}, u32[]{:S(2)}) collective-permute-start(bf16[64,1536]{1,0:T(8,128)(2,1)S(1)} %stack_mate.1), channel_id=1, source_target_pairs={{0,3},{1,2},{2,1},{3,0},{4,7},{5,6},{6,5},{7,4},{8,11},{9,10},{10,... | collective-permute-start | bytes 589832 | tf_op jit(solution)/shard_map/ppermute | solution.py:566
  25.6 5.5 %collective-permute-start.4 = (bf16[32,1536]{1,0:T(8,128)(2,1)S(1)}, bf16[32,1536]{1,0:T(8,128)(2,1)S(1)}, u32[]{:S(2)}, u32[]{:S(2)}) collective-permute-start(bf16[32,1536]{1,0:T(8,128)(2,1)S(1)} %get-tuple-element.66.first.l0), channel_id=1, source_target_pairs={{0,1},{1,0},{2,3},{3,2},{4,5},{5,4},{6,7},{7,6},{8,9},{9,8},{10,11... | collective-permute-start | bytes 294920 | tf_op jit(solution)/shard_map/ppermute | solution.py:566
  31.1 10.0 %collective-permute-start.5 = (bf16[64,1536]{1,0:T(8,128)(2,1)S(1)}, bf16[64,1536]{1,0:T(8,128)(2,1)S(1)}, u32[]{:S(2)}, u32[]{:S(2)}) collective-permute-start(bf16[64,1536]{1,0:T(8,128)(2,1)S(1)} %stack_latents.1.after), channel_id=1, source_target_pairs={{0,3},{1,2},{2,1},{3,0},{4,7},{5,6},{6,5},{7,4},{8,11},{9,10},{10,... | collective-permute-start | bytes 589832 | tf_op jit(solution)/shard_map/ppermute | solution.py:566
  36.1 5.2 %collective-permute-start.6 = (bf16[64,1536]{1,0:T(8,128)(2,1)S(1)}, bf16[64,1536]{1,0:T(8,128)(2,1)S(1)}, u32[]{:S(2)}, u32[]{:S(2)}) collective-permute-start(bf16[64,1536]{1,0:T(8,128)(2,1)S(1)} %get-tuple-element.73.after), channel_id=1, source_target_pairs={{0,4},{4,0},{8,12},{12,8},{16,20},{20,16},{24,28},{28,24},{32,36},... | collective-permute-start | bytes 589832 | tf_op jit(solution)/shard_map/ppermute | solution.py:561
  37.3 7.2 %collective-permute-start.7 = (bf16[64,1536]{1,0:T(8,128)(2,1)S(1)}, bf16[64,1536]{1,0:T(8,128)(2,1)S(1)}, u32[]{:S(2)}, u32[]{:S(2)}) collective-permute-start(bf16[64,1536]{1,0:T(8,128)(2,1)S(1)} %get-tuple-element.83), channel_id=1, source_target_pairs={{0,1},{1,0},{2,3},{3,2},{4,8},{5,9},{6,10},{7,11},{8,4},{9,5},{10,... | collective-permute-start | bytes 589832 | tf_op jit(solution)/shard_map/ppermute | solution.py:560

commit v7 on v5

--- a/solution.py
+++ b/solution.py
@@ -69,7 +69,7 @@
     return out
 
 
-def prepare(fc_in, tl_in, audio, grads, send_a, send_b, own, pair, mate, fc, tl, g_buf, sems):
+def prepare(fc_in, tl_in, audio, grads, send_a, send_b, own, pair, mate, placing, fc, tl, g_buf, sems):
     cf = pltpu.make_async_copy(fc_in, fc, sems.at[0])
     ct = pltpu.make_async_copy(tl_in, tl, sems.at[1])
     cf.start()
@@ -108,6 +108,14 @@
             hit = (place // 4 == (j + 3) % 4) & (r < lives[j]) & (slot == r + starts[j])
             chosen = jnp.where(hit, 1.0, chosen)
         picked.append(chosen.astype(BF))
+    slot = lax.broadcasted_iota(jnp.int32, (SLOTS, NREC * LR), 0) + llm * SLOTS
+    col = lax.broadcasted_iota(jnp.int32, (SLOTS, NREC * LR), 1)
+    chosen = jnp.zeros((SLOTS, NREC * LR), F32)
+    for j, apart in enumerate((0, 1, 3, 2)):
+        r = col - j * LR
+        hit = (r >= 0) & (r < LR) & (r < lives[apart]) & (slot == r + starts[apart])
+        chosen = jnp.where(hit, 1.0, chosen)
+    placing[...] = chosen.astype(BF)
     cg.wait()
     moved = dot(jnp.concatenate(picked, axis=0), g_buf[...]).astype(BF)
     own[...] = moved[:LR]
@@ -478,13 +486,8 @@
 
 
 def project_back(
-    fc_in, tl_in, after, ds_s, k_s, dk, dv, wq_s, wkt_s, wvt_s, x_s, gains, l0, l1, l23,
-    g_o, along_o, inv_o, rows_o, fc, tl, dq_s, sems,
+    after, ds_s, k_s, dk, dv, wq_s, wkt_s, wvt_s, x_s, gains, g_o, along_o, inv_o, dq_s,
 ):
-    cf = pltpu.make_async_copy(fc_in, fc, sems.at[0])
-    ct = pltpu.make_async_copy(tl_in, tl, sems.at[1])
-    cf.start()
-    ct.start()
     for g in range(4):
         dq = [None] * 3
         for j, (lo, hi) in enumerate(WINDOWS):
@@ -505,21 +508,10 @@
     inv = lax.rsqrt(jnp.sum(squares, axis=-1, keepdims=True) * (1.0 / D) + EPSILON)
     inv_o[...] = jnp.broadcast_to(inv, (FR, LANE))
 
-    tm = lax.axis_index("tm")
-    llm = lax.axis_index("llm")
-    cf.wait()
-    ct.wait()
-    starts, lives = routes(fc, tl, tm)
-    slot = lax.broadcasted_iota(jnp.int32, (SLOTS, NREC * LR), 0) + llm * SLOTS
-    col = lax.broadcasted_iota(jnp.int32, (SLOTS, NREC * LR), 1)
-    chosen = jnp.zeros((SLOTS, NREC * LR), F32)
-    for j, apart in enumerate((0, 1, 3, 2)):
-        b = llm ^ apart
-        r = col - j * LR
-        hit = (r >= 0) & (r < LR) & (r < pick(lives, b)) & (slot == r + pick(starts, b))
-        chosen = jnp.where(hit, 1.0, chosen)
+
+def place_rows(after, chosen, l0, l1, l23, rows_o):
     latents = jnp.concatenate([l0[...], l1[...], l23[...]], axis=0)
-    rows_o[...] = dot(chosen.astype(BF), latents).astype(BF)
+    rows_o[...] = dot(chosen[...], latents).astype(BF)
 
 
 def finish(
@@ -623,10 +615,10 @@
     def sems(*dims):
         return pltpu.SemaphoreType.DMA(dims)
 
-    send_a, send_b, own, pair, mate = call(
+    send_a, send_b, own, pair, mate, placing = call(
         prepare,
         mark("h", frame_counts, tl_in, signal, llm_grads[0]),
-        [rows(HALO + 16), rows(HALO + 16), rows(LR), rows(2 * LR), rows(LR)],
+        [rows(HALO + 16), rows(HALO + 16), rows(LR), rows(2 * LR), rows(LR), ((SLOTS, NREC * LR), BF)],
         [fc, tl, V((SLOTS, D), BF), sems(5)],
         100_000_000,
     )
@@ -682,13 +674,19 @@
         6_000_000_000,
     )
     ret_a, ret_b = swap(n_tm, back_a, back_b)
-    g_own, along, inv_x, placed = call(
+    g_own, along, inv_x = call(
         project_back,
-        mark("h", frame_counts, tl_in)
-        + mark("v", back_a, ds, k, dk, dv, wq, wkt, wvt, x, gains, latent, latent_1, latent_23),
-        [rows(FR, F32), ((FR, LANE), F32), ((FR, LANE), F32), rows(SLOTS)],
-        [fc, tl, V((FR, D), BF), sems(2)],
+        mark("v", back_a, ds, k, dk, dv, wq, wkt, wvt, x, gains),
+        [rows(FR, F32), ((FR, LANE), F32), ((FR, LANE), F32)],
+        [V((FR, D), BF)],
         3_000_000_000,
+    )
+    (placed,) = call(
+        place_rows,
+        mark("v", along, placing, latent, latent_1, latent_23),
+        [rows(SLOTS)],
+        [],
+        50_000_000,
     )
     out_rows, grad = call(
         finish,

time: 44.3 us -> 44.2 us (level)
    ppermute x4, waiting for transfers between devices: 1.17 us -> 0.01 us  [trade(): return lax.ppermute(cells, 'llm', [(i, i ^ apart) for i in range(n)])]
    ppermute x2, waiting for transfers between devices: 3.11 us -> 4.15 us  [swap(): lax.ppermute(cells_b, ('tm', 'llm'), full_b)]
    pallas_call x11 -> x12, Pallas kernels: 29 us -> 29 us  [call(): pl.pallas_call(kernel, out_shape=shapes, in_specs=[spec[kind] for kind, _...]
  transfers between devices with their start and end apart: 8 -> 8, of which waited for: 3 -> 2; matrix products, arithmetic and copies ran while one was open for 0% -> 0% of each run, Pallas kernels for 60% -> 60%
where the time goes in v7:
time: 44.2 us; the launch traced here: 44 us
  Pallas kernels  29 us (66%)
  starting transfers between devices  9.94 us (22%)
  waiting for transfers between devices  4.16 us (9%)
  between operations  0.92 us (2%)
    pallas_call x12, Pallas kernels, call(): pl.pallas_call(kernel, out_shape=shapes, in_specs=[spec[kind] for kind, _...  29 us
    ppermute x4, starting transfers between devices, trade(): return lax.ppermute(cells, 'llm', [(i, i ^ apart) for i in range(n)])  5.42 us
    ppermute x2, waiting for transfers between devices, swap(): lax.ppermute(cells_b, ('tm', 'llm'), full_b)  4.15 us
    ppermute x2, starting transfers between devices, swap(): lax.ppermute(cells_b, ('tm', 'llm'), full_b)  3.39 us
    ppermute x2, starting transfers between devices, swap(): lax.ppermute(cells_a, 'tm', pairs_a)  1.13 us
  transfers between devices with their start and end apart: 8, of which 2 were waited for; matrix products, arithmetic and copies ran while one was open for 0% of the time, Pallas kernels for 60%

profile of v7, /device:TPU:39, one launch (start us, length us, event | category | flops | bytes accessed | tf_op | source)
XLA Modules:
  0.0 44.0 jit_solution(5113961314741965075)
XLA Ops:
  0.6 1.2 %prepare.1 = (bf16[112,1536]{1,0:T(8,128)(2,1)S(1)}, bf16[112,1536]{1,0:T(8,128)(2,1)S(1)}, bf16[32,1536]{1,0:T(8,128)(2,1)S(1)}, bf16[64,1536]{1,0:T(8,128)(2,1...) custom-call(s32[4]{0:T(128)} %fc_in.7, s32[4,32]{1,0:T(4,128)} %bitcast.11, bf16[128,1536]{1,0:T(8,128)(2,1)} %bitcast.8, ...), custom_call_target="tpu_custom_call" | custom-call | flops 100000000 | bytes 1000000 | tf_op jit(solution)/shard_map/prepare/pallas_call | solution.py:582
  1.9 0.7 %collective-permute-start = (bf16[112,1536]{1,0:T(8,128)(2,1)S(1)}, bf16[112,1536]{1,0:T(8,128)(2,1)S(1)}, u32[]{:S(2)}, u32[]{:S(2)}) collective-permute-start(bf16[112,1536]{1,0:T(8,128)(2,1)S(1)} %get-tuple-element.49), channel_id=1, source_target_pairs={{0,4},{4,0},{8,12},{12,8},{16,20},{20,16},{24,28},{28,24},{32,36},... | collective-permute-start | bytes 1032200 | tf_op jit(solution)/shard_map/ppermute | solution.py:559
  2.6 1.5 %collective-permute-start.1 = (bf16[112,1536]{1,0:T(8,128)(2,1)S(1)}, bf16[112,1536]{1,0:T(8,128)(2,1)S(1)}, u32[]{:S(2)}, u32[]{:S(2)}) collective-permute-start(bf16[112,1536]{1,0:T(8,128)(2,1)S(1)} %get-tuple-element.50), channel_id=1, source_target_pairs={{0,1},{1,0},{2,3},{3,2},{4,8},{5,9},{6,10},{7,11},{8,4},{9,5},{10,... | collective-permute-start | bytes 1032200 | tf_op jit(solution)/shard_map/ppermute | solution.py:559
  4.2 5.2 %project_own.1 = (bf16[128,1536]{1,0:T(8,128)(2,1)S(1)}, f32[12,128]{1,0:T(8,128)S(1)}, bf16[128,1536]{1,0:T(8,128)(2,1)S(1)}, bf16[128,1536]{1,0:T(8,128)(2,1)S...) custom-call(bf16[32,1536]{1,0:T(8,128)(2,1)S(1)} %get-tuple-element., ...), custom_call_target="tpu_custom_call" | custom-call | flops 6000000000 | bytes 1000000 | tf_op jit(solution)/shard_map/project_own/pallas_call | solution.py:582
  9.4 0.0 collective-permute-done.recv_a
  9.4 2.0 %collective-permute-done.1.recv_b = bf16[112,1536]{1,0:T(8,128)(2,1)S(1)} collective-permute-done((bf16[112,1536]{1,0:T(8,128)(2,1)S(1)}, bf16[112,1536]{1,0:T(8,128)(2,1)S(1)}, u32[]{:S(2)}, u32[]{:S(2)}) %collective-permute-start.1) | collective-permute-done | bytes 344096 | tf_op jit(solution)/shard_map/ppermute | solution.py:559
  11.4 1.4 %collective-permute-start.2 = (bf16[80,1536]{1,0:T(8,128)(2,1)S(1)}, bf16[80,1536]{1,0:T(8,128)(2,1)S(1)}, u32[]{:S(2)}, u32[]{:S(2)}) collective-permute-start(bf16[80,1536]{1,0:T(8,128)(2,1)S(1)} %stack_pair.1), channel_id=1, source_target_pairs={{0,1},{1,0},{2,3},{3,2},{4,5},{5,4},{6,7},{7,6},{8,9},{9,8},{10,11... | collective-permute-start | bytes 737288 | tf_op jit(solution)/shard_map/ppermute | solution.py:564
  12.8 5.9 %attend.1 = (bf16[192,1536]{1,0:T(8,128)(2,1)S(1)}, bf16[192,1536]{1,0:T(8,128)(2,1)S(1)}, bf16[320,1536]{1,0:T(8,128)(2,1)S(1)}, bf16[320,1536]{1,0:T(8,128)(2,...) custom-call(s32[4]{0:T(128)} %fc_in.7, ...), custom_call_target="tpu_custom_call" | custom-call | flops 8000000000 | bytes 1000000 | tf_op jit(solution)/shard_map/attend/pallas_call | solution.py:582
  18.7 0.0 collective-permute-done.2.got_pair
  18.7 2.0 %collective-permute-start.3 = (bf16[64,1536]{1,0:T(8,128)(2,1)S(1)}, bf16[64,1536]{1,0:T(8,128)(2,1)S(1)}, u32[]{:S(2)}, u32[]{:S(2)}) collective-permute-start(bf16[64,1536]{1,0:T(8,128)(2,1)S(1)} %stack_mate.1), channel_id=1, source_target_pairs={{0,3},{1,2},{2,1},{3,0},{4,7},{5,6},{6,5},{7,4},{8,11},{9,10},{10,... | collective-permute-start | bytes 589832 | tf_op jit(solution)/shard_map/ppermute | solution.py:564
  20.7 5.3 %convolve.1 = (bf16[32,1536]{1,0:T(8,128)(2,1)S(1)}, f32[12,192,128]{2,1,0:T(8,128)S(1)}, f32[12,160,128]{2,1,0:T(8,128)S(1)}, f32[12,40,128]{2,1,0:T(8,128)S(1)...) custom-call(s32[4]{0:T(128)} %fc_in.7, ...), custom_call_target="tpu_custom_call" | custom-call | flops 5000000000 | bytes 1000000 | tf_op jit(solution)/shard_map/convolve/pallas_call | solution.py:582
  26.1 0.5 %collective-permute-start.4 = (bf16[32,1536]{1,0:T(8,128)(2,1)S(1)}, bf16[32,1536]{1,0:T(8,128)(2,1)S(1)}, u32[]{:S(2)}, u32[]{:S(2)}) collective-permute-start(bf16[32,1536]{1,0:T(8,128)(2,1)S(1)} %get-tuple-element.70.first.l0), channel_id=1, source_target_pairs={{0,1},{1,0},{2,3},{3,2},{4,5},{5,4},{6,7},{7,6},{8,9},{9,8},{10,11... | collective-permute-start | bytes 294920 | tf_op jit(solution)/shard_map/ppermute | solution.py:564
  26.5 0.0 collective-permute-done.3.got_mate
  26.5 3.9 %convolve_back.1 = (bf16[128,1536]{1,0:T(8,128)(2,1)S(1)}, bf16[128,1536]{1,0:T(8,128)(2,1)S(1)}) custom-call(s32[4]{0:T(128)} %fc_in.7, bf16[32,1536]{1,0:T(8,128)(2,1)S(1)} %get-tuple-element.46.after.own, bf16[80,1536]{1,0:T(8,128)(2,1)S(1)} %collective-permute-done.2.got_pair, bf16[64,1536]{1,0:T(8,128)(2,1)S(1)} %collective-permute-done.3.got_mate, ...), custom_call_target="tpu_custom_call" | custom-call | flops 5000000000 | bytes 1000000 | tf_op jit(solution)/shard_map/convolve_back/pallas_call | solution.py:582
  30.5 0.0 collective-permute-done.4.second.l1
  30.5 1.6 %collective-permute-start.5 = (bf16[64,1536]{1,0:T(8,128)(2,1)S(1)}, bf16[64,1536]{1,0:T(8,128)(2,1)S(1)}, u32[]{:S(2)}, u32[]{:S(2)}) collective-permute-start(bf16[64,1536]{1,0:T(8,128)(2,1)S(1)} %stack_latents.1.after), channel_id=1, source_target_pairs={{0,3},{1,2},{2,1},{3,0},{4,7},{5,6},{6,5},{7,4},{8,11},{9,10},{10,... | collective-permute-start | bytes 589832 | tf_op jit(solution)/shard_map/ppermute | solution.py:564
  32.1 2.9 %attend_back.1 = (bf16[64,1536]{1,0:T(8,128)(2,1)S(1)}, bf16[64,1536]{1,0:T(8,128)(2,1)S(1)}, bf16[16,128,256]{2,1,0:T(8,128)(2,1)S(1)}, bf16[128,1536]{1,0:T(8,128)(2,1)S(1)}, bf16[128,1536]{1,0:T(8,128)(2,1)S(1)}) custom-call(bf16[64,1536]{1,0:T(8,128)(2,1)S(1)} %stack_latents.1.after, bf16[192,1536]{1,0:T(8,128)(2,1)S(1)} %get-tuple-element.71.q_s, ...), custom_call_target="tpu_custom_call" | custom-call | flops 6000000000 | bytes 1000000 | tf_op jit(solution)/shard_map/attend_back/pallas_call | solution.py:582
  35.0 0.4 collective-permute-start.6
  35.4 1.9 %collective-permute-start.7 = (bf16[64,1536]{1,0:T(8,128)(2,1)S(1)}, bf16[64,1536]{1,0:T(8,128)(2,1)S(1)}, u32[]{:S(2)}, u32[]{:S(2)}) collective-permute-start(bf16[64,1536]{1,0:T(8,128)(2,1)S(1)} %get-tuple-element.87), channel_id=1, source_target_pairs={{0,1},{1,0},{2,3},{3,2},{4,8},{5,9},{6,10},{7,11},{8,4},{9,5},{10,... | collective-permute-start | bytes 589832 | tf_op jit(solution)/shard_map/ppermute | solution.py:559
  37.3 3.0 %project_back.1 = (f32[128,1536]{1,0:T(8,128)S(1)}, f32[128,128]{1,0:T(8,128)S(1)}, f32[128,128]{1,0:T(8,128)S(1)}) custom-call(bf16[64,1536]{1,0:T(8,128)(2,1)S(1)} %get-tuple-element.77.after, bf16[16,128,256]{2,1,0:T(8,128)(2,1)S(1)} %get-tuple-element.78.ds_s, bf16[320,1536]{1,0:T(8,128)(2,1)S(1)} %get-tuple-element.79.k_s, ...), custom_call_target="tpu_custom_call" | custom-call | flops 3000000000 | bytes 1000000 | tf_op jit(solution)/shard_map/project_back/pallas_call | solution.py:582
  40.2 0.0 collective-permute-done.5.l23
  40.3 0.2 place_rows.1.rows
  40.5 0.0 collective-permute-done.6.recv_a
  40.5 2.2 %collective-permute-done.7.recv_b = bf16[64,1536]{1,0:T(8,128)(2,1)S(1)} collective-permute-done((bf16[64,1536]{1,0:T(8,128)(2,1)S(1)}, bf16[64,1536]{1,0:T(8,128)(2,1)S(1)}, u32[]{:S(2)}, u32[]{:S(2)}) %collective-permute-start.7) | collective-permute-done | bytes 196640 | tf_op jit(solution)/shard_map/ppermute | solution.py:559
  42.6 1.2 %finish.1 = (bf16[64,1536]{1,0:T(8,128)(2,1)}, bf16[128,1536]{1,0:T(8,128)(2,1)}) custom-call(bf16[64,1536]{1,0:T(8,128)(2,1)S(1)} %place_rows.1.rows, bf16[128,1536]{1,0:T(8,128)(2,1)S(1)} %get-tuple-element.51.x_own.x_s, bf16[128,1536]{1,0:T(8,128)(2,1)S(1)} %get-tuple-element.69.after.dh_s, f32[128,1536]{1,0:T(8,128)S(1)} %get-tuple-element.85.g_own, ...), custom_call_target="tpu_custom_call" | custom-call | flops 1000000000 | bytes 1000000 | tf_op jit(solution)/shard_map/finish/pallas_call | solution.py:582
  (3 shorter events, 0.1 us)
Async XLA Ops:
  1.9 7.5 %collective-permute-start = (bf16[112,1536]{1,0:T(8,128)(2,1)S(1)}, bf16[112,1536]{1,0:T(8,128)(2,1)S(1)}, u32[]{:S(2)}, u32[]{:S(2)}) collective-permute-start(bf16[112,1536]{1,0:T(8,128)(2,1)S(1)} %get-tuple-element.49), channel_id=1, source_target_pairs={{0,4},{4,0},{8,12},{12,8},{16,20},{20,16},{24,28},{28,24},{32,36},... | collective-permute-start | bytes 1032200 | tf_op jit(solution)/shard_map/ppermute | solution.py:559
  2.6 8.8 %collective-permute-start.1 = (bf16[112,1536]{1,0:T(8,128)(2,1)S(1)}, bf16[112,1536]{1,0:T(8,128)(2,1)S(1)}, u32[]{:S(2)}, u32[]{:S(2)}) collective-permute-start(bf16[112,1536]{1,0:T(8,128)(2,1)S(1)} %get-tuple-element.50), channel_id=1, source_target_pairs={{0,1},{1,0},{2,3},{3,2},{4,8},{5,9},{6,10},{7,11},{8,4},{9,5},{10,... | collective-permute-start | bytes 1032200 | tf_op jit(solution)/shard_map/ppermute | solution.py:559
  11.4 7.3 %collective-permute-start.2 = (bf16[80,1536]{1,0:T(8,128)(2,1)S(1)}, bf16[80,1536]{1,0:T(8,128)(2,1)S(1)}, u32[]{:S(2)}, u32[]{:S(2)}) collective-permute-start(bf16[80,1536]{1,0:T(8,128)(2,1)S(1)} %stack_pair.1), channel_id=1, source_target_pairs={{0,1},{1,0},{2,3},{3,2},{4,5},{5,4},{6,7},{7,6},{8,9},{9,8},{10,11... | collective-permute-start | bytes 737288 | tf_op jit(solution)/shard_map/ppermute | solution.py:564
  18.7 7.8 %collective-permute-start.3 = (bf16[64,1536]{1,0:T(8,128)(2,1)S(1)}, bf16[64,1536]{1,0:T(8,128)(2,1)S(1)}, u32[]{:S(2)}, u32[]{:S(2)}) collective-permute-start(bf16[64,1536]{1,0:T(8,128)(2,1)S(1)} %stack_mate.1), channel_id=1, source_target_pairs={{0,3},{1,2},{2,1},{3,0},{4,7},{5,6},{6,5},{7,4},{8,11},{9,10},{10,... | collective-permute-start | bytes 589832 | tf_op jit(solution)/shard_map/ppermute | solution.py:564
  26.1 4.4 %collective-permute-start.4 = (bf16[32,1536]{1,0:T(8,128)(2,1)S(1)}, bf16[32,1536]{1,0:T(8,128)(2,1)S(1)}, u32[]{:S(2)}, u32[]{:S(2)}) collective-permute-start(bf16[32,1536]{1,0:T(8,128)(2,1)S(1)} %get-tuple-element.70.first.l0), channel_id=1, source_target_pairs={{0,1},{1,0},{2,3},{3,2},{4,5},{5,4},{6,7},{7,6},{8,9},{9,8},{10,11... | collective-permute-start | bytes 294920 | tf_op jit(solution)/shard_map/ppermute | solution.py:564
  30.5 9.7 %collective-permute-start.5 = (bf16[64,1536]{1,0:T(8,128)(2,1)S(1)}, bf16[64,1536]{1,0:T(8,128)(2,1)S(1)}, u32[]{:S(2)}, u32[]{:S(2)}) collective-permute-start(bf16[64,1536]{1,0:T(8,128)(2,1)S(1)} %stack_latents.1.after), channel_id=1, source_target_pairs={{0,3},{1,2},{2,1},{3,0},{4,7},{5,6},{6,5},{7,4},{8,11},{9,10},{10,... | collective-permute-start | bytes 589832 | tf_op jit(solution)/shard_map/ppermute | solution.py:564
  35.0 5.4 %collective-permute-start.6 = (bf16[64,1536]{1,0:T(8,128)(2,1)S(1)}, bf16[64,1536]{1,0:T(8,128)(2,1)S(1)}, u32[]{:S(2)}, u32[]{:S(2)}) collective-permute-start(bf16[64,1536]{1,0:T(8,128)(2,1)S(1)} %get-tuple-element.77.after), channel_id=1, source_target_pairs={{0,4},{4,0},{8,12},{12,8},{16,20},{20,16},{24,28},{28,24},{32,36},... | collective-permute-start | bytes 589832 | tf_op jit(solution)/shard_map/ppermute | solution.py:559
  35.4 7.2 %collective-permute-start.7 = (bf16[64,1536]{1,0:T(8,128)(2,1)S(1)}, bf16[64,1536]{1,0:T(8,128)(2,1)S(1)}, u32[]{:S(2)}, u32[]{:S(2)}) collective-permute-start(bf16[64,1536]{1,0:T(8,128)(2,1)S(1)} %get-tuple-element.87), channel_id=1, source_target_pairs={{0,1},{1,0},{2,3},{3,2},{4,8},{5,9},{6,10},{7,11},{8,4},{9,5},{10,... | collective-permute-start | bytes 589832 | tf_op jit(solution)/shard_map/ppermute | solution.py:559
